TPU v7x, 256 devices: a whole 4x4x8 slice. The times are simulated.
256 devices in a mesh: seq: 128 (over y, x, z), head: 2 (over core).
Axes of the slice: x: 4, y: 4, z: 8, core: 2. Of those that a mesh axis runs over, the one named last changes fastest.
Arguments:
- query_raw: bfloat16 [16384, 2048], P('seq', 'head'), may hold values from -6 to 6
- key_raw: bfloat16 [16384, 2048], P('seq', 'head'), may hold values from -6 to 6
- value_raw: bfloat16 [16384, 2048], P('seq', 'head'), may hold values from -6 to 6
- gate_raw: float32 [16384, 2048], P('seq', 'head')
- beta_raw: float32 [16384, 16], P('seq', 'head'), may hold values from -8.5 to 3.5
- conv_weight: float32 [3, 4, 2048], P(None, None, 'head'), may hold values from -3 to 3
- decay_log: float32 [2048], P('head')
- grad_out: bfloat16 [16384, 2048], P('seq', 'head'), may hold values from -6 to 6
Outputs:
- query_grad: bfloat16 [16384, 2048], P('seq', 'head')
- key_grad: bfloat16 [16384, 2048], P('seq', 'head')
- value_grad: bfloat16 [16384, 2048], P('seq', 'head')
- gate_grad: float32 [16384, 2048], P('seq', 'head')
- beta_grad: float32 [16384, 16], P('seq', 'head')
- conv_grad: float32 [3, 4, 2048], P(None, None, 'head')
- decay_grad: float32 [2048], P('head')
All inputs are finite; a program needn't handle non-finite values.
Results may differ from a plain program's by a relative error of at most 0.0018.
Values may be sent and summed in bfloat16 or wider, within the bound.
No kernel may reach another device: no remote copies, remote signals or barrier semaphores. Data moves between devices by JAX's collectives and lax.ppermute only.
A program may use at most 128 MiB of HBM per device.

v0:
```python
import jax
import jax.numpy as jnp
from jax import lax
from jax.sharding import PartitionSpec as P

BLOCK = 64


largest_entry = lax.Precision.HIGHEST
epsilon = 1e-06


def shifted(block, axis, distance):
    devices = range(lax.axis_size(axis))
    route = [(i - distance, i) for i in devices if i - distance in devices]
    return lax.ppermute(block, axis, route)


def product(formula, left, right):
    return jnp.einsum(formula, left, right, precision=largest_entry)


def conv_silu(extended, weights, length):
    summed = weights[0] * extended[0:length]
    for offset in range(1, weights.shape[0]):
        summed = summed + weights[offset] * extended[offset : offset + length]
    return jax.nn.silu(summed)


def unit_heads(vectors):
    return vectors * lax.rsqrt(jnp.sum(vectors * vectors, axis=-1, keepdims=True) + epsilon)


def to_blocks(array):
    length, head_count, head_width = array.shape
    return array.reshape(length // BLOCK, BLOCK, head_count, head_width).transpose(2, 0, 1, 3)


def prepare(query_ext, key_ext, value_ext, gate_raw, beta_raw, conv_weight, decay_log):
    length = gate_raw.shape[0]
    head_count = beta_raw.shape[1]
    head_width = gate_raw.shape[1] // head_count
    head_shape = (length, head_count, head_width)
    queries = to_blocks(
        unit_heads(conv_silu(query_ext, conv_weight[0], length).reshape(head_shape))
    )
    keys = to_blocks(unit_heads(conv_silu(key_ext, conv_weight[1], length).reshape(head_shape)))
    values = to_blocks(conv_silu(value_ext, conv_weight[2], length).reshape(head_shape))
    log_decay = to_blocks((-jnp.exp(decay_log) * jax.nn.softplus(gate_raw)).reshape(head_shape))
    beta_rate = (
        jax.nn.sigmoid(beta_raw).reshape(length // BLOCK, BLOCK, head_count).transpose(2, 0, 1)
    )
    return (queries, keys, values, log_decay, beta_rate)


def unit_inverse(coupling):
    size = coupling.shape[-1]
    ident = jnp.eye(size, dtype=jnp.float32)
    result = ident - coupling
    power = coupling
    for level in range(size.bit_length() - 2):
        power = product("...ij,...jk->...ik", power, power)
        result = product("...ij,...jk->...ik", result, ident + power)
    return result


def block_parts(queries, keys, log_decay, beta_rate):
    size = keys.shape[-2]
    cumul = jnp.cumsum(log_decay, axis=-2)
    middle = cumul[..., size // 2 : size // 2 + 1, :]
    last = cumul[..., size - 1 : size, :]
    keys_up = keys * jnp.exp(cumul - middle)
    keys_down = keys * jnp.exp(middle - cumul)
    query_up = queries * jnp.exp(cumul - middle)
    query_full = queries * jnp.exp(cumul)
    keys_full = keys * jnp.exp(cumul)
    keys_end = keys * jnp.exp(last - cumul)
    positions = jnp.arange(size)
    strict = (positions[:, None] > positions[None, :]).astype(jnp.float32)
    lower = (positions[:, None] >= positions[None, :]).astype(jnp.float32)
    coupling = product("...tc,...sc->...ts", keys_up, keys_down) * strict * beta_rate[..., :, None]
    inverse = unit_inverse(coupling)
    attend = product("...tc,...sc->...ts", query_up, keys_down) * lower
    return (query_full, keys_full, keys_end, jnp.exp(last[..., 0, :]), inverse, attend)


def block_maps(parts, values, beta_rate, grad_blocks):
    query_full, keys_full, keys_end, decay_end, inverse, attend = parts
    by_values = product("...ts,...sd->...td", inverse, beta_rate[..., None] * values)
    by_keys = product("...ts,...sd->...td", inverse, beta_rate[..., None] * keys_full)
    ident = jnp.eye(decay_end.shape[-1], dtype=jnp.float32)
    trans = ident * decay_end[..., :, None] - product("...sc,...sd->...cd", keys_end, by_keys)
    offset = product("...sc,...sd->...cd", keys_end, by_values)
    reached = product("...ts,...td->...sd", attend, grad_blocks)
    adjoint = product("...tc,...td->...cd", query_full, grad_blocks) - product(
        "...sc,...sd->...cd", by_keys, reached
    )
    return (trans, offset, adjoint)


def identity_maps(trans):
    return jnp.broadcast_to(
        jnp.eye(trans.shape[-1], dtype=jnp.float32), (trans.shape[0],) + trans.shape[2:]
    )


def compose_triples(trans, offset, adjoint):
    sliced = (jnp.moveaxis(trans, 1, 0), jnp.moveaxis(offset, 1, 0), jnp.moveaxis(adjoint, 1, 0))
    zeros = jnp.zeros(offset.shape[:1] + offset.shape[2:], jnp.float32)

    def compose_advance(carry, item):
        summed, offsets, adjoints = carry
        here_trans, here_offset, here_adjoint = item
        adjoints = adjoints + product("hcd,hce->hde", summed, here_adjoint)
        offsets = product("hcd,hde->hce", here_trans, offsets) + here_offset
        summed = product("hcd,hde->hce", here_trans, summed)
        return ((summed, offsets, adjoints), None)

    (summed, offsets, adjoints), unused = lax.scan(
        compose_advance, (identity_maps(trans), zeros, zeros), sliced
    )
    return (summed, offsets, adjoints)


def local_run(
    query_ext, key_ext, value_ext, gate_raw, beta_raw, conv_weight, decay_log, start_state
):
    queries, keys, values, log_decay, beta_rate = prepare(
        query_ext, key_ext, value_ext, gate_raw, beta_raw, conv_weight, decay_log
    )
    parts = block_parts(queries, keys, log_decay, beta_rate)

    def local_advance(recall_memory, item):
        (
            block_query,
            block_keys,
            block_end,
            block_decay,
            block_inverse,
            block_attend,
            block_values,
            block_beta,
        ) = item
        errors = block_beta[..., None] * (
            block_values - product("htc,hcd->htd", block_keys, recall_memory)
        )
        deltas = product("hts,hsd->htd", block_inverse, errors)
        result = product("htc,hcd->htd", block_query, recall_memory) + product(
            "hts,hsd->htd", block_attend, deltas
        )
        recall_memory = block_decay[..., None] * recall_memory + product(
            "hsc,hsd->hcd", block_end, deltas
        )
        return (recall_memory, result)

    sliced = tuple((jnp.moveaxis(array, 1, 0) for array in parts + (values, beta_rate)))
    end_state, results = lax.scan(local_advance, start_state, sliced)
    length = gate_raw.shape[0]
    return (results.transpose(0, 2, 1, 3).reshape(length, gate_raw.shape[1]), end_state)


def forward_join(earlier, later):
    return (
        product("hcd,hde->hce", later[0], earlier[0]),
        product("hcd,hde->hce", later[0], earlier[1]) + later[1],
    )


def backward_join(earlier, later):
    return (
        product("hcd,hde->hce", earlier[0], later[0]),
        later[1] + product("hcd,hce->hde", later[0], earlier[1]),
    )


def doubling_prefix(stacked, neutral, combine, mover, reverse):
    count = lax.axis_size("seq")
    position = lax.axis_index("seq")
    offsets = [1]
    stride = 1
    while stride < count:
        offsets.append(stride)
        stride = stride * 2
    current = stacked
    for number, stride in enumerate(offsets):
        moved = mover(current, -stride if reverse else stride)
        if reverse:
            present = position + stride < count
        else:
            present = position - stride >= 0
        moved = jnp.where(present, moved, neutral)
        if number == 0:
            current = moved
        else:
            joined = combine((moved[0], moved[1]), (current[0], current[1]))
            current = jnp.stack(joined)
    return (current[0], current[1])


def per_device(query_raw, key_raw, value_raw, gate_raw, beta_raw, conv_weight, decay_log, grad_out):
    margin = conv_weight.shape[1] - 1
    length = gate_raw.shape[0]
    head_count = beta_raw.shape[1]
    head_width = gate_raw.shape[1] // head_count
    edges = jnp.stack(
        [query_raw[length - margin :], key_raw[length - margin :], value_raw[length - margin :]]
    )
    before = shifted(edges, "seq", 1)
    query_ext = jnp.concatenate([before[0], query_raw], 0).astype(jnp.float32)
    key_ext = jnp.concatenate([before[1], key_raw], 0).astype(jnp.float32)
    value_ext = jnp.concatenate([before[2], value_raw], 0).astype(jnp.float32)
    grad_float = grad_out.astype(jnp.float32)
    queries, keys, values, log_decay, beta_rate = prepare(
        query_ext, key_ext, value_ext, gate_raw, beta_raw, conv_weight, decay_log
    )
    parts = block_parts(queries, keys, log_decay, beta_rate)
    zero_state = jnp.zeros((head_count, head_width, head_width), jnp.float32)
    grad_blocks = to_blocks(grad_float.reshape(length, head_count, head_width))
    trans, offset, adjoint = block_maps(parts, values, beta_rate, grad_blocks)
    local_trans, local_offset, local_adjoint = compose_triples(trans, offset, adjoint)
    ident = identity_maps(local_trans[:, None])
    neutral = jnp.stack([ident, zero_state])

    def move_states(stacked, stride):
        return shifted(stacked, "seq", stride)

    def move_adjoints(stacked, stride):
        return shifted(stacked, "seq", stride)

    prefix = doubling_prefix(
        jnp.stack([local_trans, local_offset]), neutral, forward_join, move_states, False
    )
    suffix = doubling_prefix(
        jnp.stack([local_trans, local_adjoint]), neutral, backward_join, move_adjoints, True
    )
    outputs, pullback = jax.vjp(
        local_run,
        query_ext,
        key_ext,
        value_ext,
        gate_raw,
        beta_raw,
        conv_weight,
        decay_log,
        prefix[1],
    )
    grads = pullback((grad_float, suffix[1]))
    tails = jnp.stack([grads[0][:margin], grads[1][:margin], grads[2][:margin]])
    after = shifted(tails.astype(jnp.bfloat16), "seq", -1).astype(tails.dtype)

    def finish(full, extra):
        owned = full[margin:]
        return jnp.concatenate(
            [owned[: length - margin], owned[length - margin :] + extra], 0
        ).astype(jnp.bfloat16)

    conv_sum, decay_sum = lax.psum((grads[5], grads[6]), "seq")
    return (
        finish(grads[0], after[0]),
        finish(grads[1], after[1]),
        finish(grads[2], after[2]),
        grads[3],
        grads[4],
        conv_sum,
        decay_sum,
    )


def solution(mesh):
    in_specs = (
        P("seq", "head"),
        P("seq", "head"),
        P("seq", "head"),
        P("seq", "head"),
        P("seq", "head"),
        P(None, None, "head"),
        P("head"),
        P("seq", "head"),
    )
    out_specs = (
        P("seq", "head"),
        P("seq", "head"),
        P("seq", "head"),
        P("seq", "head"),
        P("seq", "head"),
        P(None, None, "head"),
        P("head"),
    )
    return jax.shard_map(
        per_device, mesh=mesh, in_specs=in_specs, out_specs=out_specs, check_vma=False
    )
```

profile of v0, /device:TPU:0, one launch (start us, length us, event | category | flops | bytes accessed | tf_op | source)
XLA Modules:
  0.0 1376.3 jit_solution(15598430832608772263)
XLA Ops:
  49.5 14.1 %while.69 = (s32[]{:T(128)}, f32[8,128,128]{2,1,0:T(8,128)S(1)}, f32[8,128,128]{2,1,0:T(8,128)}, f32[8,128,128]{1,2,0:T(8,128)}, f32[2,8,128,128]{3,2,0,1:T(8,12...) while((s32[]{:T(128)}, f32[8,128,128]{2,1,0:T(8,128)S(1)}, ...), condition=%wide.region_4.5_spmd.clone, body=%wide.region_3.4_spmd.clone.sunk | while | flops 604504064 | bytes 16254120 | solution.py:119
  70.3 22.4 %collective-permute-done.9 = f32[2,8,128,128]{3,2,1,0:T(8,128)S(1)} collective-permute-done((f32[2,8,128,128]{3,2,1,0:T(8,128)}, f32[2,8,128,128]{3,2,1,0:T(8,128)S(1)}, u32[]{:S(2)}, u32[]{:S(2)}) %collective-permute-start.9) | collective-permute-done | bytes 1048608 | tf_op jit(solution)/shard_map/ppermute | solution.py:16
  97.2 21.1 %collective-permute-done.10 = f32[2,8,128,128]{3,2,1,0:T(8,128)S(1)} collective-permute-done((f32[2,8,128,128]{3,2,1,0:T(8,128)S(1)}, f32[2,8,128,128]{3,2,1,0:T(8,128)S(1)}, u32[]{:S(2)}, u32[]{:S(2)}) %collective-permute-start.10) | collective-permute-done | bytes 1048608 | tf_op jit(solution)/shard_map/ppermute | solution.py:16
  120.9 7.5 collective-permute-start.11
  128.4 42.1 %collective-permute-done.11 = f32[2,8,128,128]{3,2,1,0:T(8,128)} collective-permute-done((f32[2,8,128,128]{3,2,1,0:T(8,128)}, f32[2,8,128,128]{3,2,1,0:T(8,128)}, u32[]{:S(2)}, u32[]{:S(2)}) %collective-permute-start.11) | collective-permute-done | bytes 1048608 | tf_op jit(solution)/shard_map/ppermute | solution.py:16
  173.5 13.2 collective-permute-start.12
  186.7 43.6 %collective-permute-done.12 = f32[2,8,128,128]{3,2,1,0:T(8,128)} collective-permute-done((f32[2,8,128,128]{3,2,1,0:T(8,128)}, f32[2,8,128,128]{3,2,1,0:T(8,128)}, u32[]{:S(2)}, u32[]{:S(2)}) %collective-permute-start.12) | collective-permute-done | bytes 1048608 | tf_op jit(solution)/shard_map/ppermute | solution.py:16
  233.3 7.9 collective-permute-start.13
  242.4 20.6 %collective-permute-done.13 = f32[2,8,128,128]{3,2,1,0:T(8,128)} collective-permute-done((f32[2,8,128,128]{3,2,1,0:T(8,128)}, f32[2,8,128,128]{3,2,1,0:T(8,128)}, u32[]{:S(2)}, u32[]{:S(2)}) %collective-permute-start.13) | collective-permute-done | bytes 1048608 | tf_op jit(solution)/shard_map/ppermute | solution.py:16
  266.0 8.1 collective-permute-start.14
  274.2 21.1 %collective-permute-done.14 = f32[2,8,128,128]{3,2,1,0:T(8,128)} collective-permute-done((f32[2,8,128,128]{3,2,1,0:T(8,128)}, f32[2,8,128,128]{3,2,1,0:T(8,128)}, u32[]{:S(2)}, u32[]{:S(2)}) %collective-permute-start.14) | collective-permute-done | bytes 1048608 | tf_op jit(solution)/shard_map/ppermute | solution.py:16
  300.5 16.7 %collective-permute-start.15 = (f32[2,8,128,128]{3,2,1,0:T(8,128)}, f32[2,8,128,128]{3,2,1,0:T(8,128)}, u32[]{:S(2)}, u32[]{:S(2)}) collective-permute-start(f32[2,8,128,128]{3,2,1,0:T(8,128)} %pad_maximum_fusion.12), channel_id=1, source_target_pairs={{0,64},{2,66},{4,68},{6,70},{8,72},{10,74},{12,76},{14,78},{16,80}... | collective-permute-start | bytes 3145736 | tf_op jit(solution)/shard_map/ppermute | solution.py:16
  318.5 18.4 %collective-permute-done.15 = f32[2,8,128,128]{3,2,1,0:T(8,128)} collective-permute-done((f32[2,8,128,128]{3,2,1,0:T(8,128)}, f32[2,8,128,128]{3,2,1,0:T(8,128)}, u32[]{:S(2)}, u32[]{:S(2)}) %collective-permute-start.15) | collective-permute-done | bytes 1048608 | tf_op jit(solution)/shard_map/ppermute | solution.py:16
  336.9 5.5 collective-permute-done.2
  351.5 55.3 %collective-permute-done.3 = f32[2,8,128,128]{3,2,1,0:T(8,128)} collective-permute-done((f32[2,8,128,128]{3,2,1,0:T(8,128)}, f32[2,8,128,128]{3,2,1,0:T(8,128)}, u32[]{:S(2)}, u32[]{:S(2)}) %collective-permute-start.3) | collective-permute-done | bytes 1048608 | tf_op jit(solution)/shard_map/ppermute | solution.py:16
  412.6 29.1 %collective-permute-done.4 = f32[2,8,128,128]{3,2,1,0:T(8,128)} collective-permute-done((f32[2,8,128,128]{3,2,1,0:T(8,128)}, f32[2,8,128,128]{3,2,1,0:T(8,128)}, u32[]{:S(2)}, u32[]{:S(2)}) %collective-permute-start.4) | collective-permute-done | bytes 1048608 | tf_op jit(solution)/shard_map/ppermute | solution.py:16
  447.6 33.4 %collective-permute-done.5 = f32[2,8,128,128]{3,2,1,0:T(8,128)} collective-permute-done((f32[2,8,128,128]{3,2,1,0:T(8,128)}, f32[2,8,128,128]{3,2,1,0:T(8,128)}, u32[]{:S(2)}, u32[]{:S(2)}) %collective-permute-start.5) | collective-permute-done | bytes 1048608 | tf_op jit(solution)/shard_map/ppermute | solution.py:16
  490.6 9.1 collective-permute-start.16
  499.8 11.8 collective-permute-done.6
  524.4 17.8 %collective-permute-done.7 = f32[2,8,128,128]{3,2,1,0:T(8,128)} collective-permute-done((f32[2,8,128,128]{3,2,1,0:T(8,128)}, f32[2,8,128,128]{3,2,1,0:T(8,128)}, u32[]{:S(2)}, u32[]{:S(2)}) %collective-permute-start.7) | collective-permute-done | bytes 1048608 | tf_op jit(solution)/shard_map/ppermute | solution.py:16
  550.6 10.9 while.67
  561.4 11.3 collective-permute-done.8
  580.2 32.5 %while.68 = (s32[]{:T(128)}, f32[8,128,128]{2,1,0:T(8,128)S(1)}, f32[2,8,64,128]{3,2,0,1:T(8,128)}, f32[2,8,64,128]{3,2,0,1:T(8,128)}, f32[2,8,64,128]{3,2,0,1:T...) while((s32[]{:T(128)}, f32[8,128,128]{2,1,0:T(8,128)S(1)}, ...), condition=%wide.region_10.11_spmd, body=%wide.region_7.10_spmd.sunk | while | flops 806484480 | bytes 46715652 | solution.py:157
  658.7 714.2 %all-reduce.30 = (f32[3,4,1024]{2,1,0:T(4,128)}, f32[1024]{0:T(1024)}) all-reduce(f32[3,4,1024]{2,1,0:T(4,128)S(1)} %pad_add_fusion.3, f32[1024]{0:T(1024)S(1)} %negate_multiply_fusion), channel_id=1, replica_groups=mesh['seq'=128,'head'=2] {'seq'}, use_global_device_ids=true, to_apply=%region_31.32 | all-reduce | flops 13312 | bytes 106496 | tf_op jit(solution)/shard_map/psum | solution.py:257
  (656 shorter events, 242.0 us)
Async XLA Ops:
  2.1 7.8 collective-permute-start
  28.8 11.4 copy-start.8
  32.8 485.2 %copy-start = (f32[16,8,8,128]{3,2,1,0:T(8,128)}, f32[16,8,8,128]{3,2,1,0:T(8,128)S(1)}, u32[]{:S(2)}) copy-start(f32[16,8,8,128]{3,2,1,0:T(8,128)S(1)} %copy.395) | copy-start | bytes 1572868
  66.5 26.3 %collective-permute-start.9 = (f32[2,8,128,128]{3,2,1,0:T(8,128)}, f32[2,8,128,128]{3,2,1,0:T(8,128)S(1)}, u32[]{:S(2)}, u32[]{:S(2)}) collective-permute-start(f32[2,8,128,128]{3,2,1,0:T(8,128)} %get-tuple-element.878), channel_id=1, source_target_pairs={{0,2},{2,4},{4,6},{6,8},{8,10},{10,12},{12,14},{14,16},{16,18},{18... | collective-permute-start | bytes 3145736 | tf_op jit(solution)/shard_map/ppermute | solution.py:16
  92.9 25.5 %collective-permute-start.10 = (f32[2,8,128,128]{3,2,1,0:T(8,128)S(1)}, f32[2,8,128,128]{3,2,1,0:T(8,128)S(1)}, u32[]{:S(2)}, u32[]{:S(2)}) collective-permute-start(f32[2,8,128,128]{3,2,1,0:T(8,128)S(1)} %pad_select_fusion.5), channel_id=1, source_target_pairs={{0,2},{2,4},{4,6},{6,8},{8,10},{10,12},{12,14},{14,16},{16,18},{18... | collective-permute-start | bytes 3145736 | tf_op jit(solution)/shard_map/ppermute | solution.py:16
  120.9 49.6 %collective-permute-start.11 = (f32[2,8,128,128]{3,2,1,0:T(8,128)}, f32[2,8,128,128]{3,2,1,0:T(8,128)}, u32[]{:S(2)}, u32[]{:S(2)}) collective-permute-start(f32[2,8,128,128]{3,2,1,0:T(8,128)} %pad_maximum_fusion.8), channel_id=1, source_target_pairs={{0,4},{2,6},{4,8},{6,10},{8,12},{10,14},{12,16},{14,18},{16,20},{1... | collective-permute-start | bytes 3145736 | tf_op jit(solution)/shard_map/ppermute | solution.py:16
  173.5 56.8 %collective-permute-start.12 = (f32[2,8,128,128]{3,2,1,0:T(8,128)}, f32[2,8,128,128]{3,2,1,0:T(8,128)}, u32[]{:S(2)}, u32[]{:S(2)}) collective-permute-start(f32[2,8,128,128]{3,2,1,0:T(8,128)} %pad_maximum_fusion.9), channel_id=1, source_target_pairs={{0,8},{2,10},{4,12},{6,14},{8,16},{10,18},{12,20},{14,22},{16,24},... | collective-permute-start | bytes 3145736 | tf_op jit(solution)/shard_map/ppermute | solution.py:16
  233.3 29.8 %collective-permute-start.13 = (f32[2,8,128,128]{3,2,1,0:T(8,128)}, f32[2,8,128,128]{3,2,1,0:T(8,128)}, u32[]{:S(2)}, u32[]{:S(2)}) collective-permute-start(f32[2,8,128,128]{3,2,1,0:T(8,128)} %pad_maximum_fusion.10), channel_id=1, source_target_pairs={{0,16},{2,18},{4,20},{6,22},{8,24},{10,26},{12,28},{14,30},{16,32}... | collective-permute-start | bytes 3145736 | tf_op jit(solution)/shard_map/ppermute | solution.py:16
  241.2 33.0 %collective-permute-start.1 = (f32[2,8,128,128]{3,2,1,0:T(8,128)}, f32[2,8,128,128]{3,2,1,0:T(8,128)}, u32[]{:S(2)}, u32[]{:S(2)}) collective-permute-start(f32[2,8,128,128]{3,2,1,0:T(8,128)} %get-tuple-element.879), channel_id=1, source_target_pairs={{2,0},{4,2},{6,4},{8,6},{10,8},{12,10},{14,12},{16,14},{18,16},{20... | collective-permute-start | bytes 3145736 | tf_op jit(solution)/shard_map/ppermute | solution.py:16
  266.0 29.2 %collective-permute-start.14 = (f32[2,8,128,128]{3,2,1,0:T(8,128)}, f32[2,8,128,128]{3,2,1,0:T(8,128)}, u32[]{:S(2)}, u32[]{:S(2)}) collective-permute-start(f32[2,8,128,128]{3,2,1,0:T(8,128)} %pad_maximum_fusion.11), channel_id=1, source_target_pairs={{0,32},{2,34},{4,36},{6,38},{8,40},{10,42},{12,44},{14,46},{16,48}... | collective-permute-start | bytes 3145736 | tf_op jit(solution)/shard_map/ppermute | solution.py:16
  300.5 36.4 %collective-permute-start.15 = (f32[2,8,128,128]{3,2,1,0:T(8,128)}, f32[2,8,128,128]{3,2,1,0:T(8,128)}, u32[]{:S(2)}, u32[]{:S(2)}) collective-permute-start(f32[2,8,128,128]{3,2,1,0:T(8,128)} %pad_maximum_fusion.12), channel_id=1, source_target_pairs={{0,64},{2,66},{4,68},{6,70},{8,72},{10,74},{12,76},{14,78},{16,80}... | collective-permute-start | bytes 3145736 | tf_op jit(solution)/shard_map/ppermute | solution.py:16
  317.2 25.2 %collective-permute-start.2 = (f32[2,8,128,128]{3,2,1,0:T(8,128)}, f32[2,8,128,128]{3,2,1,0:T(8,128)}, u32[]{:S(2)}, u32[]{:S(2)}) collective-permute-start(f32[2,8,128,128]{3,2,1,0:T(8,128)} %get-tuple-element.877), channel_id=1, source_target_pairs={{2,0},{4,2},{6,4},{8,6},{10,8},{12,10},{14,12},{16,14},{18,16},{20... | collective-permute-start | bytes 3145736 | tf_op jit(solution)/shard_map/ppermute | solution.py:16
  350.2 56.6 %collective-permute-start.3 = (f32[2,8,128,128]{3,2,1,0:T(8,128)}, f32[2,8,128,128]{3,2,1,0:T(8,128)}, u32[]{:S(2)}, u32[]{:S(2)}) collective-permute-start(f32[2,8,128,128]{3,2,1,0:T(8,128)} %pad_maximum_fusion.2), channel_id=1, source_target_pairs={{4,0},{6,2},{8,4},{10,6},{12,8},{14,10},{16,12},{18,14},{20,16},{2... | collective-permute-start | bytes 3145736 | tf_op jit(solution)/shard_map/ppermute | solution.py:16
  351.4 56.7 %copy-start.42 = (f32[8,128,128]{2,1,0:T(8,128)S(1)}, f32[8,128,128]{2,1,0:T(8,128)}, u32[]{:S(2)}) copy-start(f32[8,128,128]{2,1,0:T(8,128)} %copy-done.41) | copy-start | bytes 1572868
  411.3 30.4 %collective-permute-start.4 = (f32[2,8,128,128]{3,2,1,0:T(8,128)}, f32[2,8,128,128]{3,2,1,0:T(8,128)}, u32[]{:S(2)}, u32[]{:S(2)}) collective-permute-start(f32[2,8,128,128]{3,2,1,0:T(8,128)} %pad_maximum_fusion.3), channel_id=1, source_target_pairs={{8,0},{10,2},{12,4},{14,6},{16,8},{18,10},{20,12},{22,14},{24,16},... | collective-permute-start | bytes 3145736 | tf_op jit(solution)/shard_map/ppermute | solution.py:16
  446.3 34.7 %collective-permute-start.5 = (f32[2,8,128,128]{3,2,1,0:T(8,128)}, f32[2,8,128,128]{3,2,1,0:T(8,128)}, u32[]{:S(2)}, u32[]{:S(2)}) collective-permute-start(f32[2,8,128,128]{3,2,1,0:T(8,128)} %pad_maximum_fusion.4), channel_id=1, source_target_pairs={{16,0},{18,2},{20,4},{22,6},{24,8},{26,10},{28,12},{30,14},{32,16}... | collective-permute-start | bytes 3145736 | tf_op jit(solution)/shard_map/ppermute | solution.py:16
  447.6 34.7 %copy-start.40 = (f32[8,128,128]{2,1,0:T(8,128)S(1)}, f32[8,128,128]{2,1,0:T(8,128)}, u32[]{:S(2)}) copy-start(f32[8,128,128]{2,1,0:T(8,128)} %copy-done.39) | copy-start | bytes 1572868
  485.6 25.9 %collective-permute-start.6 = (f32[2,8,128,128]{3,2,1,0:T(8,128)}, f32[2,8,128,128]{3,2,1,0:T(8,128)}, u32[]{:S(2)}, u32[]{:S(2)}) collective-permute-start(f32[2,8,128,128]{3,2,1,0:T(8,128)} %pad_maximum_fusion.5), channel_id=1, source_target_pairs={{32,0},{34,2},{36,4},{38,6},{40,8},{42,10},{44,12},{46,14},{48,16}... | collective-permute-start | bytes 3145736 | tf_op jit(solution)/shard_map/ppermute | solution.py:16
  490.6 22.2 %copy-start.91 = (f32[8,128,128]{2,1,0:T(8,128)S(1)}, f32[8,128,128]{2,1,0:T(8,128)}, u32[]{:S(2)}) copy-start(f32[8,128,128]{2,1,0:T(8,128)} %copy-done.90) | copy-start | bytes 1572868
  490.6 31.5 %collective-permute-start.16 = (f32[2,8,128,128]{3,2,1,0:T(8,128)}, f32[2,8,128,128]{3,2,1,0:T(8,128)}, u32[]{:S(2)}, u32[]{:S(2)}) collective-permute-start(f32[2,8,128,128]{3,2,1,0:T(8,128)} %pad_maximum_fusion.13), channel_id=1, source_target_pairs={{0,128},{2,130},{4,132},{6,134},{8,136},{10,138},{12,140},{14,142}... | collective-permute-start | bytes 3145736 | tf_op jit(solution)/shard_map/ppermute | solution.py:16
  515.7 26.4 %collective-permute-start.7 = (f32[2,8,128,128]{3,2,1,0:T(8,128)}, f32[2,8,128,128]{3,2,1,0:T(8,128)}, u32[]{:S(2)}, u32[]{:S(2)}) collective-permute-start(f32[2,8,128,128]{3,2,1,0:T(8,128)} %pad_maximum_fusion.6), channel_id=1, source_target_pairs={{64,0},{66,2},{68,4},{70,6},{72,8},{74,10},{76,12},{78,14},{80,16}... | collective-permute-start | bytes 3145736 | tf_op jit(solution)/shard_map/ppermute | solution.py:16
  524.3 19.1 %copy-start.38 = (f32[8,128,128]{2,1,0:T(8,128)S(1)}, f32[8,128,128]{2,1,0:T(8,128)}, u32[]{:S(2)}) copy-start(f32[8,128,128]{2,1,0:T(8,128)} %copy-done.37) | copy-start | bytes 1572868
  546.7 26.0 %collective-permute-start.8 = (f32[2,8,128,128]{3,2,1,0:T(8,128)}, f32[2,8,128,128]{3,2,1,0:T(8,128)}, u32[]{:S(2)}, u32[]{:S(2)}) collective-permute-start(f32[2,8,128,128]{3,2,1,0:T(8,128)} %pad_maximum_fusion.7), channel_id=1, source_target_pairs={{128,0},{130,2},{132,4},{134,6},{136,8},{138,10},{140,12},{142,14}... | collective-permute-start | bytes 3145736 | tf_op jit(solution)/shard_map/ppermute | solution.py:16
  657.3 715.8 %collective-permute-start.17 = (bf16[3,3,1024]{2,1,0:T(4,128)(2,1)S(1)}, bf16[3,3,1024]{2,1,0:T(4,128)(2,1)S(1)}, u32[]{:S(2)}, u32[]{:S(2)}) collective-permute-start(bf16[3,3,1024]{2,1,0:T(4,128)(2,1)S(1)} %pad_maximum_fusion.18), channel_id=1, source_target_pairs={{2,0},{4,2},{6,4},{8,6},{10,8},{12,10},{14,12},{16,14},{18,16},{20... | collective-permute-start | bytes 55304 | tf_op jit(solution)/shard_map/ppermute | solution.py:16
  (180 other events, 251.7 us)
where the time goes:
time: 1390 us; the launch traced here: 1380 us
  blocking collectives  714 us (51%)
  waiting for transfers between devices  354 us (25%)
  matrix products  110 us (8%)
  starting transfers between devices  84.5 us (6%)
  local copies, waits for them, and re-layouts  61.6 us (4%)
  other arithmetic  48.6 us (3%)
    psum x1, blocking collectives, per_device(): conv_sum, decay_sum = lax.psum((grads[5], grads[6]), 'seq')  714 us
    ppermute x18, waiting for transfers between devices, shifted(): return lax.ppermute(block, axis, route)  354 us
    dot_general x101, matrix products, product(): return jnp.einsum(formula, left, right, precision=largest_entry)  110 us
    ppermute x18, starting transfers between devices, shifted(): return lax.ppermute(block, axis, route)  84.5 us
  transfers between devices with their start and end apart: 18, of which 14 were waited for; matrix products, arithmetic and copies ran while one was open for 2% of the time, Pallas kernels for 0%

commit v1 on v0

v1 whole, which is shorter than its diff:
```python
import functools

import jax
import jax.numpy as jnp
from jax import lax
from jax.experimental import pallas as pl
from jax.experimental.pallas import tpu as pltpu
from jax.sharding import Mesh
from jax.sharding import PartitionSpec as P

F32 = jnp.float32
BF16 = jnp.bfloat16
EPS = 1e-06
T = 128
SEQ = ("y", "x", "z")
NN = (((1,), (0,)), ((), ()))
NT = (((1,), (1,)), ((), ()))
TN = (((0,), (0,)), ((), ()))
MIB = 1024 * 1024


def split(x):
    hi = x.astype(BF16)
    return (hi, (x - hi.astype(F32)).astype(BF16))


def dot(a, b, dims):
    total = None
    for i, left in enumerate(a):
        for j, right in enumerate(b):
            if i + j < 2:
                term = lax.dot_general(left, right, dims, preferred_element_type=F32)
                total = term if total is None else total + term
    return total


def lanes(*parts):
    return tuple(jnp.concatenate(terms, axis=1) for terms in zip(*parts))


def rows(*parts):
    return tuple(jnp.concatenate(terms, axis=0) for terms in zip(*parts))


def iota(shape, dim):
    return lax.broadcasted_iota(jnp.int32, shape, dim)


def sigmoid(x):
    return 1.0 / (1.0 + jnp.exp(-x))


def column(block, head):
    return jnp.sum(jnp.where(iota(block.shape, 1) == head, block, 0.0), axis=1, keepdims=True)


def gate_factors(cumul):
    row = iota((T, T), 0)
    late = row >= T // 2
    mid0 = cumul[T // 4 : T // 4 + 1]
    mid1 = cumul[3 * T // 4 : 3 * T // 4 + 1]
    last = cumul[T - 1 : T]
    up0 = jnp.exp(cumul - mid0)
    up1 = jnp.where(late, jnp.exp(jnp.where(late, cumul - mid1, 0.0)), 0.0)
    down = jnp.exp(jnp.where(late, mid1, mid0) - cumul)
    return up0, up1, down, jnp.exp(cumul), jnp.exp(last - cumul), jnp.exp(last), late


def unit_inverse(coupling):
    row, col = iota((T, T), 0), iota((T, T), 1)
    ident = jnp.where(row == col, 1.0, 0.0)

    def same(size):
        return (row // size) == (col // size)

    inner = [jnp.where(same(16), c, 0.0) for c in coupling]
    result = [ident - c for c in inner]
    power = []
    for c in inner:
        s = split(c)
        power.append(dot(s, s, NN))
    for level in range(2):
        out = []
        for p, r in zip(power, result):
            s = split(p)
            out.append(dot(rows(s, split(r)), s, NN))
        power = [o[:T] for o in out]
        result = [r + o[T:] for r, o in zip(result, out)]
    result = [r + dot(split(r), split(p), NN) for r, p in zip(result, power)]
    for size in (32, 64, 128):
        pick = same(size) & ~same(size // 2)
        parts = [split(r) for r in result]
        half = [dot(split(jnp.where(pick, c, 0.0)), s, NN) for c, s in zip(coupling, parts)]
        result = [r - dot(s, split(h), NN) for r, s, h in zip(result, parts, half)]
    return result


def maps_kernel(
    heads,
    q_ref, k_ref, v_ref, halo_ref, gate_ref, beta_ref, conv_ref, decay_ref, grad_ref,
    maps_ref, q_out, k_out, fq_out, fk_out, fv_out, cum_out, gf_out, ld_out, w_out, u_out, pg_out, inv_out,
    ext,
):
    row, col = iota((T, T), 0), iota((T, T), 1)
    strict = row > col
    lower = row >= col
    ident = jnp.where(row == col, 1.0, 0.0)
    tri = jnp.where(lower, 1.0, 0.0).astype(BF16)
    beta_all = sigmoid(beta_ref[...])
    base = pl.program_id(0) * heads
    each = range(heads)
    at = [slice(h * T, (h + 1) * T) for h in each]
    cumul, qs, ks, vs, betas = [], [], [], [], []
    for h in each:
        gate = gate_ref[:, at[h]]
        speed = -jnp.exp(decay_ref[:, at[h]])
        log_decay = speed * (jnp.maximum(gate, 0.0) + jnp.log1p(jnp.exp(-jnp.abs(gate))))
        ld_out[:, at[h]] = log_decay
        gf_out[:, at[h]] = speed * sigmoid(gate)
        both = lax.dot_general(
            tri, jnp.concatenate(split(log_decay), axis=1), NN, preferred_element_type=F32
        )
        cumul.append(both[:, :T] + both[:, T:])
        cum_out[:, at[h]] = cumul[h]
        betas.append(column(beta_all, base + h))
        acts = []
        for j, (raw, factor) in enumerate(((q_ref, fq_out), (k_ref, fk_out), (v_ref, fv_out))):
            ext[j, h, 0:8] = halo_ref[j, :, at[h]].astype(F32)
            ext[j, h, 8:136] = raw[:, at[h]].astype(F32)
            pre = conv_ref[j, 0:1, at[h]] * ext[j, h, 5 : 5 + T]
            for i in range(1, 4):
                pre = pre + conv_ref[j, i : i + 1, at[h]] * ext[j, h, 5 + i : 5 + i + T]
            s = sigmoid(pre)
            act = pre * s
            slope = s * (1.0 + pre * (1.0 - s))
            if j < 2:
                scale = lax.rsqrt(jnp.sum(act * act, axis=1, keepdims=True) + EPS)
                act = act * scale
                slope = slope * scale
            factor[:, at[h]] = slope
            acts.append(act)
        qs.append(acts[0])
        ks.append(acts[1])
        vs.append(acts[2])
        q_out[:, at[h]] = acts[0]
        k_out[:, at[h]] = acts[1]
    factors = [gate_factors(c) for c in cumul]
    couple, attend = [], []
    for h in each:
        up0, up1, down, full, end, last, late = factors[h]
        kd = ks[h] * down
        right = lanes(split(jnp.where(late, 0.0, kd)), split(jnp.where(late, kd, 0.0)))
        left = rows(
            lanes(split(ks[h] * up0), split(ks[h] * up1)), lanes(split(qs[h] * up0), split(qs[h] * up1))
        )
        both = dot(left, right, NT)
        couple.append(jnp.where(strict, both[:T], 0.0) * betas[h])
        attend.append(jnp.where(lower, both[T:], 0.0))
    inverse = unit_inverse(couple)
    for h in each:
        up0, up1, down, full, end, last, late = factors[h]
        inv_out[h] = inverse[h]
        both = dot(
            split(inverse[h]), lanes(split(betas[h] * ks[h] * full), split(betas[h] * vs[h])), NN
        )
        w, u = both[:, :T], both[:, T:]
        w_out[h] = w
        u_out[h] = u
        both = dot(split(ks[h] * end), split(both), TN)
        maps_ref[h, 0:T] = ident * last - both[:, :T]
        maps_ref[h, T : 2 * T] = both[:, T:]
        grad = (grad_ref[:, at[h]],)
        pg = dot(split(attend[h]), grad, TN)
        pg_out[h] = pg
        maps_ref[h, 2 * T : 3 * T] = dot(split(qs[h] * full), grad, TN) - dot(split(w), split(pg), TN)


def join(early, late):
    ea, eb, ed = early
    la, lb, ld = late
    sa = split(ea)
    both = dot(split(la), lanes(sa, split(eb)), NN)
    return (both[:, :T], both[:, T:] + lb, ed + dot(sa, split(ld), TN))


def tree(items):
    while len(items) > 1:
        items = [join(items[i], items[i + 1]) for i in range(0, len(items), 2)]
    return items[0]


def triple(ref, i):
    return tuple(ref[i, m * T : (m + 1) * T] for m in range(3))


def line_kernel(maps_ref, out_ref):
    total = tree([triple(maps_ref, i) for i in range(maps_ref.shape[0])])
    for m in range(3):
        out_ref[m * T : (m + 1) * T] = total[m]


def plane_kernel(where_ref, lines_ref, out_ref):
    count = lines_ref.shape[0]
    mine = where_ref[1]
    total = tree([triple(lines_ref, lax.rem(mine - i + count, count)) for i in range(count)])
    for m in range(3):
        out_ref[m * T : (m + 1) * T] = total[m]


def states_kernel(where_ref, maps_ref, lines_ref, planes_ref, out_ref):
    state = jnp.zeros((T, T), F32)
    grad = jnp.zeros((T, T), F32)
    for ref, mine in ((planes_ref, where_ref[0]), (lines_ref, where_ref[1])):
        count = ref.shape[0]
        for i in range(count - 1):
            slot = lax.rem(mine - i + count, count)
            a, b, d = triple(ref, slot)
            state = jnp.where(i < mine, dot(split(a), split(state), NN) + b, state)
            j = count - 1 - i
            slot = lax.rem(mine - j + count, count)
            a, b, d = triple(ref, slot)
            grad = jnp.where(j > mine, dot(split(a), split(grad), TN) + d, grad)
    count = maps_ref.shape[0]
    for i in range(count):
        j = count - 1 - i
        out_ref[i, 0:T] = state
        out_ref[j, T : 2 * T] = grad
        if i < count - 1:
            a, b, d = triple(maps_ref, i)
            state = dot(split(a), split(state), NN) + b
            a, b, d = triple(maps_ref, j)
            grad = dot(split(a), split(grad), TN) + d


def grads_kernel(
    heads,
    q_ref, k_ref, v_ref, halo_ref, beta_ref, conv_ref, grad_ref, states_ref,
    q_in, k_in, fq_in, fk_in, fv_in, cum_in, gf_in, ld_in, w_in, u_in, pg_in, inv_in,
    dq_out, dk_out, dv_out, edge_out, tail_out, dgate_out, dbeta_out, param_out,
    ext, back,
):
    row, col = iota((T, T), 0), iota((T, T), 1)
    strict = row > col
    lower = row >= col
    upper = jnp.where(row <= col, 1.0, 0.0).astype(BF16)
    ones = jnp.ones((8, T), BF16)
    beta_all = sigmoid(beta_ref[...])
    base = pl.program_id(0) * heads
    each = range(heads)
    at = [slice(h * T, (h + 1) * T) for h in each]
    deltas, dds, grads = [], [], []
    betas = [column(beta_all, base + h) for h in each]
    factors = [gate_factors(cum_in[:, at[h]]) for h in each]
    ms = [split(states_ref[h, 0:T]) for h in each]
    gs = [split(states_ref[h, T : 2 * T]) for h in each]
    qs = [q_in[:, at[h]] for h in each]
    ks = [k_in[:, at[h]] for h in each]
    dbeta = jnp.zeros(dbeta_out.shape, F32)
    for h in each:
        deltas.append(u_in[h] - dot(split(w_in[h]), ms[h], NN))
        dds.append(pg_in[h] + dot(split(ks[h] * factors[h][4]), gs[h], NN))
    des = [dot(split(inv_in[h]), split(dds[h]), TN) for h in each]
    dvs = [betas[h] * des[h] for h in each]
    dsp = [split(deltas[h]) for h in each]
    firsts = []
    for h in each:
        grad = grad_ref[:, at[h]]
        left = rows((grad, jnp.zeros_like(grad)), split(-dvs[h]))
        firsts.append(dot(left, rows(dsp[h], ms[h]), NT))
    ends = [dot(dsp[h], gs[h], NT) for h in each]
    for h in each:
        up0, up1, down, full, end, last, late = factors[h]
        q, k = qs[h], ks[h]
        first = firsts[h]
        sp = split(jnp.where(lower, first[:T, :T], 0.0))
        sl = split(jnp.where(strict, first[T:, :T], 0.0))
        kd = k * down
        right = lanes(split(jnp.where(late, 0.0, kd)), split(jnp.where(late, kd, 0.0)))
        by_row = dot(rows(sp, sl), right, NN)
        up = rows(lanes(split(k * up0), split(k * up1)), lanes(split(q * up0), split(q * up1)))
        by_col = dot(rows(sl, sp), up, TN)
        dq = full * first[:T, T:] + up0 * by_row[:T, :T] + up1 * by_row[:T, T:]
        dk_row = full * first[T:, T:] + up0 * by_row[T:, :T] + up1 * by_row[T:, T:]
        dk_end = end * ends[h]
        dk_col = down * jnp.where(late, by_col[:, T:], by_col[:, :T]) + dk_end
        dk = dk_row + dk_col
        dcum = q * dq + k * (dk_row - dk_col)
        held = states_ref[h, 0:T] * states_ref[h, T : 2 * T]
        dlast = jnp.sum(k * dk_end, axis=0, keepdims=True) + last * dot((ones,), split(held), NT)[0:1]
        both = lax.dot_general(
            upper, jnp.concatenate(split(dcum), axis=1), NN, preferred_element_type=F32
        )
        dlog = both[:, :T] + both[:, T:] + dlast
        dgate_out[:, at[h]] = dlog * gf_in[:, at[h]]
        param_out[12:13, at[h]] = jnp.sum(dlog * ld_in[:, at[h]], axis=0, keepdims=True)
        write = jnp.sum(des[h] * deltas[h], axis=1, keepdims=True) * (1.0 - betas[h])
        dbeta = jnp.where(iota(dbeta.shape, 1) == base + h, write, dbeta)
        pres = (
            fq_in[:, at[h]] * (dq - q * jnp.sum(q * dq, axis=1, keepdims=True)),
            fk_in[:, at[h]] * (dk - k * jnp.sum(k * dk, axis=1, keepdims=True)),
            fv_in[:, at[h]] * dvs[h],
        )
        for j, (raw, out) in enumerate(((q_ref, dq_out), (k_ref, dk_out), (v_ref, dv_out))):
            ext[j, h, 0:8] = halo_ref[j, :, at[h]].astype(F32)
            ext[j, h, 8:136] = raw[:, at[h]].astype(F32)
            back[j, h, 0:8] = jnp.zeros((8, T), F32)
            back[j, h, 8:136] = pres[j]
            back[j, h, 136:144] = jnp.zeros((8, T), F32)
            whole = None
            for i in range(4):
                part = conv_ref[j, i : i + 1, at[h]] * back[j, h, 3 - i : 3 - i + 136]
                whole = part if whole is None else whole + part
                param_out[4 * j + i : 4 * j + i + 1, at[h]] = jnp.sum(
                    pres[j] * ext[j, h, 5 + i : 5 + i + T], axis=0, keepdims=True
                )
            out[:, at[h]] = whole[8:136].astype(BF16)
            tail_out[j, :, at[h]] = whole[0:8]
            edge_out[j, :, at[h]] = whole[120:136]
    param_out[13:16] = jnp.zeros((3, heads * T), F32)

    @pl.when(pl.program_id(0) == 0)
    def _():
        dbeta_out[...] = dbeta

    @pl.when(pl.program_id(0) > 0)
    def _():
        dbeta_out[...] = dbeta_out[...] + dbeta


def per_device(query_raw, key_raw, value_raw, gate_raw, beta_raw, conv_weight, decay_log, grad_out):
    length, channels = gate_raw.shape
    count = beta_raw.shape[1]
    lines, planes = lax.axis_size("x"), lax.axis_size("y")
    depth = lax.axis_size("z")
    devices = lines * planes * depth
    heads = GROUP
    wide = heads * T
    wheres = jnp.stack([lax.axis_index("y"), lax.axis_index("x")]).astype(jnp.int32)
    ends = jnp.stack([query_raw[length - 8 :], key_raw[length - 8 :], value_raw[length - 8 :]])
    halo = lax.ppermute(ends, SEQ, [(i, i + 1) for i in range(devices - 1)])
    decay_row = decay_log.reshape(1, channels)

    tall = pl.BlockSpec((T, wide), lambda h: (0, h))
    edge = pl.BlockSpec((3, 8, wide), lambda h: (0, 0, h))
    taps = pl.BlockSpec((3, 4, wide), lambda h: (0, 0, h))
    beta_spec = pl.BlockSpec((T, count), lambda h: (0, 0))
    square = pl.BlockSpec((heads, T, T), lambda h: (h, 0, 0))

    def stack_spec(n):
        return pl.BlockSpec((heads, n * T, T), lambda h: (h, 0, 0))

    def like(*shape, dtype=F32):
        return jax.ShapeDtypeStruct(shape, dtype)

    params = pltpu.CompilerParams(
        dimension_semantics=("arbitrary",), vmem_limit_bytes=48 * MIB
    )
    saved_shapes = [like(length, channels)] * 8 + [like(count, T, T)] * 4
    saved_specs = [tall] * 8 + [square] * 4
    maps, *saved = pl.pallas_call(
        functools.partial(maps_kernel, heads),
        grid=(count // heads,),
        in_specs=[tall, tall, tall, edge, tall, beta_spec, taps, pl.BlockSpec((1, wide), lambda h: (0, h)), tall],
        out_specs=[stack_spec(3)] + saved_specs,
        out_shape=[like(count, 3 * T, T)] + saved_shapes,
        scratch_shapes=[pltpu.VMEM((3, heads, 136, T), F32)],
        compiler_params=params,
        name="block_maps",
    )(query_raw, key_raw, value_raw, halo, gate_raw, beta_raw, conv_weight, decay_row, grad_out)

    line_maps = lax.all_to_all(maps, "z", 0, 0, tiled=True)
    line_total = pl.pallas_call(
        line_kernel, out_shape=like(3 * T, T), name="line_total",
        compiler_params=pltpu.CompilerParams(vmem_limit_bytes=32 * MIB),
    )(line_maps)

    def around(block, axis):
        size = lax.axis_size(axis)
        moved = [
            lax.ppermute(block, axis, [(i, (i + d) % size) for i in range(size)])
            for d in range(1, size)
        ]
        return [block] + moved

    smem = pl.BlockSpec(memory_space=pltpu.SMEM)
    vmem = pl.BlockSpec(memory_space=pltpu.VMEM)
    line_totals = jnp.stack(around(line_total, "x"))
    plane_total = pl.pallas_call(
        plane_kernel, out_shape=like(3 * T, T), in_specs=[smem, vmem], name="plane_total",
        compiler_params=pltpu.CompilerParams(vmem_limit_bytes=32 * MIB),
    )(wheres, line_totals)
    plane_totals = jnp.stack(around(plane_total, "y"))
    line_states = pl.pallas_call(
        states_kernel, out_shape=like(depth, 2 * T, T), in_specs=[smem, vmem, vmem, vmem], name="line_states",
        compiler_params=pltpu.CompilerParams(vmem_limit_bytes=32 * MIB),
    )(wheres, line_maps, line_totals, plane_totals)
    states = lax.all_to_all(line_states, "z", 0, 0, tiled=True)

    dq, dk, dv, edges, tails, dgate, dbeta, partial = pl.pallas_call(
        functools.partial(grads_kernel, heads),
        grid=(count // heads,),
        in_specs=[tall, tall, tall, edge, beta_spec, taps, tall, stack_spec(2)] + saved_specs,
        out_specs=[
            tall, tall, tall,
            pl.BlockSpec((3, 16, wide), lambda h: (0, 0, h)), edge, tall, beta_spec,
            pl.BlockSpec((16, wide), lambda h: (0, h)),
        ],
        out_shape=[like(length, channels, dtype=BF16)] * 3
        + [like(3, 16, channels), like(3, 8, channels), like(length, channels), like(length, count), like(16, channels)],
        scratch_shapes=[pltpu.VMEM((3, heads, 136, T), F32), pltpu.VMEM((3, heads, 144, T), F32)],
        compiler_params=params,
        name="block_grads",
    )(query_raw, key_raw, value_raw, halo, beta_raw, conv_weight, grad_out, states, *saved)

    after = lax.ppermute(tails, SEQ, [(i + 1, i) for i in range(devices - 1)])
    fixed = edges + jnp.pad(after, ((0, 0), (8, 0), (0, 0)))

    def finish(full, extra):
        return lax.dynamic_update_slice(full, extra.astype(BF16), (length - 16, 0))

    total = partial
    for axis in ("x", "y"):
        own, one, two, three = around(total, axis)
        total = (own + two) + (one + three)
    for stride in (1, 2, 4):
        total = total + lax.ppermute(total, "z", [(i, i ^ stride) for i in range(depth)])
    return (
        finish(dq, fixed[0]),
        finish(dk, fixed[1]),
        finish(dv, fixed[2]),
        dgate,
        dbeta,
        total[:12].reshape(3, 4, channels),
        total[12],
    )


GROUP = 2


def solution(mesh):
    inner = Mesh(mesh.devices.reshape(4, 4, 8, 2), SEQ + ("head",))
    wide = P(SEQ, "head")
    in_specs = (wide, wide, wide, wide, wide, P(None, None, "head"), P("head"), wide)
    out_specs = (wide, wide, wide, wide, wide, P(None, None, "head"), P("head"))
    return jax.shard_map(
        per_device, mesh=inner, in_specs=in_specs, out_specs=out_specs, check_vma=False
    )
```

time: 1390 us -> 188 us (0.14)
  blocking collectives: 714 us -> 83.6 us
  waiting for transfers between devices: 354 us -> 41.5 us
  matrix products: 110 us -> 0 us
  starting transfers between devices: 84.5 us -> 19.8 us
  local copies, waits for them, and re-layouts: 61.6 us -> 10.1 us
  other arithmetic: 48.6 us -> 1.38 us
  Pallas kernels: 0 us -> 29.9 us
    psum x1 -> x0, blocking collectives: 714 us -> none  [per_device(): conv_sum, decay_sum = lax.psum((grads[5], grads[6]), 'seq')]
    ppermute x18 -> x17, waiting for transfers between devices: 354 us -> 41.5 us  [the longest x12 25 us: around(): lax.ppermute(block, axis, [(i, (i + d) % size) for i in range(size)])]
    dot_general x101 -> x0, matrix products: 110 us -> none  [product(): return jnp.einsum(formula, left, right, precision=largest_entry)]
    all_to_all x0 -> x2, blocking collectives: none -> 83.6 us  [the longest x1 48.9 us: per_device(): line_maps = lax.all_to_all(maps, 'z', 0, 0, tiled=True)]
    ppermute x18 -> x17, starting transfers between devices: 84.5 us -> 19.8 us  [the longest x12 14 us: around(): lax.ppermute(block, axis, [(i, (i + d) % size) for i in range(size)])]
    pallas_call x0 -> x5, Pallas kernels: none -> 29.9 us  [the longest x1 16.4 us: per_device(): pl.pallas_call(functools.partial(maps_kernel, heads), grid=(count // head...]
    while x107 -> x0, local copies, waits for them, and re-layouts: 19.2 us -> none
    another operation x21 -> x5, other arithmetic: 18.3 us -> 1.32 us  [the longest x1 1.17 us: per_device(): line_totals = jnp.stack(around(line_total, 'x'))]
  transfers between devices with their start and end apart: 18 -> 17, of which waited for: 14 -> 16; matrix products, arithmetic and copies ran while one was open for 2% -> 1% of each run, Pallas kernels for 0% -> 0%
where the time goes in v1:
time: 188 us; the launch traced here: 187 us
  blocking collectives  83.6 us (44%)
  waiting for transfers between devices  41.5 us (22%)
  Pallas kernels  29.9 us (16%)
  starting transfers between devices  19.8 us (11%)
  local copies, waits for them, and re-layouts  10.1 us (5%)
    all_to_all x1, blocking collectives, per_device(): line_maps = lax.all_to_all(maps, 'z', 0, 0, tiled=True)  48.9 us
    all_to_all x1, blocking collectives, per_device(): states = lax.all_to_all(line_states, 'z', 0, 0, tiled=True)  34.6 us
    ppermute x12, waiting for transfers between devices, around(): lax.ppermute(block, axis, [(i, (i + d) % size) for i in range(size)])  25 us
    pallas_call x1, Pallas kernels, per_device(): pl.pallas_call(functools.partial(maps_kernel, heads), grid=(count // head...  16.4 us
    ppermute x3, waiting for transfers between devices, per_device(): lax.ppermute(total, 'z', [(i, i ^ stride) for i in range(depth)])  15.5 us
    ppermute x12, starting transfers between devices, around(): lax.ppermute(block, axis, [(i, (i + d) % size) for i in range(size)])  14 us
    pallas_call x1, Pallas kernels, per_device(): pl.pallas_call(functools.partial(grads_kernel, heads), grid=(count // hea...  8.69 us
    unnamed x46, local copies, waits for them, and re-layouts  6.81 us
  transfers between devices with their start and end apart: 17, of which 16 were waited for; matrix products, arithmetic and copies ran while one was open for 1% of the time, Pallas kernels for 0%

profile of v1, /device:TPU:0, one launch (start us, length us, event | category | flops | bytes accessed | tf_op | source)
XLA Modules:
  0.0 187.2 jit_solution(191903962080162974)
XLA Ops:
  2.1 2.1 %collective-permute-start = (bf16[3,8,1024]{2,1,0:T(8,128)(2,1)S(1)}, bf16[3,8,1024]{2,1,0:T(8,128)(2,1)S(1)}, u32[]{:S(2)}, u32[]{:S(2)}) collective-permute-start(bf16[3,8,1024]{2,1,0:T(8,128)(2,1)S(1)} %pad_maximum_fusion.2), channel_id=1, source_target_pairs={{0,2},{2,4},{4,6},{6,8},{8,10},{10,12},{12,14},{14,16},{16,18},{18... | collective-permute-start | bytes 147464 | tf_op jit(solution)/shard_map/ppermute | solution.py:340
  11.2 16.4 %block_maps.1 = (f32[8,384,128]{2,1,0:T(8,128)}, f32[128,1024]{1,0:T(8,128)S(1)}, f32[128,1024]{1,0:T(8,128)S(1)}, f32[128,1024]{1,0:T(8,128)S(1)}, f32[128,1024...) custom-call(bf16[128,1024]{1,0:T(8,128)(2,1)S(1)} %copy-done, ...), custom_call_target="tpu_custom_call" | custom-call | tf_op jit(solution)/shard_map/block_maps/pallas_call | solution.py:360
  27.6 48.9 %all_to_all.10.maps_ref = f32[8,384,128]{2,1,0:T(8,128)S(1)} all-to-all(f32[8,384,128]{2,1,0:T(8,128)} %get-tuple-element.28), channel_id=1, replica_groups=mesh['y'=4,'x'=4,'z'=8,'head'=2] {'z'}, dimensions={0} | all-to-all | bytes 3145728 | tf_op jit(solution)/shard_map/all_to_all | solution.py:371
  77.5 2.8 %collective-permute-start.3 = (f32[384,128]{1,0:T(8,128)S(1)}, f32[384,128]{1,0:T(8,128)}, u32[]{:S(2)}, u32[]{:S(2)}) collective-permute-start(f32[384,128]{1,0:T(8,128)S(1)} %line_total.1), channel_id=1, source_target_pairs={{0,48},{16,0},{32,16},{48,32},{1,49},{17,1},{33,17},{49,33},{2,50}... | collective-permute-start | bytes 589832 | tf_op jit(solution)/shard_map/ppermute | solution.py:380
  82.1 3.6 %collective-permute-done.3 = f32[384,128]{1,0:T(8,128)} collective-permute-done((f32[384,128]{1,0:T(8,128)S(1)}, f32[384,128]{1,0:T(8,128)}, u32[]{:S(2)}, u32[]{:S(2)}) %collective-permute-start.3) | collective-permute-done | bytes 196640 | tf_op jit(solution)/shard_map/ppermute | solution.py:380
  85.7 2.1 %collective-permute-done.2 = f32[384,128]{1,0:T(8,128)} collective-permute-done((f32[384,128]{1,0:T(8,128)S(1)}, f32[384,128]{1,0:T(8,128)}, u32[]{:S(2)}, u32[]{:S(2)}) %collective-permute-start.2) | collective-permute-done | bytes 196640 | tf_op jit(solution)/shard_map/ppermute | solution.py:380
  87.7 2.0 %collective-permute-done.1 = f32[384,128]{1,0:T(8,128)} collective-permute-done((f32[384,128]{1,0:T(8,128)S(1)}, f32[384,128]{1,0:T(8,128)}, u32[]{:S(2)}, u32[]{:S(2)}) %collective-permute-start.1) | collective-permute-done | bytes 196640 | tf_op jit(solution)/shard_map/ppermute | solution.py:380
  92.0 3.1 %collective-permute-start.6 = (f32[384,128]{1,0:T(8,128)S(1)}, f32[384,128]{1,0:T(8,128)S(1)}, u32[]{:S(2)}, u32[]{:S(2)}) collective-permute-start(f32[384,128]{1,0:T(8,128)S(1)} %plane_total.1), channel_id=1, source_target_pairs={{0,192},{64,0},{128,64},{192,128},{1,193},{65,1},{129,65},{193,129... | collective-permute-start | bytes 589832 | tf_op jit(solution)/shard_map/ppermute | solution.py:380
  96.6 3.7 %collective-permute-done.6 = f32[384,128]{1,0:T(8,128)S(1)} collective-permute-done((f32[384,128]{1,0:T(8,128)S(1)}, f32[384,128]{1,0:T(8,128)S(1)}, u32[]{:S(2)}, u32[]{:S(2)}) %collective-permute-start.6) | collective-permute-done | bytes 196640 | tf_op jit(solution)/shard_map/ppermute | solution.py:380
  100.4 1.9 %collective-permute-done.5 = f32[384,128]{1,0:T(8,128)S(1)} collective-permute-done((f32[384,128]{1,0:T(8,128)S(1)}, f32[384,128]{1,0:T(8,128)S(1)}, u32[]{:S(2)}, u32[]{:S(2)}) %collective-permute-start.5) | collective-permute-done | bytes 196640 | tf_op jit(solution)/shard_map/ppermute | solution.py:380
  102.3 2.0 %collective-permute-done.4 = f32[384,128]{1,0:T(8,128)S(1)} collective-permute-done((f32[384,128]{1,0:T(8,128)S(1)}, f32[384,128]{1,0:T(8,128)S(1)}, u32[]{:S(2)}, u32[]{:S(2)}) %collective-permute-start.4) | collective-permute-done | bytes 196640 | tf_op jit(solution)/shard_map/ppermute | solution.py:380
  104.4 2.9 %line_states.1 = f32[8,256,128]{2,1,0:T(8,128)S(1)} custom-call(s32[2]{0:T(128)S(1)} %pad_add_fusion.where_ref, f32[8,384,128]{2,1,0:T(8,128)S(1)} %all_to_all.10.maps_ref, f32[4,384,128]{2,1,0:T(8,128)S(1)} %pad_maximum_fusion.lines_ref, f32[4,384,128]{2,1,0:T(8,128)S(1)} %pad_maximum_fusion.1.planes_ref), custom_call_target="tpu_custom_call" | custom-call | tf_op jit(solution)/shard_map/line_states/pallas_call | solution.py:393
  107.4 34.6 %all_to_all.11.states_ref = f32[8,256,128]{2,1,0:T(8,128)} all-to-all(f32[8,256,128]{2,1,0:T(8,128)S(1)} %line_states.1), channel_id=1, replica_groups=mesh['y'=4,'x'=4,'z'=8,'head'=2] {'z'}, dimensions={0} | all-to-all | bytes 2097152 | tf_op jit(solution)/shard_map/all_to_all | solution.py:397
  142.1 8.7 %block_grads.1 = (bf16[128,1024]{1,0:T(8,128)(2,1)}, bf16[128,1024]{1,0:T(8,128)(2,1)}, bf16[128,1024]{1,0:T(8,128)(2,1)}, f32[3,16,1024]{2,1,0:T(8,128)S(1)}, f...) custom-call(bf16[128,1024]{1,0:T(8,128)(2,1)S(1)} %copy-done.1, ...), custom_call_target="tpu_custom_call" | custom-call | tf_op jit(solution)/shard_map/block_grads/pallas_call | solution.py:399
  151.0 2.0 %collective-permute-start.9 = (f32[16,1024]{1,0:T(8,128)S(1)}, f32[16,1024]{1,0:T(8,128)S(1)}, u32[]{:S(2)}, u32[]{:S(2)}) collective-permute-start(f32[16,1024]{1,0:T(8,128)S(1)} %get-tuple-element.48), channel_id=1, source_target_pairs={{0,16},{16,32},{32,48},{48,0},{1,17},{17,33},{33,49},{49,1},{2,18}... | collective-permute-start | bytes 196616 | tf_op jit(solution)/shard_map/ppermute | solution.py:380
  153.2 2.0 %collective-permute-done.10 = f32[16,1024]{1,0:T(8,128)S(1)} collective-permute-done((f32[16,1024]{1,0:T(8,128)S(1)}, f32[16,1024]{1,0:T(8,128)S(1)}, u32[]{:S(2)}, u32[]{:S(2)}) %collective-permute-start.10) | collective-permute-done | bytes 65568 | tf_op jit(solution)/shard_map/ppermute | solution.py:380
  155.2 1.5 collective-permute-done.9
  156.8 2.0 %collective-permute-done.8 = f32[16,1024]{1,0:T(8,128)S(1)} collective-permute-done((f32[16,1024]{1,0:T(8,128)S(1)}, f32[16,1024]{1,0:T(8,128)S(1)}, u32[]{:S(2)}, u32[]{:S(2)}) %collective-permute-start.8) | collective-permute-done | bytes 65568 | tf_op jit(solution)/shard_map/ppermute | solution.py:380
  158.9 2.0 %collective-permute-start.12 = (f32[16,1024]{1,0:T(8,128)S(1)}, f32[16,1024]{1,0:T(8,128)S(1)}, u32[]{:S(2)}, u32[]{:S(2)}) collective-permute-start(f32[16,1024]{1,0:T(8,128)S(1)} %add_add_fusion.1), channel_id=1, source_target_pairs={{0,64},{64,128},{128,192},{192,0},{1,65},{65,129},{129,193},{193,1... | collective-permute-start | bytes 196616 | tf_op jit(solution)/shard_map/ppermute | solution.py:380
  164.4 2.2 %collective-permute-done.11 = f32[16,1024]{1,0:T(8,128)S(1)} collective-permute-done((f32[16,1024]{1,0:T(8,128)S(1)}, f32[16,1024]{1,0:T(8,128)S(1)}, u32[]{:S(2)}, u32[]{:S(2)}) %collective-permute-start.11) | collective-permute-done | bytes 65568 | tf_op jit(solution)/shard_map/ppermute | solution.py:380
  168.0 3.0 %collective-permute-done.14 = f32[16,1024]{1,0:T(8,128)S(1)} collective-permute-done((f32[16,1024]{1,0:T(8,128)S(1)}, f32[16,1024]{1,0:T(8,128)S(1)}, u32[]{:S(2)}, u32[]{:S(2)}) %collective-permute-start.14) | collective-permute-done | bytes 65568 | tf_op jit(solution)/shard_map/ppermute | solution.py:426
  171.2 6.5 %collective-permute-done.15 = f32[16,1024]{1,0:T(8,128)S(1)} collective-permute-done((f32[16,1024]{1,0:T(8,128)S(1)}, f32[16,1024]{1,0:T(8,128)S(1)}, u32[]{:S(2)}, u32[]{:S(2)}) %collective-permute-start.15) | collective-permute-done | bytes 65568 | tf_op jit(solution)/shard_map/ppermute | solution.py:426
  177.7 1.7 collective-permute-start.16
  180.1 5.9 %collective-permute-done.16 = f32[16,1024]{1,0:T(8,128)S(1)} collective-permute-done((f32[16,1024]{1,0:T(8,128)S(1)}, f32[16,1024]{1,0:T(8,128)S(1)}, u32[]{:S(2)}, u32[]{:S(2)}) %collective-permute-start.16) | collective-permute-done | bytes 65568 | tf_op jit(solution)/shard_map/ppermute | solution.py:426
  (78 shorter events, 22.5 us)
Async XLA Ops:
  2.1 3.8 %collective-permute-start = (bf16[3,8,1024]{2,1,0:T(8,128)(2,1)S(1)}, bf16[3,8,1024]{2,1,0:T(8,128)(2,1)S(1)}, u32[]{:S(2)}, u32[]{:S(2)}) collective-permute-start(bf16[3,8,1024]{2,1,0:T(8,128)(2,1)S(1)} %pad_maximum_fusion.2), channel_id=1, source_target_pairs={{0,2},{2,4},{4,6},{6,8},{8,10},{10,12},{12,14},{14,16},{16,18},{18... | collective-permute-start | bytes 147464 | tf_op jit(solution)/shard_map/ppermute | solution.py:340
  27.6 49.0 %copy-start.8 = (f32[128,1024]{1,0:T(8,128)}, f32[128,1024]{1,0:T(8,128)S(1)}, u32[]{:S(2)}) copy-start(f32[128,1024]{1,0:T(8,128)S(1)} %get-tuple-element.32.fk_in) | copy-start | bytes 1572868
  27.6 49.0 %copy-start.10 = (f32[128,1024]{1,0:T(8,128)}, f32[128,1024]{1,0:T(8,128)S(1)}, u32[]{:S(2)}) copy-start(f32[128,1024]{1,0:T(8,128)S(1)} %get-tuple-element.33.fv_in) | copy-start | bytes 1572868
  27.6 49.0 %copy-start.12 = (f32[128,1024]{1,0:T(8,128)}, f32[128,1024]{1,0:T(8,128)S(1)}, u32[]{:S(2)}) copy-start(f32[128,1024]{1,0:T(8,128)S(1)} %get-tuple-element.34.cum_in) | copy-start | bytes 1572868
  27.6 49.0 %copy-start.14 = (f32[128,1024]{1,0:T(8,128)}, f32[128,1024]{1,0:T(8,128)S(1)}, u32[]{:S(2)}) copy-start(f32[128,1024]{1,0:T(8,128)S(1)} %get-tuple-element.35.gf_in) | copy-start | bytes 1572868
  27.6 49.0 %copy-start.16 = (f32[128,1024]{1,0:T(8,128)}, f32[128,1024]{1,0:T(8,128)S(1)}, u32[]{:S(2)}) copy-start(f32[128,1024]{1,0:T(8,128)S(1)} %get-tuple-element.36.ld_in) | copy-start | bytes 1572868
  27.6 49.0 %copy-start.18 = (f32[8,128,128]{2,1,0:T(8,128)}, f32[8,128,128]{2,1,0:T(8,128)S(1)}, u32[]{:S(2)}) copy-start(f32[8,128,128]{2,1,0:T(8,128)S(1)} %get-tuple-element.37.w_in) | copy-start | bytes 1572868
  77.5 8.2 %collective-permute-start.3 = (f32[384,128]{1,0:T(8,128)S(1)}, f32[384,128]{1,0:T(8,128)}, u32[]{:S(2)}, u32[]{:S(2)}) collective-permute-start(f32[384,128]{1,0:T(8,128)S(1)} %line_total.1), channel_id=1, source_target_pairs={{0,48},{16,0},{32,16},{48,32},{1,49},{17,1},{33,17},{49,33},{2,50}... | collective-permute-start | bytes 589832 | tf_op jit(solution)/shard_map/ppermute | solution.py:380
  80.3 7.4 %collective-permute-start.2 = (f32[384,128]{1,0:T(8,128)S(1)}, f32[384,128]{1,0:T(8,128)}, u32[]{:S(2)}, u32[]{:S(2)}) collective-permute-start(f32[384,128]{1,0:T(8,128)S(1)} %line_total.1), channel_id=1, source_target_pairs={{0,32},{16,48},{32,0},{48,16},{1,33},{17,49},{33,1},{49,17},{2,34}... | collective-permute-start | bytes 589832 | tf_op jit(solution)/shard_map/ppermute | solution.py:380
  81.1 8.6 %collective-permute-start.1 = (f32[384,128]{1,0:T(8,128)S(1)}, f32[384,128]{1,0:T(8,128)}, u32[]{:S(2)}, u32[]{:S(2)}) collective-permute-start(f32[384,128]{1,0:T(8,128)S(1)} %line_total.1), channel_id=1, source_target_pairs={{0,16},{16,32},{32,48},{48,0},{1,17},{17,33},{33,49},{49,1},{2,18}... | collective-permute-start | bytes 589832 | tf_op jit(solution)/shard_map/ppermute | solution.py:380
  92.0 8.4 %collective-permute-start.6 = (f32[384,128]{1,0:T(8,128)S(1)}, f32[384,128]{1,0:T(8,128)S(1)}, u32[]{:S(2)}, u32[]{:S(2)}) collective-permute-start(f32[384,128]{1,0:T(8,128)S(1)} %plane_total.1), channel_id=1, source_target_pairs={{0,192},{64,0},{128,64},{192,128},{1,193},{65,1},{129,65},{193,129... | collective-permute-start | bytes 589832 | tf_op jit(solution)/shard_map/ppermute | solution.py:380
  95.0 7.3 %collective-permute-start.5 = (f32[384,128]{1,0:T(8,128)S(1)}, f32[384,128]{1,0:T(8,128)S(1)}, u32[]{:S(2)}, u32[]{:S(2)}) collective-permute-start(f32[384,128]{1,0:T(8,128)S(1)} %plane_total.1), channel_id=1, source_target_pairs={{0,128},{64,192},{128,0},{192,64},{1,129},{65,193},{129,1},{193,65... | collective-permute-start | bytes 589832 | tf_op jit(solution)/shard_map/ppermute | solution.py:380
  95.7 8.6 %collective-permute-start.4 = (f32[384,128]{1,0:T(8,128)S(1)}, f32[384,128]{1,0:T(8,128)S(1)}, u32[]{:S(2)}, u32[]{:S(2)}) collective-permute-start(f32[384,128]{1,0:T(8,128)S(1)} %plane_total.1), channel_id=1, source_target_pairs={{0,64},{64,128},{128,192},{192,0},{1,65},{65,129},{129,193},{193,1... | collective-permute-start | bytes 589832 | tf_op jit(solution)/shard_map/ppermute | solution.py:380
  104.4 37.6 %copy-start.13 = (f32[128,1024]{1,0:T(8,128)S(1)}, f32[128,1024]{1,0:T(8,128)}, u32[]{:S(2)}) copy-start(f32[128,1024]{1,0:T(8,128)} %copy-done.12) | copy-start | bytes 1572868
  150.8 4.5 %collective-permute-start.10 = (f32[16,1024]{1,0:T(8,128)S(1)}, f32[16,1024]{1,0:T(8,128)S(1)}, u32[]{:S(2)}, u32[]{:S(2)}) collective-permute-start(f32[16,1024]{1,0:T(8,128)S(1)} %get-tuple-element.48), channel_id=1, source_target_pairs={{0,48},{16,0},{32,16},{48,32},{1,49},{17,1},{33,17},{49,33},{2,50}... | collective-permute-start | bytes 196616 | tf_op jit(solution)/shard_map/ppermute | solution.py:380
  151.0 5.8 %collective-permute-start.9 = (f32[16,1024]{1,0:T(8,128)S(1)}, f32[16,1024]{1,0:T(8,128)S(1)}, u32[]{:S(2)}, u32[]{:S(2)}) collective-permute-start(f32[16,1024]{1,0:T(8,128)S(1)} %get-tuple-element.48), channel_id=1, source_target_pairs={{0,16},{16,32},{32,48},{48,0},{1,17},{17,33},{33,49},{49,1},{2,18}... | collective-permute-start | bytes 196616 | tf_op jit(solution)/shard_map/ppermute | solution.py:380
  153.0 5.8 %collective-permute-start.8 = (f32[16,1024]{1,0:T(8,128)S(1)}, f32[16,1024]{1,0:T(8,128)S(1)}, u32[]{:S(2)}, u32[]{:S(2)}) collective-permute-start(f32[16,1024]{1,0:T(8,128)S(1)} %get-tuple-element.48), channel_id=1, source_target_pairs={{0,32},{16,48},{32,0},{48,16},{1,33},{17,49},{33,1},{49,17},{2,34}... | collective-permute-start | bytes 196616 | tf_op jit(solution)/shard_map/ppermute | solution.py:380
  158.8 4.3 %collective-permute-start.13 = (f32[16,1024]{1,0:T(8,128)S(1)}, f32[16,1024]{1,0:T(8,128)S(1)}, u32[]{:S(2)}, u32[]{:S(2)}) collective-permute-start(f32[16,1024]{1,0:T(8,128)S(1)} %add_add_fusion.1), channel_id=1, source_target_pairs={{0,192},{64,0},{128,64},{192,128},{1,193},{65,1},{129,65},{193,129... | collective-permute-start | bytes 196616 | tf_op jit(solution)/shard_map/ppermute | solution.py:380
  158.9 5.6 %collective-permute-start.12 = (f32[16,1024]{1,0:T(8,128)S(1)}, f32[16,1024]{1,0:T(8,128)S(1)}, u32[]{:S(2)}, u32[]{:S(2)}) collective-permute-start(f32[16,1024]{1,0:T(8,128)S(1)} %add_add_fusion.1), channel_id=1, source_target_pairs={{0,64},{64,128},{128,192},{192,0},{1,65},{65,129},{129,193},{193,1... | collective-permute-start | bytes 196616 | tf_op jit(solution)/shard_map/ppermute | solution.py:380
  160.9 5.8 %collective-permute-start.11 = (f32[16,1024]{1,0:T(8,128)S(1)}, f32[16,1024]{1,0:T(8,128)S(1)}, u32[]{:S(2)}, u32[]{:S(2)}) collective-permute-start(f32[16,1024]{1,0:T(8,128)S(1)} %add_add_fusion.1), channel_id=1, source_target_pairs={{0,128},{64,192},{128,0},{192,64},{1,129},{65,193},{129,1},{193,65... | collective-permute-start | bytes 196616 | tf_op jit(solution)/shard_map/ppermute | solution.py:380
  161.1 10.0 %collective-permute-start.7 = (f32[3,8,1024]{2,1,0:T(8,128)S(1)}, f32[3,8,1024]{2,1,0:T(8,128)S(1)}, u32[]{:S(2)}, u32[]{:S(2)}) collective-permute-start(f32[3,8,1024]{2,1,0:T(8,128)S(1)} %get-tuple-element.43), channel_id=1, source_target_pairs={{2,0},{4,2},{6,4},{8,6},{10,8},{12,10},{14,12},{16,14},{18,16},{20... | collective-permute-start | bytes 294920 | tf_op jit(solution)/shard_map/ppermute | solution.py:415
  166.7 4.4 %collective-permute-start.14 = (f32[16,1024]{1,0:T(8,128)S(1)}, f32[16,1024]{1,0:T(8,128)S(1)}, u32[]{:S(2)}, u32[]{:S(2)}) collective-permute-start(f32[16,1024]{1,0:T(8,128)S(1)} %add_add_fusion), channel_id=1, source_target_pairs={{0,2},{2,0},{4,6},{6,4},{8,10},{10,8},{12,14},{14,12},{1,3},{3,1},... | collective-permute-start | bytes 196616 | tf_op jit(solution)/shard_map/ppermute | solution.py:426
  171.0 6.7 %collective-permute-start.15 = (f32[16,1024]{1,0:T(8,128)S(1)}, f32[16,1024]{1,0:T(8,128)S(1)}, u32[]{:S(2)}, u32[]{:S(2)}) collective-permute-start(f32[16,1024]{1,0:T(8,128)S(1)} %add.39), channel_id=1, source_target_pairs={{0,4},{2,6},{4,0},{6,2},{8,12},{10,14},{12,8},{14,10},{1,5},{3,7},... | collective-permute-start | bytes 196616 | tf_op jit(solution)/shard_map/ppermute | solution.py:426
  177.7 8.3 %collective-permute-start.16 = (f32[16,1024]{1,0:T(8,128)S(1)}, f32[16,1024]{1,0:T(8,128)S(1)}, u32[]{:S(2)}, u32[]{:S(2)}) collective-permute-start(f32[16,1024]{1,0:T(8,128)S(1)} %add.40), channel_id=1, source_target_pairs={{0,8},{2,10},{4,12},{6,14},{8,0},{10,2},{12,4},{14,6},{1,9},{3,11}... | collective-permute-start | bytes 196616 | tf_op jit(solution)/shard_map/ppermute | solution.py:426
  (15 other events, 326.3 us)

commit v2 on v1

--- a/solution.py
+++ b/solution.py
@@ -17,6 +17,10 @@
 NT = (((1,), (1,)), ((), ()))
 TN = (((0,), (0,)), ((), ()))
 MIB = 1024 * 1024
+AUX = 16
+LINK = jnp.float16
+TOP = 13.0
+FLOOR = -200.0
 
 
 def split(x):
@@ -167,20 +171,50 @@
         w_out[h] = w
         u_out[h] = u
         both = dot(split(ks[h] * end), split(both), TN)
-        maps_ref[h, 0:T] = ident * last - both[:, :T]
-        maps_ref[h, T : 2 * T] = both[:, T:]
         grad = (grad_ref[:, at[h]],)
         pg = dot(split(attend[h]), grad, TN)
         pg_out[h] = pg
-        maps_ref[h, 2 * T : 3 * T] = dot(split(qs[h] * full), grad, TN) - dot(split(w), split(pg), TN)
+        adjoint = dot(split(qs[h] * full), grad, TN) - dot(split(w), split(pg), TN)
+        put(maps_ref.at[h], (-both[:, :T], both[:, T:], adjoint), cumul[h][T - 1 : T])
+
+
+def put(ref, parts, log_decay):
+    row = iota((AUX, T), 0)
+    packed = jnp.zeros((AUX, T), F32)
+    place = 0
+    for i, square in enumerate(parts):
+        largest = jnp.max(jnp.max(jnp.abs(square), axis=0, keepdims=True), axis=1, keepdims=True)
+        power = jnp.floor(jnp.log2(jnp.maximum(largest, 1e-30)))
+        ref[place : place + T] = square * jnp.exp2(TOP - power)
+        packed = jnp.where(row == 3 + i, power, packed)
+        place += T
+    if log_decay is not None:
+        rest = jnp.maximum(log_decay, FLOOR)
+        for i in range(3):
+            term = rest.astype(BF16).astype(F32)
+            rest = rest - term
+            packed = jnp.where(row == i, term, packed)
+    ref[place : place + AUX] = packed
+
+
+def get(ref):
+    count = (ref.shape[0] - AUX) // T
+    aux = ref[count * T : count * T + AUX]
+    squares = [ref[m * T : (m + 1) * T] * jnp.exp2(aux[3 + m : 4 + m] - TOP) for m in range(count)]
+    return (*squares, (aux[0:1] + aux[1:2]) + aux[2:3])
+
+
+def whole_map(move, log_decay):
+    row, col = iota((T, T), 0), iota((T, T), 1)
+    return move + jnp.where(row == col, jnp.exp(log_decay), 0.0)
 
 
 def join(early, late):
-    ea, eb, ed = early
-    la, lb, ld = late
-    sa = split(ea)
-    both = dot(split(la), lanes(sa, split(eb)), NN)
-    return (both[:, :T], both[:, T:] + lb, ed + dot(sa, split(ld), TN))
+    ee, eb, ed, eg = early
+    le, lb, ld, lg = late
+    both = dot(split(whole_map(le, lg)), lanes(split(ee), split(eb)), NN)
+    adjoint = ed + dot(split(whole_map(ee, eg)), split(ld), TN)
+    return (both[:, :T] + le * jnp.exp(eg), both[:, T:] + lb, adjoint, eg + lg)
 
 
 def tree(items):
@@ -189,55 +223,63 @@
     return items[0]
 
 
-def triple(ref, i):
-    return tuple(ref[i, m * T : (m + 1) * T] for m in range(3))
-
-
 def line_kernel(maps_ref, out_ref):
-    total = tree([triple(maps_ref, i) for i in range(maps_ref.shape[0])])
-    for m in range(3):
-        out_ref[m * T : (m + 1) * T] = total[m]
-
-
-def plane_kernel(where_ref, lines_ref, out_ref):
-    count = lines_ref.shape[0]
-    mine = where_ref[1]
-    total = tree([triple(lines_ref, lax.rem(mine - i + count, count)) for i in range(count)])
-    for m in range(3):
-        out_ref[m * T : (m + 1) * T] = total[m]
-
-
-def states_kernel(where_ref, maps_ref, lines_ref, planes_ref, out_ref):
+    *squares, log_decay = tree([get(maps_ref.at[i]) for i in range(maps_ref.shape[0])])
+    put(out_ref, squares, log_decay)
+
+
+def plane_kernel(where_ref, *refs):
+    *lines, one, two, three, held = refs
+    count = len(lines)
+    mine, plane = where_ref[1], where_ref[0]
+    for d, line in enumerate(lines):
+        held[lax.rem(mine - d + count, count)] = line[...]
+    move, offset, adjoint, log_decay = tree([get(held.at[i]) for i in range(count)])
+    for d, out in enumerate((one, two, three)):
+        put(out, (move, jnp.where(plane + d + 1 < count, offset, adjoint)), log_decay)
+
+
+def advance(part, state, active):
+    move, offset, log_decay = part
+    new = dot(split(whole_map(move, log_decay)), split(state), NN) + offset
+    return new if active is None else jnp.where(active, new, state)
+
+
+def retreat(part, grad, active):
+    move, adjoint, log_decay = part
+    new = dot(split(whole_map(move, log_decay)), split(grad), TN) + adjoint
+    return new if active is None else jnp.where(active, new, grad)
+
+
+def states_kernel(where_ref, maps_ref, *refs):
+    *moved, out_ref = refs
+    lines, planes = moved[:3], moved[3:]
     state = jnp.zeros((T, T), F32)
     grad = jnp.zeros((T, T), F32)
-    for ref, mine in ((planes_ref, where_ref[0]), (lines_ref, where_ref[1])):
-        count = ref.shape[0]
-        for i in range(count - 1):
-            slot = lax.rem(mine - i + count, count)
-            a, b, d = triple(ref, slot)
-            state = jnp.where(i < mine, dot(split(a), split(state), NN) + b, state)
-            j = count - 1 - i
-            slot = lax.rem(mine - j + count, count)
-            a, b, d = triple(ref, slot)
-            grad = jnp.where(j > mine, dot(split(a), split(grad), TN) + d, grad)
+    for refs, mine in ((planes, where_ref[0]), (lines, where_ref[1])):
+        parts = [get(ref) for ref in refs]
+        for i in range(3):
+            part = parts[2 - i]
+            state = advance((part[0], part[1], part[-1]), state, mine >= 3 - i)
+            part = parts[i]
+            grad = retreat((part[0], part[-2], part[-1]), grad, mine < i + 1)
     count = maps_ref.shape[0]
+    states, grads = [state], [grad]
+    for i in range(count - 1):
+        move, offset, adjoint, log_decay = get(maps_ref.at[i])
+        states.append(advance((move, offset, log_decay), states[-1], None))
+        move, offset, adjoint, log_decay = get(maps_ref.at[count - 1 - i])
+        grads.append(retreat((move, adjoint, log_decay), grads[-1], None))
     for i in range(count):
-        j = count - 1 - i
-        out_ref[i, 0:T] = state
-        out_ref[j, T : 2 * T] = grad
-        if i < count - 1:
-            a, b, d = triple(maps_ref, i)
-            state = dot(split(a), split(state), NN) + b
-            a, b, d = triple(maps_ref, j)
-            grad = dot(split(a), split(grad), TN) + d
+        put(out_ref.at[i], (states[i], grads[count - 1 - i]), None)
 
 
 def grads_kernel(
     heads,
-    q_ref, k_ref, v_ref, halo_ref, beta_ref, conv_ref, grad_ref, states_ref,
+    q_ref, k_ref, v_ref, halo_ref, beta_ref, conv_ref, grad_ref, states_ref, where_ref,
     q_in, k_in, fq_in, fk_in, fv_in, cum_in, gf_in, ld_in, w_in, u_in, pg_in, inv_in,
-    dq_out, dk_out, dv_out, edge_out, tail_out, dgate_out, dbeta_out, param_out,
-    ext, back,
+    dq_out, dk_out, dv_out, edge_out, tail_out, dgate_out, dbeta_out, sum0_out, sum1_out, sum2_out, sum3_out,
+    ext, back, params,
 ):
     row, col = iota((T, T), 0), iota((T, T), 1)
     strict = row > col
@@ -251,8 +293,9 @@
     deltas, dds, grads = [], [], []
     betas = [column(beta_all, base + h) for h in each]
     factors = [gate_factors(cum_in[:, at[h]]) for h in each]
-    ms = [split(states_ref[h, 0:T]) for h in each]
-    gs = [split(states_ref[h, T : 2 * T]) for h in each]
+    states = [get(states_ref.at[h]) for h in each]
+    ms = [split(states[h][0]) for h in each]
+    gs = [split(states[h][1]) for h in each]
     qs = [q_in[:, at[h]] for h in each]
     ks = [k_in[:, at[h]] for h in each]
     dbeta = jnp.zeros(dbeta_out.shape, F32)
@@ -266,7 +309,8 @@
     for h in each:
         grad = grad_ref[:, at[h]]
         left = rows((grad, jnp.zeros_like(grad)), split(-dvs[h]))
-        firsts.append(dot(left, rows(dsp[h], ms[h]), NT))
+        both = [dot(left, dsp[h], NT), dot(left, ms[h], NT)]
+        firsts.append(jnp.concatenate(both, axis=1))
     ends = [dot(dsp[h], gs[h], NT) for h in each]
     for h in each:
         up0, up1, down, full, end, last, late = factors[h]
@@ -285,14 +329,14 @@
         dk_col = down * jnp.where(late, by_col[:, T:], by_col[:, :T]) + dk_end
         dk = dk_row + dk_col
         dcum = q * dq + k * (dk_row - dk_col)
-        held = states_ref[h, 0:T] * states_ref[h, T : 2 * T]
+        held = states[h][0] * states[h][1]
         dlast = jnp.sum(k * dk_end, axis=0, keepdims=True) + last * dot((ones,), split(held), NT)[0:1]
         both = lax.dot_general(
             upper, jnp.concatenate(split(dcum), axis=1), NN, preferred_element_type=F32
         )
         dlog = both[:, :T] + both[:, T:] + dlast
         dgate_out[:, at[h]] = dlog * gf_in[:, at[h]]
-        param_out[12:13, at[h]] = jnp.sum(dlog * ld_in[:, at[h]], axis=0, keepdims=True)
+        params[base + h, 12:13] = jnp.sum(dlog * ld_in[:, at[h]], axis=0, keepdims=True)
         write = jnp.sum(des[h] * deltas[h], axis=1, keepdims=True) * (1.0 - betas[h])
         dbeta = jnp.where(iota(dbeta.shape, 1) == base + h, write, dbeta)
         pres = (
@@ -310,13 +354,12 @@
             for i in range(4):
                 part = conv_ref[j, i : i + 1, at[h]] * back[j, h, 3 - i : 3 - i + 136]
                 whole = part if whole is None else whole + part
-                param_out[4 * j + i : 4 * j + i + 1, at[h]] = jnp.sum(
+                params[base + h, 4 * j + i : 4 * j + i + 1] = jnp.sum(
                     pres[j] * ext[j, h, 5 + i : 5 + i + T], axis=0, keepdims=True
                 )
             out[:, at[h]] = whole[8:136].astype(BF16)
             tail_out[j, :, at[h]] = whole[0:8]
             edge_out[j, :, at[h]] = whole[120:136]
-    param_out[13:16] = jnp.zeros((3, heads * T), F32)
 
     @pl.when(pl.program_id(0) == 0)
     def _():
@@ -325,6 +368,30 @@
     @pl.when(pl.program_id(0) > 0)
     def _():
         dbeta_out[...] = dbeta_out[...] + dbeta
+
+    @pl.when(pl.program_id(0) == pl.num_programs(0) - 1)
+    def _():
+        for d, out in enumerate((sum0_out, sum1_out, sum2_out, sum3_out)):
+            share = out.shape[0]
+            out[:, 13:16] = jnp.zeros((share, 3, T), F32)
+            for r in range(share):
+                out[r, 0:13] = params[lax.rem(where_ref[1] + d, 4) * share + r, 0:13]
+
+
+def gather_kernel(where_ref, *refs):
+    *pieces, conv_out, decay_out, held = refs
+    for d, piece in enumerate(pieces):
+        held[lax.rem(where_ref[1] - d + 4, 4)] = piece[...]
+    for p in range(4):
+        for r in range(held.shape[1]):
+            lane = (p * held.shape[1] + r) * T
+            for j in range(3):
+                conv_out[j, :, lane : lane + T] = held[p, r, 4 * j : 4 * j + 4]
+            decay_out[:, lane : lane + T] = held[p, r, 12:13]
+
+
+def widen(x):
+    return x.astype(F32)
 
 
 def per_device(query_raw, key_raw, value_raw, gate_raw, beta_raw, conv_weight, decay_log, grad_out):
@@ -353,7 +420,7 @@
         return jax.ShapeDtypeStruct(shape, dtype)
 
     params = pltpu.CompilerParams(
-        dimension_semantics=("arbitrary",), vmem_limit_bytes=48 * MIB
+        dimension_semantics=("arbitrary",), vmem_limit_bytes=60 * MIB
     )
     saved_shapes = [like(length, channels)] * 8 + [like(count, T, T)] * 4
     saved_specs = [tall] * 8 + [square] * 4
@@ -361,81 +428,89 @@
         functools.partial(maps_kernel, heads),
         grid=(count // heads,),
         in_specs=[tall, tall, tall, edge, tall, beta_spec, taps, pl.BlockSpec((1, wide), lambda h: (0, h)), tall],
-        out_specs=[stack_spec(3)] + saved_specs,
-        out_shape=[like(count, 3 * T, T)] + saved_shapes,
+        out_specs=[pl.BlockSpec((heads, 3 * T + AUX, T), lambda h: (h, 0, 0))] + saved_specs,
+        out_shape=[like(count, 3 * T + AUX, T)] + saved_shapes,
         scratch_shapes=[pltpu.VMEM((3, heads, 136, T), F32)],
         compiler_params=params,
         name="block_maps",
     )(query_raw, key_raw, value_raw, halo, gate_raw, beta_raw, conv_weight, decay_row, grad_out)
 
-    line_maps = lax.all_to_all(maps, "z", 0, 0, tiled=True)
+    line_maps = widen(lax.all_to_all(maps.astype(LINK), "z", 0, 0, tiled=True))
+    small = pltpu.CompilerParams(vmem_limit_bytes=32 * MIB)
     line_total = pl.pallas_call(
-        line_kernel, out_shape=like(3 * T, T), name="line_total",
-        compiler_params=pltpu.CompilerParams(vmem_limit_bytes=32 * MIB),
+        line_kernel, out_shape=like(3 * T + AUX, T), name="line_total", compiler_params=small
     )(line_maps)
 
-    def around(block, axis):
+    def around(blocks, axis):
         size = lax.axis_size(axis)
-        moved = [
-            lax.ppermute(block, axis, [(i, (i + d) % size) for i in range(size)])
-            for d in range(1, size)
+        return [
+            lax.ppermute(block, axis, [(i, (i + d + 1) % size) for i in range(size)])
+            for d, block in enumerate(blocks)
         ]
-        return [block] + moved
 
     smem = pl.BlockSpec(memory_space=pltpu.SMEM)
     vmem = pl.BlockSpec(memory_space=pltpu.VMEM)
-    line_totals = jnp.stack(around(line_total, "x"))
-    plane_total = pl.pallas_call(
-        plane_kernel, out_shape=like(3 * T, T), in_specs=[smem, vmem], name="plane_total",
-        compiler_params=pltpu.CompilerParams(vmem_limit_bytes=32 * MIB),
-    )(wheres, line_totals)
-    plane_totals = jnp.stack(around(plane_total, "y"))
+    from_lines = [widen(x) for x in around([line_total.astype(LINK)] * 3, "x")]
+    plane_totals = pl.pallas_call(
+        plane_kernel, out_shape=[like(2 * T + AUX, T)] * 3, in_specs=[smem] + [vmem] * 4,
+        scratch_shapes=[pltpu.VMEM((4, 3 * T + AUX, T), F32)], name="plane_total", compiler_params=small,
+    )(wheres, line_total, *from_lines)
+    from_planes = [widen(x) for x in around([x.astype(LINK) for x in plane_totals], "y")]
     line_states = pl.pallas_call(
-        states_kernel, out_shape=like(depth, 2 * T, T), in_specs=[smem, vmem, vmem, vmem], name="line_states",
-        compiler_params=pltpu.CompilerParams(vmem_limit_bytes=32 * MIB),
-    )(wheres, line_maps, line_totals, plane_totals)
-    states = lax.all_to_all(line_states, "z", 0, 0, tiled=True)
-
-    dq, dk, dv, edges, tails, dgate, dbeta, partial = pl.pallas_call(
+        states_kernel, out_shape=like(depth, 2 * T + AUX, T), in_specs=[smem] + [vmem] * 7,
+        name="line_states", compiler_params=small,
+    )(wheres, line_maps, *from_lines, *from_planes)
+    states = widen(lax.all_to_all(line_states.astype(LINK), "z", 0, 0, tiled=True))
+
+    dq, dk, dv, edges, tails, dgate, dbeta, *sums = pl.pallas_call(
         functools.partial(grads_kernel, heads),
         grid=(count // heads,),
-        in_specs=[tall, tall, tall, edge, beta_spec, taps, tall, stack_spec(2)] + saved_specs,
+        in_specs=[
+            tall, tall, tall, edge, beta_spec, taps, tall,
+            pl.BlockSpec((heads, 2 * T + AUX, T), lambda h: (h, 0, 0)), smem,
+        ] + saved_specs,
         out_specs=[
             tall, tall, tall,
             pl.BlockSpec((3, 16, wide), lambda h: (0, 0, h)), edge, tall, beta_spec,
-            pl.BlockSpec((16, wide), lambda h: (0, h)),
-        ],
+        ] + [pl.BlockSpec((count // lines, 16, T), lambda h: (0, 0, 0))] * lines,
         out_shape=[like(length, channels, dtype=BF16)] * 3
-        + [like(3, 16, channels), like(3, 8, channels), like(length, channels), like(length, count), like(16, channels)],
-        scratch_shapes=[pltpu.VMEM((3, heads, 136, T), F32), pltpu.VMEM((3, heads, 144, T), F32)],
+        + [like(3, 16, channels), like(3, 8, channels), like(length, channels), like(length, count)] + [like(count // lines, 16, T)] * lines,
+        scratch_shapes=[pltpu.VMEM((3, heads, 136, T), F32), pltpu.VMEM((3, heads, 144, T), F32), pltpu.VMEM((count, 16, T), F32)],
         compiler_params=params,
         name="block_grads",
-    )(query_raw, key_raw, value_raw, halo, beta_raw, conv_weight, grad_out, states, *saved)
-
-    after = lax.ppermute(tails, SEQ, [(i + 1, i) for i in range(devices - 1)])
-    fixed = edges + jnp.pad(after, ((0, 0), (8, 0), (0, 0)))
+    )(query_raw, key_raw, value_raw, halo, beta_raw, conv_weight, grad_out, states, wheres, *saved)
+
+    after = lax.ppermute(tails.astype(BF16), SEQ, [(i + 1, i) for i in range(devices - 1)])
+    fixed = edges + jnp.pad(after.astype(F32), ((0, 0), (8, 0), (0, 0)))
 
     def finish(full, extra):
         return lax.dynamic_update_slice(full, extra.astype(BF16), (length - 16, 0))
 
-    total = partial
-    for axis in ("x", "y"):
-        own, one, two, three = around(total, axis)
-        total = (own + two) + (one + three)
-    for stride in (1, 2, 4):
-        total = total + lax.ppermute(total, "z", [(i, i ^ stride) for i in range(depth)])
+    one, two, three = around(sums[1:], "x")
+    total = (sums[0] + one) + (two + three)
+    one, two, three = around([total] * 3, "y")
+    total = (total + two) + (one + three)
+    two, four, six = [
+        lax.ppermute(total, "z", [(i, (i + d) % depth) for i in range(depth)]) for d in (2, 4, 6)
+    ]
+    total = (total + four) + (two + six)
+    total = total + lax.ppermute(total, "z", [(i, i ^ 1) for i in range(depth)])
+    conv_sum, decay_sum = pl.pallas_call(
+        gather_kernel, out_shape=[like(3, 4, channels), like(1, channels)], in_specs=[smem] + [vmem] * 4,
+        scratch_shapes=[pltpu.VMEM((4, count // lines, 16, T), F32)], name="gather_sums", compiler_params=small,
+    )(wheres, total, *around([total] * 3, "x"))
     return (
         finish(dq, fixed[0]),
         finish(dk, fixed[1]),
         finish(dv, fixed[2]),
         dgate,
         dbeta,
-        total[:12].reshape(3, 4, channels),
-        total[12],
+        conv_sum,
+        decay_sum.reshape(channels),
     )
 
 
-GROUP = 2
+GROUP = 4
 
 
 def solution(mesh):

time: 188 us -> 149 us (0.79)
  blocking collectives: 83.6 us -> 16.5 us
  starting transfers between devices: 19.8 us -> 40.3 us
  waiting for transfers between devices: 41.5 us -> 49.7 us
  other arithmetic: 1.38 us -> 6.51 us
  local copies, waits for them, and re-layouts: 10.1 us -> 5.64 us
    all_to_all x2 -> x1, blocking collectives: 83.6 us -> 16.5 us  [per_device(): lax.all_to_all(line_states.astype(LINK), 'z', 0, 0, tiled=True)]
    all_to_all x0 -> x1, waiting for transfers between devices: none -> 22.7 us  [per_device(): line_maps = widen(lax.all_to_all(maps.astype(LINK), 'z', 0, 0, tiled=True))]
    ppermute x16 -> x20, waiting for transfers between devices: 40.5 us -> 26.7 us  [the longest x15 21.7 us: around(): lax.ppermute(block, axis, [(i, (i + d + 1) % size) for i in range(size)])]
    ppermute x16 -> x20, starting transfers between devices: 17.8 us -> 28.1 us  [the longest x15 22 us: around(): lax.ppermute(block, axis, [(i, (i + d + 1) % size) for i in range(size)])]
    all_to_all x0 -> x1, starting transfers between devices: none -> 10.1 us  [per_device(): line_maps = widen(lax.all_to_all(maps.astype(LINK), 'z', 0, 0, tiled=True))]
    convert_element_type x0 -> x15, other arithmetic: none -> 4.74 us  [the longest x1 2.44 us: per_device(): line_maps = widen(lax.all_to_all(maps.astype(LINK), 'z', 0, 0, tiled=True))]
    pallas_call x1, Pallas kernels: 16.4 us -> 12.7 us  [per_device(): pl.pallas_call(functools.partial(maps_kernel, heads), grid=(count // head...]
    unnamed x46 -> x8, local copies, waits for them, and re-layouts: 6.81 us -> 3.54 us
  transfers between devices with their start and end apart: 17 -> 22, of which waited for: 16 -> 19; matrix products, arithmetic and copies ran while one was open for 1% -> 4% of each run, Pallas kernels for 0% -> 0%
where the time goes in v2:
time: 149 us; the launch traced here: 148 us
  waiting for transfers between devices  49.7 us (33%)
  starting transfers between devices  40.3 us (27%)
  Pallas kernels  28.4 us (19%)
  blocking collectives  16.5 us (11%)
  other arithmetic  6.51 us (4%)
  local copies, waits for them, and re-layouts  5.64 us (4%)
    all_to_all x1, waiting for transfers between devices, per_device(): line_maps = widen(lax.all_to_all(maps.astype(LINK), 'z', 0, 0, tiled=True))  22.7 us
    ppermute x15, starting transfers between devices, around(): lax.ppermute(block, axis, [(i, (i + d + 1) % size) for i in range(size)])  22 us
    ppermute x15, waiting for transfers between devices, around(): lax.ppermute(block, axis, [(i, (i + d + 1) % size) for i in range(size)])  21.7 us
    all_to_all x1, blocking collectives, per_device(): lax.all_to_all(line_states.astype(LINK), 'z', 0, 0, tiled=True)  16.5 us
    pallas_call x1, Pallas kernels, per_device(): pl.pallas_call(functools.partial(maps_kernel, heads), grid=(count // head...  12.7 us
    all_to_all x1, starting transfers between devices, per_device(): line_maps = widen(lax.all_to_all(maps.astype(LINK), 'z', 0, 0, tiled=True))  10.1 us
    pallas_call x1, Pallas kernels, per_device(): pl.pallas_call(functools.partial(grads_kernel, heads), grid=(count // hea...  9.2 us
    ppermute x3, starting transfers between devices, per_device(): lax.ppermute(total, 'z', [(i, (i + d) % depth) for i in range(depth)])  4.17 us
  transfers between devices with their start and end apart: 22, of which 19 were waited for; matrix products, arithmetic and copies ran while one was open for 4% of the time, Pallas kernels for 0%

profile of v2, /device:TPU:0, one launch (start us, length us, event | category | flops | bytes accessed | tf_op | source)
XLA Modules:
  0.0 147.9 jit_solution(3381444218654113671)
XLA Ops:
  2.1 2.1 %collective-permute-start = (bf16[3,8,1024]{2,1,0:T(8,128)(2,1)S(1)}, bf16[3,8,1024]{2,1,0:T(8,128)(2,1)S(1)}, u32[]{:S(2)}, u32[]{:S(2)}) collective-permute-start(bf16[3,8,1024]{2,1,0:T(8,128)(2,1)S(1)} %pad_maximum_fusion), channel_id=1, source_target_pairs={{0,2},{2,4},{4,6},{6,8},{8,10},{10,12},{12,14},{14,16},{16,18},{18... | collective-permute-start | bytes 147464 | tf_op jit(solution)/shard_map/ppermute | solution.py:407
  6.6 12.7 %block_maps.1 = (f32[8,400,128]{2,1,0:T(8,128)}, f32[128,1024]{1,0:T(8,128)}, f32[128,1024]{1,0:T(8,128)}, f32[128,1024]{1,0:T(8,128)}, f32[128,1024]{1,0:T(8,12...) custom-call(bf16[128,1024]{1,0:T(8,128)(2,1)} %q_ref.3, ...), custom_call_target="tpu_custom_call" | custom-call | tf_op jit(solution)/shard_map/block_maps/pallas_call | solution.py:427
  19.3 2.4 %convert_element_type.60 = f16[8,400,128]{2,1,0:T(8,128)(2,1)} convert(f32[8,400,128]{2,1,0:T(8,128)} %get-tuple-element.36) | non-fusion elementwise | flops 409600 | bytes 2457600 | tf_op jit(solution)/shard_map/convert_element_type | solution.py:438
  21.7 10.1 %all-to-all-start = ((f16[8,400,128]{2,1,0:T(8,128)(2,1)}), f16[8,400,128]{2,1,0:T(8,128)(2,1)S(1)}, u32[]{:S(2)}, u32[]{:S(2)}) async-start(f16[8,400,128]{2,1,0:T(8,128)(2,1)} %convert_element_type.60), calls=%async_computation | async-start | bytes 1638400 | tf_op jit(solution)/shard_map/all_to_all | solution.py:438
  31.8 22.7 %all-to-all-done = f16[8,400,128]{2,1,0:T(8,128)(2,1)S(1)} async-done(((f16[8,400,128]{2,1,0:T(8,128)(2,1)}), f16[8,400,128]{2,1,0:T(8,128)(2,1)S(1)}, u32[]{:S(2)}, u32[]{:S(2)}) %all-to-all-start) | async-done | bytes 819232 | tf_op jit(solution)/shard_map/all_to_all | solution.py:438
  55.6 2.8 %collective-permute-start.3 = (f16[400,128]{1,0:T(8,128)(2,1)S(1)}, f16[400,128]{1,0:T(8,128)(2,1)S(1)}, u32[]{:S(2)}, u32[]{:S(2)}) collective-permute-start(f16[400,128]{1,0:T(8,128)(2,1)S(1)} %convert_element_type.62), channel_id=1, source_target_pairs={{0,48},{16,0},{32,16},{48,32},{1,49},{17,1},{33,17},{49,33},{2,50}... | collective-permute-start | bytes 307208 | tf_op jit(solution)/shard_map/ppermute | solution.py:447
  61.0 3.7 %collective-permute-done.2 = f16[400,128]{1,0:T(8,128)(2,1)S(1)} collective-permute-done((f16[400,128]{1,0:T(8,128)(2,1)S(1)}, f16[400,128]{1,0:T(8,128)(2,1)S(1)}, u32[]{:S(2)}, u32[]{:S(2)}) %collective-permute-start.2) | collective-permute-done | bytes 102432 | tf_op jit(solution)/shard_map/ppermute | solution.py:447
  67.1 3.1 %collective-permute-start.6 = (f16[272,128]{1,0:T(8,128)(2,1)S(1)}, f16[272,128]{1,0:T(8,128)(2,1)S(1)}, u32[]{:S(2)}, u32[]{:S(2)}) collective-permute-start(f16[272,128]{1,0:T(8,128)(2,1)S(1)} %convert_element_type.70), channel_id=1, source_target_pairs={{0,192},{64,0},{128,64},{192,128},{1,193},{65,1},{129,65},{193,129... | collective-permute-start | bytes 208904 | tf_op jit(solution)/shard_map/ppermute | solution.py:447
  72.2 3.9 %collective-permute-done.5 = f16[272,128]{1,0:T(8,128)(2,1)S(1)} collective-permute-done((f16[272,128]{1,0:T(8,128)(2,1)S(1)}, f16[272,128]{1,0:T(8,128)(2,1)S(1)}, u32[]{:S(2)}, u32[]{:S(2)}) %collective-permute-start.5) | collective-permute-done | bytes 69664 | tf_op jit(solution)/shard_map/ppermute | solution.py:447
  76.8 3.0 %line_states.1 = f32[8,272,128]{2,1,0:T(8,128)S(1)} custom-call(s32[2]{0:T(128)S(1)} %pad_add_fusion.where_ref, f32[8,400,128]{2,1,0:T(8,128)S(1)} %convert_element_type.61.maps_ref, f32[400,128]{1,0:T(8,128)S(1)} %convert_element_type.63.refs_1_.refs_0_, f32[400,128]{1,0:T(8,128)S(1)} %convert_element_type.64.refs_2_.refs_1_, ...), custom_call_target="tpu_custom_call" | custom-call | tf_op jit(solution)/shard_map/line_states/pallas_call | solution.py:459
  79.9 16.5 %all_to_all.10 = f16[8,272,128]{2,1,0:T(8,128)(2,1)S(1)} all-to-all(f16[8,272,128]{2,1,0:T(8,128)(2,1)S(1)} %convert_element_type.72), channel_id=1, replica_groups=mesh['y'=4,'x'=4,'z'=8,'head'=2] {'z'}, dimensions={0} | all-to-all | bytes 1114112 | tf_op jit(solution)/shard_map/all_to_all | solution.py:463
  97.5 9.2 %block_grads.1 = (bf16[128,1024]{1,0:T(8,128)(2,1)}, bf16[128,1024]{1,0:T(8,128)(2,1)}, bf16[128,1024]{1,0:T(8,128)(2,1)}, f32[3,16,1024]{2,1,0:T(8,128)}, f32[3...) custom-call(bf16[128,1024]{1,0:T(8,128)(2,1)} %q_ref.3, ...), custom_call_target="tpu_custom_call" | custom-call | tf_op jit(solution)/shard_map/block_grads/pallas_call | solution.py:465
  106.7 1.8 %collective-permute-start.8 = (f32[2,16,128]{2,1,0:T(8,128)}, f32[2,16,128]{2,1,0:T(8,128)S(1)}, u32[]{:S(2)}, u32[]{:S(2)}) collective-permute-start(f32[2,16,128]{2,1,0:T(8,128)} %get-tuple-element.60), channel_id=1, source_target_pairs={{0,16},{16,32},{32,48},{48,0},{1,17},{17,33},{33,49},{49,1},{2,18}... | collective-permute-start | bytes 49160 | tf_op jit(solution)/shard_map/ppermute | solution.py:447
  108.5 2.2 %collective-permute-start.9 = (f32[2,16,128]{2,1,0:T(8,128)}, f32[2,16,128]{2,1,0:T(8,128)S(1)}, u32[]{:S(2)}, u32[]{:S(2)}) collective-permute-start(f32[2,16,128]{2,1,0:T(8,128)} %get-tuple-element.61), channel_id=1, source_target_pairs={{0,32},{16,48},{32,0},{48,16},{1,33},{17,49},{33,1},{49,17},{2,34}... | collective-permute-start | bytes 49160 | tf_op jit(solution)/shard_map/ppermute | solution.py:447
  111.9 2.0 %collective-permute-done.9 = f32[2,16,128]{2,1,0:T(8,128)S(1)} collective-permute-done((f32[2,16,128]{2,1,0:T(8,128)}, f32[2,16,128]{2,1,0:T(8,128)S(1)}, u32[]{:S(2)}, u32[]{:S(2)}) %collective-permute-start.9) | collective-permute-done | bytes 16416 | tf_op jit(solution)/shard_map/ppermute | solution.py:447
  119.1 1.8 %collective-permute-done.12 = f32[2,16,128]{2,1,0:T(8,128)S(1)} collective-permute-done((f32[2,16,128]{2,1,0:T(8,128)S(1)}, f32[2,16,128]{2,1,0:T(8,128)S(1)}, u32[]{:S(2)}, u32[]{:S(2)}) %collective-permute-start.12) | collective-permute-done | bytes 16416 | tf_op jit(solution)/shard_map/ppermute | solution.py:447
  120.9 1.7 %collective-permute-done.11 = f32[2,16,128]{2,1,0:T(8,128)S(1)} collective-permute-done((f32[2,16,128]{2,1,0:T(8,128)S(1)}, f32[2,16,128]{2,1,0:T(8,128)S(1)}, u32[]{:S(2)}, u32[]{:S(2)}) %collective-permute-start.11) | collective-permute-done | bytes 16416 | tf_op jit(solution)/shard_map/ppermute | solution.py:447
  123.2 2.4 %collective-permute-start.15 = (f32[2,16,128]{2,1,0:T(8,128)S(1)}, f32[2,16,128]{2,1,0:T(8,128)S(1)}, u32[]{:S(2)}, u32[]{:S(2)}) collective-permute-start(f32[2,16,128]{2,1,0:T(8,128)S(1)} %add_add_fusion.1), channel_id=1, source_target_pairs={{0,4},{2,6},{4,8},{6,10},{8,12},{10,14},{12,0},{14,2},{1,5},{3,7},... | collective-permute-start | bytes 49160 | tf_op jit(solution)/shard_map/ppermute | solution.py:494
  126.8 1.5 %copy.17 = f32[128,8]{0,1:T(8,128)} copy(f32[128,8]{1,0:T(8,128)} %get-tuple-element.69) | data formatting | bytes 8192
  130.5 2.8 %collective-permute-done.14 = f32[2,16,128]{2,1,0:T(8,128)S(1)} collective-permute-done((f32[2,16,128]{2,1,0:T(8,128)S(1)}, f32[2,16,128]{2,1,0:T(8,128)S(1)}, u32[]{:S(2)}, u32[]{:S(2)}) %collective-permute-start.14) | collective-permute-done | bytes 16416 | tf_op jit(solution)/shard_map/ppermute | solution.py:494
  137.1 2.6 %collective-permute-start.20 = (f32[2,16,128]{2,1,0:T(8,128)S(1)}, f32[2,16,128]{2,1,0:T(8,128)S(1)}, u32[]{:S(2)}, u32[]{:S(2)}) collective-permute-start(f32[2,16,128]{2,1,0:T(8,128)S(1)} %add.45.refs_0_), channel_id=1, source_target_pairs={{0,48},{16,0},{32,16},{48,32},{1,49},{17,1},{33,17},{49,33},{2,50}... | collective-permute-start | bytes 49160 | tf_op jit(solution)/shard_map/ppermute | solution.py:447
  139.7 2.0 %collective-permute-start.19 = (f32[2,16,128]{2,1,0:T(8,128)S(1)}, f32[2,16,128]{2,1,0:T(8,128)S(1)}, u32[]{:S(2)}, u32[]{:S(2)}) collective-permute-start(f32[2,16,128]{2,1,0:T(8,128)S(1)} %add.45.refs_0_), channel_id=1, source_target_pairs={{0,32},{16,48},{32,0},{48,16},{1,33},{17,49},{33,1},{49,17},{2,34}... | collective-permute-start | bytes 49160 | tf_op jit(solution)/shard_map/ppermute | solution.py:447
  142.4 2.6 %collective-permute-done.19.refs_2_ = f32[2,16,128]{2,1,0:T(8,128)S(1)} collective-permute-done((f32[2,16,128]{2,1,0:T(8,128)S(1)}, f32[2,16,128]{2,1,0:T(8,128)S(1)}, u32[]{:S(2)}, u32[]{:S(2)}) %collective-permute-start.19) | collective-permute-done | bytes 16416 | tf_op jit(solution)/shard_map/ppermute | solution.py:447
  144.9 1.7 %collective-permute-done.18.refs_1_ = f32[2,16,128]{2,1,0:T(8,128)S(1)} collective-permute-done((f32[2,16,128]{2,1,0:T(8,128)S(1)}, f32[2,16,128]{2,1,0:T(8,128)S(1)}, u32[]{:S(2)}, u32[]{:S(2)}) %collective-permute-start.18) | collective-permute-done | bytes 16416 | tf_op jit(solution)/shard_map/ppermute | solution.py:447
  (60 shorter events, 29.7 us)
Async XLA Ops:
  2.1 3.8 %collective-permute-start = (bf16[3,8,1024]{2,1,0:T(8,128)(2,1)S(1)}, bf16[3,8,1024]{2,1,0:T(8,128)(2,1)S(1)}, u32[]{:S(2)}, u32[]{:S(2)}) collective-permute-start(bf16[3,8,1024]{2,1,0:T(8,128)(2,1)S(1)} %pad_maximum_fusion), channel_id=1, source_target_pairs={{0,2},{2,4},{4,6},{6,8},{8,10},{10,12},{12,14},{14,16},{16,18},{18... | collective-permute-start | bytes 147464 | tf_op jit(solution)/shard_map/ppermute | solution.py:407
  21.7 32.8 %all-to-all-start = ((f16[8,400,128]{2,1,0:T(8,128)(2,1)}), f16[8,400,128]{2,1,0:T(8,128)(2,1)S(1)}, u32[]{:S(2)}, u32[]{:S(2)}) async-start(f16[8,400,128]{2,1,0:T(8,128)(2,1)} %convert_element_type.60), calls=%async_computation | async-start | bytes 1638400 | tf_op jit(solution)/shard_map/all_to_all | solution.py:438
  55.6 5.4 %collective-permute-start.3 = (f16[400,128]{1,0:T(8,128)(2,1)S(1)}, f16[400,128]{1,0:T(8,128)(2,1)S(1)}, u32[]{:S(2)}, u32[]{:S(2)}) collective-permute-start(f16[400,128]{1,0:T(8,128)(2,1)S(1)} %convert_element_type.62), channel_id=1, source_target_pairs={{0,48},{16,0},{32,16},{48,32},{1,49},{17,1},{33,17},{49,33},{2,50}... | collective-permute-start | bytes 307208 | tf_op jit(solution)/shard_map/ppermute | solution.py:447
  58.5 6.2 %collective-permute-start.2 = (f16[400,128]{1,0:T(8,128)(2,1)S(1)}, f16[400,128]{1,0:T(8,128)(2,1)S(1)}, u32[]{:S(2)}, u32[]{:S(2)}) collective-permute-start(f16[400,128]{1,0:T(8,128)(2,1)S(1)} %convert_element_type.62), channel_id=1, source_target_pairs={{0,32},{16,48},{32,0},{48,16},{1,33},{17,49},{33,1},{49,17},{2,34}... | collective-permute-start | bytes 307208 | tf_op jit(solution)/shard_map/ppermute | solution.py:447
  59.3 6.5 %collective-permute-start.1 = (f16[400,128]{1,0:T(8,128)(2,1)S(1)}, f16[400,128]{1,0:T(8,128)(2,1)S(1)}, u32[]{:S(2)}, u32[]{:S(2)}) collective-permute-start(f16[400,128]{1,0:T(8,128)(2,1)S(1)} %convert_element_type.62), channel_id=1, source_target_pairs={{0,16},{16,32},{32,48},{48,0},{1,17},{17,33},{33,49},{49,1},{2,18}... | collective-permute-start | bytes 307208 | tf_op jit(solution)/shard_map/ppermute | solution.py:447
  60.2 19.6 %copy-start = (s32[2]{0:T(128)}, s32[2]{0:T(128)S(1)}, u32[]{:S(2)}) copy-start(s32[2]{0:T(128)S(1)} %pad_add_fusion.where_ref) | copy-start | bytes 28
  67.1 5.1 %collective-permute-start.6 = (f16[272,128]{1,0:T(8,128)(2,1)S(1)}, f16[272,128]{1,0:T(8,128)(2,1)S(1)}, u32[]{:S(2)}, u32[]{:S(2)}) collective-permute-start(f16[272,128]{1,0:T(8,128)(2,1)S(1)} %convert_element_type.70), channel_id=1, source_target_pairs={{0,192},{64,0},{128,64},{192,128},{1,193},{65,1},{129,65},{193,129... | collective-permute-start | bytes 208904 | tf_op jit(solution)/shard_map/ppermute | solution.py:447
  70.2 5.8 %collective-permute-start.5 = (f16[272,128]{1,0:T(8,128)(2,1)S(1)}, f16[272,128]{1,0:T(8,128)(2,1)S(1)}, u32[]{:S(2)}, u32[]{:S(2)}) collective-permute-start(f16[272,128]{1,0:T(8,128)(2,1)S(1)} %convert_element_type.68), channel_id=1, source_target_pairs={{0,128},{64,192},{128,0},{192,64},{1,129},{65,193},{129,1},{193,65... | collective-permute-start | bytes 208904 | tf_op jit(solution)/shard_map/ppermute | solution.py:447
  70.8 5.9 %collective-permute-start.4 = (f16[272,128]{1,0:T(8,128)(2,1)S(1)}, f16[272,128]{1,0:T(8,128)(2,1)S(1)}, u32[]{:S(2)}, u32[]{:S(2)}) collective-permute-start(f16[272,128]{1,0:T(8,128)(2,1)S(1)} %convert_element_type.66), channel_id=1, source_target_pairs={{0,64},{64,128},{128,192},{192,0},{1,65},{65,129},{129,193},{193,1... | collective-permute-start | bytes 208904 | tf_op jit(solution)/shard_map/ppermute | solution.py:447
  97.5 49.2 %copy-start.1 = (s32[2]{0:T(128)S(1)}, s32[2]{0:T(128)}, u32[]{:S(2)}) copy-start(s32[2]{0:T(128)} %copy-done) | copy-start | bytes 28
  106.7 5.2 %collective-permute-start.8 = (f32[2,16,128]{2,1,0:T(8,128)}, f32[2,16,128]{2,1,0:T(8,128)S(1)}, u32[]{:S(2)}, u32[]{:S(2)}) collective-permute-start(f32[2,16,128]{2,1,0:T(8,128)} %get-tuple-element.60), channel_id=1, source_target_pairs={{0,16},{16,32},{32,48},{48,0},{1,17},{17,33},{33,49},{49,1},{2,18}... | collective-permute-start | bytes 49160 | tf_op jit(solution)/shard_map/ppermute | solution.py:447
  108.5 5.5 %collective-permute-start.9 = (f32[2,16,128]{2,1,0:T(8,128)}, f32[2,16,128]{2,1,0:T(8,128)S(1)}, u32[]{:S(2)}, u32[]{:S(2)}) collective-permute-start(f32[2,16,128]{2,1,0:T(8,128)} %get-tuple-element.61), channel_id=1, source_target_pairs={{0,32},{16,48},{32,0},{48,16},{1,33},{17,49},{33,1},{49,17},{2,34}... | collective-permute-start | bytes 49160 | tf_op jit(solution)/shard_map/ppermute | solution.py:447
  110.7 3.9 %collective-permute-start.10 = (f32[2,16,128]{2,1,0:T(8,128)}, f32[2,16,128]{2,1,0:T(8,128)S(1)}, u32[]{:S(2)}, u32[]{:S(2)}) collective-permute-start(f32[2,16,128]{2,1,0:T(8,128)} %get-tuple-element.62), channel_id=1, source_target_pairs={{0,48},{16,0},{32,16},{48,32},{1,49},{17,1},{33,17},{49,33},{2,50}... | collective-permute-start | bytes 49160 | tf_op jit(solution)/shard_map/ppermute | solution.py:447
  115.4 3.7 %collective-permute-start.13 = (f32[2,16,128]{2,1,0:T(8,128)S(1)}, f32[2,16,128]{2,1,0:T(8,128)S(1)}, u32[]{:S(2)}, u32[]{:S(2)}) collective-permute-start(f32[2,16,128]{2,1,0:T(8,128)S(1)} %add_add_fusion.2), channel_id=1, source_target_pairs={{0,192},{64,0},{128,64},{192,128},{1,193},{65,1},{129,65},{193,129... | collective-permute-start | bytes 49160 | tf_op jit(solution)/shard_map/ppermute | solution.py:447
  115.9 4.9 %collective-permute-start.12 = (f32[2,16,128]{2,1,0:T(8,128)S(1)}, f32[2,16,128]{2,1,0:T(8,128)S(1)}, u32[]{:S(2)}, u32[]{:S(2)}) collective-permute-start(f32[2,16,128]{2,1,0:T(8,128)S(1)} %add_add_fusion.2), channel_id=1, source_target_pairs={{0,64},{64,128},{128,192},{192,0},{1,65},{65,129},{129,193},{193,1... | collective-permute-start | bytes 49160 | tf_op jit(solution)/shard_map/ppermute | solution.py:447
  117.4 5.2 %collective-permute-start.11 = (f32[2,16,128]{2,1,0:T(8,128)S(1)}, f32[2,16,128]{2,1,0:T(8,128)S(1)}, u32[]{:S(2)}, u32[]{:S(2)}) collective-permute-start(f32[2,16,128]{2,1,0:T(8,128)S(1)} %add_add_fusion.2), channel_id=1, source_target_pairs={{0,128},{64,192},{128,0},{192,64},{1,129},{65,193},{129,1},{193,65... | collective-permute-start | bytes 49160 | tf_op jit(solution)/shard_map/ppermute | solution.py:447
  122.6 7.9 %collective-permute-start.16 = (f32[2,16,128]{2,1,0:T(8,128)S(1)}, f32[2,16,128]{2,1,0:T(8,128)S(1)}, u32[]{:S(2)}, u32[]{:S(2)}) collective-permute-start(f32[2,16,128]{2,1,0:T(8,128)S(1)} %add_add_fusion.1), channel_id=1, source_target_pairs={{0,12},{2,14},{4,0},{6,2},{8,4},{10,6},{12,8},{14,10},{1,13},{3,15... | collective-permute-start | bytes 49160 | tf_op jit(solution)/shard_map/ppermute | solution.py:494
  123.2 7.3 %collective-permute-start.15 = (f32[2,16,128]{2,1,0:T(8,128)S(1)}, f32[2,16,128]{2,1,0:T(8,128)S(1)}, u32[]{:S(2)}, u32[]{:S(2)}) collective-permute-start(f32[2,16,128]{2,1,0:T(8,128)S(1)} %add_add_fusion.1), channel_id=1, source_target_pairs={{0,4},{2,6},{4,8},{6,10},{8,12},{10,14},{12,0},{14,2},{1,5},{3,7},... | collective-permute-start | bytes 49160 | tf_op jit(solution)/shard_map/ppermute | solution.py:494
  125.6 7.6 %collective-permute-start.14 = (f32[2,16,128]{2,1,0:T(8,128)S(1)}, f32[2,16,128]{2,1,0:T(8,128)S(1)}, u32[]{:S(2)}, u32[]{:S(2)}) collective-permute-start(f32[2,16,128]{2,1,0:T(8,128)S(1)} %add_add_fusion.1), channel_id=1, source_target_pairs={{0,8},{2,10},{4,12},{6,14},{8,0},{10,2},{12,4},{14,6},{1,9},{3,11}... | collective-permute-start | bytes 49160 | tf_op jit(solution)/shard_map/ppermute | solution.py:494
  129.2 6.0 %collective-permute-start.7 = (bf16[3,8,1024]{2,1,0:T(8,128)(2,1)S(1)}, bf16[3,8,1024]{2,1,0:T(8,128)(2,1)S(1)}, u32[]{:S(2)}, u32[]{:S(2)}) collective-permute-start(bf16[3,8,1024]{2,1,0:T(8,128)(2,1)S(1)} %convert_element_type.74), channel_id=1, source_target_pairs={{2,0},{4,2},{6,4},{8,6},{10,8},{12,10},{14,12},{16,14},{18,16},{20... | collective-permute-start | bytes 147464 | tf_op jit(solution)/shard_map/ppermute | solution.py:483
  133.3 3.8 %collective-permute-start.17 = (f32[2,16,128]{2,1,0:T(8,128)S(1)}, f32[2,16,128]{2,1,0:T(8,128)S(1)}, u32[]{:S(2)}, u32[]{:S(2)}) collective-permute-start(f32[2,16,128]{2,1,0:T(8,128)S(1)} %add_add_fusion), channel_id=1, source_target_pairs={{0,2},{2,0},{4,6},{6,4},{8,10},{10,8},{12,14},{14,12},{1,3},{3,1},... | collective-permute-start | bytes 49160 | tf_op jit(solution)/shard_map/ppermute | solution.py:497
  137.1 5.2 %collective-permute-start.20 = (f32[2,16,128]{2,1,0:T(8,128)S(1)}, f32[2,16,128]{2,1,0:T(8,128)S(1)}, u32[]{:S(2)}, u32[]{:S(2)}) collective-permute-start(f32[2,16,128]{2,1,0:T(8,128)S(1)} %add.45.refs_0_), channel_id=1, source_target_pairs={{0,48},{16,0},{32,16},{48,32},{1,49},{17,1},{33,17},{49,33},{2,50}... | collective-permute-start | bytes 49160 | tf_op jit(solution)/shard_map/ppermute | solution.py:447
  139.7 5.2 %collective-permute-start.19 = (f32[2,16,128]{2,1,0:T(8,128)S(1)}, f32[2,16,128]{2,1,0:T(8,128)S(1)}, u32[]{:S(2)}, u32[]{:S(2)}) collective-permute-start(f32[2,16,128]{2,1,0:T(8,128)S(1)} %add.45.refs_0_), channel_id=1, source_target_pairs={{0,32},{16,48},{32,0},{48,16},{1,33},{17,49},{33,1},{49,17},{2,34}... | collective-permute-start | bytes 49160 | tf_op jit(solution)/shard_map/ppermute | solution.py:447
  141.7 4.9 %collective-permute-start.18 = (f32[2,16,128]{2,1,0:T(8,128)S(1)}, f32[2,16,128]{2,1,0:T(8,128)S(1)}, u32[]{:S(2)}, u32[]{:S(2)}) collective-permute-start(f32[2,16,128]{2,1,0:T(8,128)S(1)} %add.45.refs_0_), channel_id=1, source_target_pairs={{0,16},{16,32},{32,48},{48,0},{1,17},{17,33},{33,49},{49,1},{2,18}... | collective-permute-start | bytes 49160 | tf_op jit(solution)/shard_map/ppermute | solution.py:447
  (1 other events, 0.6 us)

commit v3 on v2

--- a/solution.py
+++ b/solution.py
@@ -18,6 +18,7 @@
 TN = (((0,), (0,)), ((), ()))
 MIB = 1024 * 1024
 AUX = 16
+WIDEST = 128
 LINK = jnp.float16
 TOP = 13.0
 FLOOR = -200.0
@@ -29,13 +30,26 @@
 
 
 def dot(a, b, dims):
-    total = None
-    for i, left in enumerate(a):
-        for j, right in enumerate(b):
-            if i + j < 2:
-                term = lax.dot_general(left, right, dims, preferred_element_type=F32)
-                total = term if total is None else total + term
-    return total
+    (left_dim,), (right_dim,) = dims[0]
+    width = b[0].shape[1 - right_dim]
+
+    def run(left, right):
+        return lax.dot_general(left, right, dims, preferred_element_type=F32)
+
+    if len(a) == 1 and len(b) == 1:
+        return run(a[0], b[0])
+    if len(b) == 1:
+        return run(jnp.concatenate(a, axis=left_dim), jnp.concatenate([b[0]] * 2, axis=right_dim))
+    if len(a) == 1:
+        both = run(a[0], jnp.concatenate(b, axis=1 - right_dim))
+        return both[:, :width] + both[:, width:]
+    left = jnp.concatenate(a, axis=left_dim)
+    right = jnp.concatenate([b[0]] * 2, axis=right_dim)
+    if width > WIDEST:
+        return run(left, right) + run(a[0], b[1])
+    low = jnp.concatenate([b[1]] * 2, axis=right_dim)
+    both = run(left, jnp.concatenate([right, low], axis=1 - right_dim))
+    return both[:, :width] + both[:, width:]
 
 
 def lanes(*parts):
@@ -54,8 +68,9 @@
     return 1.0 / (1.0 + jnp.exp(-x))
 
 
-def column(block, head):
-    return jnp.sum(jnp.where(iota(block.shape, 1) == head, block, 0.0), axis=1, keepdims=True)
+def column(ref, head):
+    square = iota((T, T), 0) == iota((T, T), 1)
+    return jnp.sum(jnp.where(square, sigmoid(ref[pl.ds(head, 1)]), 0.0), axis=1, keepdims=True)
 
 
 def gate_factors(cumul):
@@ -110,7 +125,6 @@
     lower = row >= col
     ident = jnp.where(row == col, 1.0, 0.0)
     tri = jnp.where(lower, 1.0, 0.0).astype(BF16)
-    beta_all = sigmoid(beta_ref[...])
     base = pl.program_id(0) * heads
     each = range(heads)
     at = [slice(h * T, (h + 1) * T) for h in each]
@@ -126,10 +140,10 @@
         )
         cumul.append(both[:, :T] + both[:, T:])
         cum_out[:, at[h]] = cumul[h]
-        betas.append(column(beta_all, base + h))
+        betas.append(column(beta_ref, base + h))
         acts = []
         for j, (raw, factor) in enumerate(((q_ref, fq_out), (k_ref, fk_out), (v_ref, fv_out))):
-            ext[j, h, 0:8] = halo_ref[j, :, at[h]].astype(F32)
+            ext[j, h, 5:8] = halo_ref[:, at[h]].astype(F32)[3 * j : 3 * j + 3]
             ext[j, h, 8:136] = raw[:, at[h]].astype(F32)
             pre = conv_ref[j, 0:1, at[h]] * ext[j, h, 5 : 5 + T]
             for i in range(1, 4):
@@ -276,29 +290,30 @@
 
 def grads_kernel(
     heads,
-    q_ref, k_ref, v_ref, halo_ref, beta_ref, conv_ref, grad_ref, states_ref, where_ref,
+    q_ref, k_ref, v_ref, halo_ref, beta_ref, conv_ref, grad_ref, states_ref,
     q_in, k_in, fq_in, fk_in, fv_in, cum_in, gf_in, ld_in, w_in, u_in, pg_in, inv_in,
-    dq_out, dk_out, dv_out, edge_out, tail_out, dgate_out, dbeta_out, sum0_out, sum1_out, sum2_out, sum3_out,
-    ext, back, params,
+    dq_out, dk_out, dv_out, edge_out, tail_out, dgate_out, dbeta_out, params,
+    ext, back, tail,
 ):
     row, col = iota((T, T), 0), iota((T, T), 1)
     strict = row > col
     lower = row >= col
     upper = jnp.where(row <= col, 1.0, 0.0).astype(BF16)
     ones = jnp.ones((8, T), BF16)
-    beta_all = sigmoid(beta_ref[...])
+    tail[9:16] = jnp.zeros((7, T), F32)
     base = pl.program_id(0) * heads
     each = range(heads)
     at = [slice(h * T, (h + 1) * T) for h in each]
     deltas, dds, grads = [], [], []
-    betas = [column(beta_all, base + h) for h in each]
+    betas = [column(beta_ref, base + h) for h in each]
     factors = [gate_factors(cum_in[:, at[h]]) for h in each]
     states = [get(states_ref.at[h]) for h in each]
     ms = [split(states[h][0]) for h in each]
     gs = [split(states[h][1]) for h in each]
     qs = [q_in[:, at[h]] for h in each]
     ks = [k_in[:, at[h]] for h in each]
-    dbeta = jnp.zeros(dbeta_out.shape, F32)
+    for h in each:
+        params[h, 13:16] = jnp.zeros((3, T), F32)
     for h in each:
         deltas.append(u_in[h] - dot(split(w_in[h]), ms[h], NN))
         dds.append(pg_in[h] + dot(split(ks[h] * factors[h][4]), gs[h], NN))
@@ -336,16 +351,16 @@
         )
         dlog = both[:, :T] + both[:, T:] + dlast
         dgate_out[:, at[h]] = dlog * gf_in[:, at[h]]
-        params[base + h, 12:13] = jnp.sum(dlog * ld_in[:, at[h]], axis=0, keepdims=True)
+        params[h, 12:13] = jnp.sum(dlog * ld_in[:, at[h]], axis=0, keepdims=True)
         write = jnp.sum(des[h] * deltas[h], axis=1, keepdims=True) * (1.0 - betas[h])
-        dbeta = jnp.where(iota(dbeta.shape, 1) == base + h, write, dbeta)
+        dbeta_out[pl.ds(base + h, 1)] = jnp.sum(jnp.where(row == col, write, 0.0), axis=0, keepdims=True)
         pres = (
             fq_in[:, at[h]] * (dq - q * jnp.sum(q * dq, axis=1, keepdims=True)),
             fk_in[:, at[h]] * (dk - k * jnp.sum(k * dk, axis=1, keepdims=True)),
             fv_in[:, at[h]] * dvs[h],
         )
         for j, (raw, out) in enumerate(((q_ref, dq_out), (k_ref, dk_out), (v_ref, dv_out))):
-            ext[j, h, 0:8] = halo_ref[j, :, at[h]].astype(F32)
+            ext[j, h, 5:8] = halo_ref[:, at[h]].astype(F32)[3 * j : 3 * j + 3]
             ext[j, h, 8:136] = raw[:, at[h]].astype(F32)
             back[j, h, 0:8] = jnp.zeros((8, T), F32)
             back[j, h, 8:136] = pres[j]
@@ -354,40 +369,38 @@
             for i in range(4):
                 part = conv_ref[j, i : i + 1, at[h]] * back[j, h, 3 - i : 3 - i + 136]
                 whole = part if whole is None else whole + part
-                params[base + h, 4 * j + i : 4 * j + i + 1] = jnp.sum(
+                params[h, 4 * j + i : 4 * j + i + 1] = jnp.sum(
                     pres[j] * ext[j, h, 5 + i : 5 + i + T], axis=0, keepdims=True
                 )
             out[:, at[h]] = whole[8:136].astype(BF16)
-            tail_out[j, :, at[h]] = whole[0:8]
+            tail[3 * j : 3 * j + 3] = whole[5:8]
             edge_out[j, :, at[h]] = whole[120:136]
-
-    @pl.when(pl.program_id(0) == 0)
-    def _():
-        dbeta_out[...] = dbeta
-
-    @pl.when(pl.program_id(0) > 0)
-    def _():
-        dbeta_out[...] = dbeta_out[...] + dbeta
-
-    @pl.when(pl.program_id(0) == pl.num_programs(0) - 1)
-    def _():
-        for d, out in enumerate((sum0_out, sum1_out, sum2_out, sum3_out)):
-            share = out.shape[0]
-            out[:, 13:16] = jnp.zeros((share, 3, T), F32)
-            for r in range(share):
-                out[r, 0:13] = params[lax.rem(where_ref[1] + d, 4) * share + r, 0:13]
-
-
-def gather_kernel(where_ref, *refs):
-    *pieces, conv_out, decay_out, held = refs
-    for d, piece in enumerate(pieces):
-        held[lax.rem(where_ref[1] - d + 4, 4)] = piece[...]
-    for p in range(4):
-        for r in range(held.shape[1]):
-            lane = (p * held.shape[1] + r) * T
-            for j in range(3):
-                conv_out[j, :, lane : lane + T] = held[p, r, 4 * j : 4 * j + 4]
-            decay_out[:, lane : lane + T] = held[p, r, 12:13]
+        tail_out[:, at[h]] = tail[...].astype(BF16)
+
+
+def ends_kernel(q_ref, k_ref, v_ref, out_ref):
+    row = iota(out_ref.shape, 0)
+    packed = jnp.zeros(out_ref.shape, F32)
+    for j, ref in enumerate((q_ref, k_ref, v_ref)):
+        turned = pltpu.roll(ref[...].astype(F32), 3 * j + 3, axis=0)
+        packed = jnp.where((row >= 3 * j) & (row < 3 * j + 3), turned, packed)
+    out_ref[...] = packed.astype(BF16)
+
+
+def share_kernel(parts_ref, out_ref):
+    total = parts_ref[0]
+    for i in range(1, parts_ref.shape[0]):
+        total = total + parts_ref[i]
+    for i in range(out_ref.shape[0]):
+        out_ref[i] = total
+
+
+def gather_kernel(parts_ref, conv_out, decay_out):
+    for h in range(parts_ref.shape[0]):
+        lane = slice(h * T, (h + 1) * T)
+        for j in range(3):
+            conv_out[j, :, lane] = parts_ref[h, 4 * j : 4 * j + 4]
+        decay_out[:, lane] = parts_ref[h, 12:13]
 
 
 def widen(x):
@@ -400,21 +413,25 @@
     lines, planes = lax.axis_size("x"), lax.axis_size("y")
     depth = lax.axis_size("z")
     devices = lines * planes * depth
-    heads = GROUP
-    wide = heads * T
     wheres = jnp.stack([lax.axis_index("y"), lax.axis_index("x")]).astype(jnp.int32)
-    ends = jnp.stack([query_raw[length - 8 :], key_raw[length - 8 :], value_raw[length - 8 :]])
+    ends = pl.pallas_call(
+        ends_kernel, grid=(1,), out_shape=jax.ShapeDtypeStruct((16, channels), BF16),
+        in_specs=[pl.BlockSpec((16, channels), lambda i: (length // 16 - 1, 0))] * 3,
+        out_specs=pl.BlockSpec((16, channels), lambda i: (0, 0)), name="last_rows",
+        compiler_params=pltpu.CompilerParams(vmem_limit_bytes=60 * MIB),
+    )(query_raw, key_raw, value_raw)
     halo = lax.ppermute(ends, SEQ, [(i, i + 1) for i in range(devices - 1)])
     decay_row = decay_log.reshape(1, channels)
 
-    tall = pl.BlockSpec((T, wide), lambda h: (0, h))
-    edge = pl.BlockSpec((3, 8, wide), lambda h: (0, 0, h))
-    taps = pl.BlockSpec((3, 4, wide), lambda h: (0, 0, h))
-    beta_spec = pl.BlockSpec((T, count), lambda h: (0, 0))
-    square = pl.BlockSpec((heads, T, T), lambda h: (h, 0, 0))
-
-    def stack_spec(n):
-        return pl.BlockSpec((heads, n * T, T), lambda h: (h, 0, 0))
+    def specs(heads):
+        wide = heads * T
+        return (
+            pl.BlockSpec((T, wide), lambda h: (0, h)),
+            pl.BlockSpec((16, wide), lambda h: (0, h)),
+            pl.BlockSpec((3, 4, wide), lambda h: (0, 0, h)),
+            pl.BlockSpec((count, T), lambda h: (0, 0)),
+            pl.BlockSpec((heads, T, T), lambda h: (h, 0, 0)),
+        )
 
     def like(*shape, dtype=F32):
         return jax.ShapeDtypeStruct(shape, dtype)
@@ -423,6 +440,9 @@
         dimension_semantics=("arbitrary",), vmem_limit_bytes=60 * MIB
     )
     saved_shapes = [like(length, channels)] * 8 + [like(count, T, T)] * 4
+    heads = MAPS_GROUP
+    wide = heads * T
+    tall, edge, taps, beta_spec, square = specs(heads)
     saved_specs = [tall] * 8 + [square] * 4
     maps, *saved = pl.pallas_call(
         functools.partial(maps_kernel, heads),
@@ -433,7 +453,7 @@
         scratch_shapes=[pltpu.VMEM((3, heads, 136, T), F32)],
         compiler_params=params,
         name="block_maps",
-    )(query_raw, key_raw, value_raw, halo, gate_raw, beta_raw, conv_weight, decay_row, grad_out)
+    )(query_raw, key_raw, value_raw, halo, gate_raw, beta_raw.T, conv_weight, decay_row, grad_out)
 
     line_maps = widen(lax.all_to_all(maps.astype(LINK), "z", 0, 0, tiled=True))
     small = pltpu.CompilerParams(vmem_limit_bytes=32 * MIB)
@@ -462,55 +482,62 @@
     )(wheres, line_maps, *from_lines, *from_planes)
     states = widen(lax.all_to_all(line_states.astype(LINK), "z", 0, 0, tiled=True))
 
-    dq, dk, dv, edges, tails, dgate, dbeta, *sums = pl.pallas_call(
+    heads = GRADS_GROUP
+    wide = heads * T
+    tall, edge, taps, beta_spec, square = specs(heads)
+    saved_specs = [tall] * 8 + [square] * 4
+    dq, dk, dv, edges, tails, dgate, dbeta, sums = pl.pallas_call(
         functools.partial(grads_kernel, heads),
         grid=(count // heads,),
         in_specs=[
             tall, tall, tall, edge, beta_spec, taps, tall,
-            pl.BlockSpec((heads, 2 * T + AUX, T), lambda h: (h, 0, 0)), smem,
+            pl.BlockSpec((heads, 2 * T + AUX, T), lambda h: (h, 0, 0)),
         ] + saved_specs,
         out_specs=[
             tall, tall, tall,
             pl.BlockSpec((3, 16, wide), lambda h: (0, 0, h)), edge, tall, beta_spec,
-        ] + [pl.BlockSpec((count // lines, 16, T), lambda h: (0, 0, 0))] * lines,
+            pl.BlockSpec((heads, 16, T), lambda h: (h, 0, 0)),
+        ],
         out_shape=[like(length, channels, dtype=BF16)] * 3
-        + [like(3, 16, channels), like(3, 8, channels), like(length, channels), like(length, count)] + [like(count // lines, 16, T)] * lines,
-        scratch_shapes=[pltpu.VMEM((3, heads, 136, T), F32), pltpu.VMEM((3, heads, 144, T), F32), pltpu.VMEM((count, 16, T), F32)],
+        + [like(3, 16, channels), like(16, channels, dtype=BF16), like(length, channels), like(count, length), like(count, 16, T)],
+        scratch_shapes=[pltpu.VMEM((3, heads, 136, T), F32), pltpu.VMEM((3, heads, 144, T), F32), pltpu.VMEM((16, T), F32)],
         compiler_params=params,
         name="block_grads",
-    )(query_raw, key_raw, value_raw, halo, beta_raw, conv_weight, grad_out, states, wheres, *saved)
-
-    after = lax.ppermute(tails.astype(BF16), SEQ, [(i + 1, i) for i in range(devices - 1)])
-    fixed = edges + jnp.pad(after.astype(F32), ((0, 0), (8, 0), (0, 0)))
-
+    )(query_raw, key_raw, value_raw, halo, beta_raw.T, conv_weight, grad_out, states, *saved)
+
+    after = lax.ppermute(tails, SEQ, [(i + 1, i) for i in range(devices - 1)])
     def finish(full, extra):
         return lax.dynamic_update_slice(full, extra.astype(BF16), (length - 16, 0))
 
-    one, two, three = around(sums[1:], "x")
-    total = (sums[0] + one) + (two + three)
-    one, two, three = around([total] * 3, "y")
-    total = (total + two) + (one + three)
-    two, four, six = [
-        lax.ppermute(total, "z", [(i, (i + d) % depth) for i in range(depth)]) for d in (2, 4, 6)
-    ]
-    total = (total + four) + (two + six)
-    total = total + lax.ppermute(total, "z", [(i, i ^ 1) for i in range(depth)])
+
+    def share(parts, copies):
+        return pl.pallas_call(
+            share_kernel, out_shape=like(copies, 16, T), name="share_sums", compiler_params=small
+        )(parts)
+
+    across = ("y", "x")
+    sums = share(lax.all_to_all(sums, "z", 0, 0, tiled=True), lines * planes)
+    sums = share(lax.all_to_all(sums, across, 0, 0, tiled=True), depth)
+    sums, after = lax.optimization_barrier((sums, after))
+    fixed = edges + jnp.pad(after[:9].astype(F32).reshape(3, 3, channels), ((0, 0), (13, 0), (0, 0)))
+
     conv_sum, decay_sum = pl.pallas_call(
-        gather_kernel, out_shape=[like(3, 4, channels), like(1, channels)], in_specs=[smem] + [vmem] * 4,
-        scratch_shapes=[pltpu.VMEM((4, count // lines, 16, T), F32)], name="gather_sums", compiler_params=small,
-    )(wheres, total, *around([total] * 3, "x"))
+        gather_kernel, out_shape=[like(3, 4, channels), like(1, channels)],
+        name="gather_sums", compiler_params=small,
+    )(lax.all_to_all(sums, "z", 0, 0, tiled=True))
     return (
         finish(dq, fixed[0]),
         finish(dk, fixed[1]),
         finish(dv, fixed[2]),
         dgate,
-        dbeta,
+        dbeta.T,
         conv_sum,
         decay_sum.reshape(channels),
     )
 
 
-GROUP = 4
+MAPS_GROUP = 8
+GRADS_GROUP = 4
 
 
 def solution(mesh):

time: 149 us -> 144 us (0.966); the launches traced: 148 us -> 141 us
  blocking collectives: 16.5 us -> 28.1 us
  starting transfers between devices: 40.3 us -> 30.8 us
  local copies, waits for them, and re-layouts: 5.64 us -> 1.28 us
  other arithmetic: 6.51 us -> 4.87 us
  waiting for transfers between devices: 49.7 us -> 48.1 us
    all_to_all x0 -> x2, waiting for transfers between devices: none -> 13.4 us  [the longest x1 6.7 us: per_device(): lax.all_to_all(sums, 'z', 0, 0, tiled=True)]
    ppermute x15 -> x6, starting transfers between devices: 22 us -> 9.47 us  [around(): lax.ppermute(block, axis, [(i, (i + d + 1) % size) for i in range(size)])]
    all_to_all x0 -> x1, blocking collectives: none -> 11.6 us  [per_device(): sums = share(lax.all_to_all(sums, 'z', 0, 0, tiled=True), lines * planes)]
    ppermute x15 -> x6, waiting for transfers between devices: 21.7 us -> 10.1 us  [around(): lax.ppermute(block, axis, [(i, (i + d + 1) % size) for i in range(size)])]
    all_to_all x0 -> x2, starting transfers between devices: none -> 7.97 us  [the longest x1 4.61 us: per_device(): sums = share(lax.all_to_all(sums, across, 0, 0, tiled=True), depth)]
    ppermute x5 -> x1, waiting for transfers between devices: 4.98 us -> 0.01 us  [per_device(): after = lax.ppermute(tails, SEQ, [(i + 1, i) for i in range(devices - 1)])]
    ppermute x5 -> x1, starting transfers between devices: 6.11 us -> 1.29 us  [per_device(): after = lax.ppermute(tails, SEQ, [(i + 1, i) for i in range(devices - 1)])]
    unnamed x8 -> x2, local copies, waits for them, and re-layouts: 3.54 us -> 0.61 us
  transfers between devices with their start and end apart: 22 -> 11, of which waited for: 19 -> 10; matrix products, arithmetic and copies ran while one was open for 4% -> 1% of each run, Pallas kernels for 0% -> 0%
where the time goes in v3:
time: 144 us; the launch traced here: 141 us
  waiting for transfers between devices  48.1 us (33%)
  starting transfers between devices  30.8 us (21%)
  blocking collectives  28.1 us (20%)
  Pallas kernels  27 us (19%)
  other arithmetic  4.87 us (3%)
    all_to_all x1, waiting for transfers between devices, per_device(): line_maps = widen(lax.all_to_all(maps.astype(LINK), 'z', 0, 0, tiled=True))  22.7 us
    all_to_all x1, blocking collectives, per_device(): lax.all_to_all(line_states.astype(LINK), 'z', 0, 0, tiled=True)  16.5 us
    all_to_all x1, blocking collectives, per_device(): sums = share(lax.all_to_all(sums, 'z', 0, 0, tiled=True), lines * planes)  11.6 us
    pallas_call x1, Pallas kernels, per_device(): pl.pallas_call(functools.partial(maps_kernel, heads), grid=(count // head...  10.6 us
    ppermute x6, waiting for transfers between devices, around(): lax.ppermute(block, axis, [(i, (i + d + 1) % size) for i in range(size)])  10.1 us
    all_to_all x1, starting transfers between devices, per_device(): line_maps = widen(lax.all_to_all(maps.astype(LINK), 'z', 0, 0, tiled=True))  9.97 us
    ppermute x6, starting transfers between devices, around(): lax.ppermute(block, axis, [(i, (i + d + 1) % size) for i in range(size)])  9.47 us
    pallas_call x1, Pallas kernels, per_device(): pl.pallas_call(functools.partial(grads_kernel, heads), grid=(count // hea...  7.91 us
  transfers between devices with their start and end apart: 11, of which 10 were waited for; matrix products, arithmetic and copies ran while one was open for 1% of the time, Pallas kernels for 0%

profile of v3, /device:TPU:0, one launch (start us, length us, event | category | flops | bytes accessed | tf_op | source)
XLA Modules:
  0.0 140.9 jit_solution(6421851471475729193)
XLA Ops:
  0.6 1.4 %last_rows.1 = bf16[16,1024]{1,0:T(8,128)(2,1)} custom-call(bf16[128,1024]{1,0:T(8,128)(2,1)} %q_ref.5, bf16[128,1024]{1,0:T(8,128)(2,1)} %k_ref.5, bf16[128,1024]{1,0:T(8,128)(2,1)} %v_ref.5), custom_call_target="tpu_custom_call" | custom-call | tf_op jit(solution)/shard_map/last_rows/pallas_call | solution.py:417
  2.1 2.1 %collective-permute-start = (bf16[16,1024]{1,0:T(8,128)(2,1)}, bf16[16,1024]{1,0:T(8,128)(2,1)S(1)}, u32[]{:S(2)}, u32[]{:S(2)}) collective-permute-start(bf16[16,1024]{1,0:T(8,128)(2,1)} %last_rows.1), channel_id=1, source_target_pairs={{0,2},{2,4},{4,6},{6,8},{8,10},{10,12},{12,14},{14,16},{16,18},{18... | collective-permute-start | bytes 98312 | tf_op jit(solution)/shard_map/ppermute | solution.py:423
  4.1 1.9 %collective-permute-done.halo_ref = bf16[16,1024]{1,0:T(8,128)(2,1)S(1)} collective-permute-done((bf16[16,1024]{1,0:T(8,128)(2,1)}, bf16[16,1024]{1,0:T(8,128)(2,1)S(1)}, u32[]{:S(2)}, u32[]{:S(2)}) %collective-permute-start) | collective-permute-done | bytes 32800 | tf_op jit(solution)/shard_map/ppermute | solution.py:423
  6.7 10.6 %block_maps.1 = (f32[8,400,128]{2,1,0:T(8,128)}, f32[128,1024]{1,0:T(8,128)}, f32[128,1024]{1,0:T(8,128)}, f32[128,1024]{1,0:T(8,128)}, f32[128,1024]{1,0:T(8,12...) custom-call(bf16[128,1024]{1,0:T(8,128)(2,1)} %q_ref.5, ...), custom_call_target="tpu_custom_call" | custom-call | tf_op jit(solution)/shard_map/block_maps/pallas_call | solution.py:447
  17.2 2.4 %convert_element_type.57 = f16[8,400,128]{2,1,0:T(8,128)(2,1)} convert(f32[8,400,128]{2,1,0:T(8,128)} %get-tuple-element.35) | non-fusion elementwise | flops 409600 | bytes 2457600 | tf_op jit(solution)/shard_map/convert_element_type | solution.py:458
  19.7 10.0 %all-to-all-start = ((f16[8,400,128]{2,1,0:T(8,128)(2,1)}), f16[8,400,128]{2,1,0:T(8,128)(2,1)S(1)}, u32[]{:S(2)}, u32[]{:S(2)}) async-start(f16[8,400,128]{2,1,0:T(8,128)(2,1)} %convert_element_type.57), calls=%async_computation | async-start | bytes 1638400 | tf_op jit(solution)/shard_map/all_to_all | solution.py:458
  29.6 22.7 %all-to-all-done = f16[8,400,128]{2,1,0:T(8,128)(2,1)S(1)} async-done(((f16[8,400,128]{2,1,0:T(8,128)(2,1)}), f16[8,400,128]{2,1,0:T(8,128)(2,1)S(1)}, u32[]{:S(2)}, u32[]{:S(2)}) %all-to-all-start) | async-done | bytes 819232 | tf_op jit(solution)/shard_map/all_to_all | solution.py:458
  53.3 2.8 %collective-permute-start.3 = (f16[400,128]{1,0:T(8,128)(2,1)S(1)}, f16[400,128]{1,0:T(8,128)(2,1)S(1)}, u32[]{:S(2)}, u32[]{:S(2)}) collective-permute-start(f16[400,128]{1,0:T(8,128)(2,1)S(1)} %convert_element_type.59), channel_id=1, source_target_pairs={{0,48},{16,0},{32,16},{48,32},{1,49},{17,1},{33,17},{49,33},{2,50}... | collective-permute-start | bytes 307208 | tf_op jit(solution)/shard_map/ppermute | solution.py:467
  58.7 3.7 %collective-permute-done.2 = f16[400,128]{1,0:T(8,128)(2,1)S(1)} collective-permute-done((f16[400,128]{1,0:T(8,128)(2,1)S(1)}, f16[400,128]{1,0:T(8,128)(2,1)S(1)}, u32[]{:S(2)}, u32[]{:S(2)}) %collective-permute-start.2) | collective-permute-done | bytes 102432 | tf_op jit(solution)/shard_map/ppermute | solution.py:467
  62.4 1.0 collective-permute-done.1
  63.5 1.2 plane_total.1
  64.7 3.1 %collective-permute-start.6 = (f16[272,128]{1,0:T(8,128)(2,1)S(1)}, f16[272,128]{1,0:T(8,128)(2,1)S(1)}, u32[]{:S(2)}, u32[]{:S(2)}) collective-permute-start(f16[272,128]{1,0:T(8,128)(2,1)S(1)} %convert_element_type.67), channel_id=1, source_target_pairs={{0,192},{64,0},{128,64},{192,128},{1,193},{65,1},{129,65},{193,129... | collective-permute-start | bytes 208904 | tf_op jit(solution)/shard_map/ppermute | solution.py:467
  68.5 1.2 collective-permute-start.4
  69.8 3.9 %collective-permute-done.5 = f16[272,128]{1,0:T(8,128)(2,1)S(1)} collective-permute-done((f16[272,128]{1,0:T(8,128)(2,1)S(1)}, f16[272,128]{1,0:T(8,128)(2,1)S(1)}, u32[]{:S(2)}, u32[]{:S(2)}) %collective-permute-start.5) | collective-permute-done | bytes 69664 | tf_op jit(solution)/shard_map/ppermute | solution.py:467
  74.4 3.0 %line_states.1 = f32[8,272,128]{2,1,0:T(8,128)S(1)} custom-call(s32[2]{0:T(128)S(1)} %pad_add_fusion.where_ref, f32[8,400,128]{2,1,0:T(8,128)S(1)} %convert_element_type.58.maps_ref, f32[400,128]{1,0:T(8,128)S(1)} %convert_element_type.60.refs_1_.refs_0_, f32[400,128]{1,0:T(8,128)S(1)} %convert_element_type.61.refs_2_.refs_1_, ...), custom_call_target="tpu_custom_call" | custom-call | tf_op jit(solution)/shard_map/line_states/pallas_call | solution.py:479
  77.5 16.5 %all_to_all.25 = f16[8,272,128]{2,1,0:T(8,128)(2,1)S(1)} all-to-all(f16[8,272,128]{2,1,0:T(8,128)(2,1)S(1)} %convert_element_type.69), channel_id=1, replica_groups=mesh['y'=4,'x'=4,'z'=8,'head'=2] {'z'}, dimensions={0} | all-to-all | bytes 1114112 | tf_op jit(solution)/shard_map/all_to_all | solution.py:483
  94.0 1.1 convert_element_type.70.states_ref
  95.1 7.9 %block_grads.1 = (bf16[128,1024]{1,0:T(8,128)(2,1)}, bf16[128,1024]{1,0:T(8,128)(2,1)}, bf16[128,1024]{1,0:T(8,128)(2,1)}, f32[3,16,1024]{2,1,0:T(8,128)}, bf16[...) custom-call(bf16[128,1024]{1,0:T(8,128)(2,1)} %q_ref.5, ...), custom_call_target="tpu_custom_call" | custom-call | tf_op jit(solution)/shard_map/block_grads/pallas_call | solution.py:489
  103.0 11.6 %all_to_all.26.parts_ref = f32[8,16,128]{2,1,0:T(8,128)S(1)} all-to-all(f32[8,16,128]{2,1,0:T(8,128)} %get-tuple-element.53), channel_id=1, replica_groups=mesh['y'=4,'x'=4,'z'=8,'head'=2] {'z'}, dimensions={0} | all-to-all | bytes 131072 | tf_op jit(solution)/shard_map/all_to_all | solution.py:519
  115.3 4.6 %all-to-all-start.3 = ((f32[16,16,128]{2,1,0:T(8,128)}), f32[16,16,128]{2,1,0:T(8,128)S(1)}, u32[]{:S(2)}, u32[]{:S(2)}) async-start(f32[16,16,128]{2,1,0:T(8,128)} %share_sums.2), calls=%async_computation.3 | async-start | bytes 262144 | tf_op jit(solution)/shard_map/all_to_all | solution.py:520
  119.9 1.3 collective-permute-start.7
  121.2 6.7 %all-to-all-done.3.parts_ref = f32[16,16,128]{2,1,0:T(8,128)S(1)} async-done(((f32[16,16,128]{2,1,0:T(8,128)}), f32[16,16,128]{2,1,0:T(8,128)S(1)}, u32[]{:S(2)}, u32[]{:S(2)}) %all-to-all-start.3) | async-done | bytes 131104 | tf_op jit(solution)/shard_map/all_to_all | solution.py:520
  128.6 3.4 %all-to-all-start.4 = ((f32[8,16,128]{2,1,0:T(8,128)}), f32[8,16,128]{2,1,0:T(8,128)S(1)}, u32[]{:S(2)}, u32[]{:S(2)}) async-start(f32[8,16,128]{2,1,0:T(8,128)} %share_sums.3), calls=%async_computation.4 | async-start | bytes 131072 | tf_op jit(solution)/shard_map/all_to_all | solution.py:527
  133.6 6.7 %all-to-all-done.4.parts_ref = f32[8,16,128]{2,1,0:T(8,128)S(1)} async-done(((f32[8,16,128]{2,1,0:T(8,128)}), f32[8,16,128]{2,1,0:T(8,128)S(1)}, u32[]{:S(2)}, u32[]{:S(2)}) %all-to-all-start.4) | async-done | bytes 65568 | tf_op jit(solution)/shard_map/all_to_all | solution.py:527
  (29 shorter events, 9.3 us)
Async XLA Ops:
  2.1 4.0 %collective-permute-start = (bf16[16,1024]{1,0:T(8,128)(2,1)}, bf16[16,1024]{1,0:T(8,128)(2,1)S(1)}, u32[]{:S(2)}, u32[]{:S(2)}) collective-permute-start(bf16[16,1024]{1,0:T(8,128)(2,1)} %last_rows.1), channel_id=1, source_target_pairs={{0,2},{2,4},{4,6},{6,8},{8,10},{10,12},{12,14},{14,16},{16,18},{18... | collective-permute-start | bytes 98312 | tf_op jit(solution)/shard_map/ppermute | solution.py:423
  6.0 0.6 copy-start
  19.7 32.6 %all-to-all-start = ((f16[8,400,128]{2,1,0:T(8,128)(2,1)}), f16[8,400,128]{2,1,0:T(8,128)(2,1)S(1)}, u32[]{:S(2)}, u32[]{:S(2)}) async-start(f16[8,400,128]{2,1,0:T(8,128)(2,1)} %convert_element_type.57), calls=%async_computation | async-start | bytes 1638400 | tf_op jit(solution)/shard_map/all_to_all | solution.py:458
  53.3 5.4 %collective-permute-start.3 = (f16[400,128]{1,0:T(8,128)(2,1)S(1)}, f16[400,128]{1,0:T(8,128)(2,1)S(1)}, u32[]{:S(2)}, u32[]{:S(2)}) collective-permute-start(f16[400,128]{1,0:T(8,128)(2,1)S(1)} %convert_element_type.59), channel_id=1, source_target_pairs={{0,48},{16,0},{32,16},{48,32},{1,49},{17,1},{33,17},{49,33},{2,50}... | collective-permute-start | bytes 307208 | tf_op jit(solution)/shard_map/ppermute | solution.py:467
  56.2 6.2 %collective-permute-start.2 = (f16[400,128]{1,0:T(8,128)(2,1)S(1)}, f16[400,128]{1,0:T(8,128)(2,1)S(1)}, u32[]{:S(2)}, u32[]{:S(2)}) collective-permute-start(f16[400,128]{1,0:T(8,128)(2,1)S(1)} %convert_element_type.59), channel_id=1, source_target_pairs={{0,32},{16,48},{32,0},{48,16},{1,33},{17,49},{33,1},{49,17},{2,34}... | collective-permute-start | bytes 307208 | tf_op jit(solution)/shard_map/ppermute | solution.py:467
  57.0 6.5 %collective-permute-start.1 = (f16[400,128]{1,0:T(8,128)(2,1)S(1)}, f16[400,128]{1,0:T(8,128)(2,1)S(1)}, u32[]{:S(2)}, u32[]{:S(2)}) collective-permute-start(f16[400,128]{1,0:T(8,128)(2,1)S(1)} %convert_element_type.59), channel_id=1, source_target_pairs={{0,16},{16,32},{32,48},{48,0},{1,17},{17,33},{33,49},{49,1},{2,18}... | collective-permute-start | bytes 307208 | tf_op jit(solution)/shard_map/ppermute | solution.py:467
  64.7 5.1 %collective-permute-start.6 = (f16[272,128]{1,0:T(8,128)(2,1)S(1)}, f16[272,128]{1,0:T(8,128)(2,1)S(1)}, u32[]{:S(2)}, u32[]{:S(2)}) collective-permute-start(f16[272,128]{1,0:T(8,128)(2,1)S(1)} %convert_element_type.67), channel_id=1, source_target_pairs={{0,192},{64,0},{128,64},{192,128},{1,193},{65,1},{129,65},{193,129... | collective-permute-start | bytes 208904 | tf_op jit(solution)/shard_map/ppermute | solution.py:467
  67.8 5.8 %collective-permute-start.5 = (f16[272,128]{1,0:T(8,128)(2,1)S(1)}, f16[272,128]{1,0:T(8,128)(2,1)S(1)}, u32[]{:S(2)}, u32[]{:S(2)}) collective-permute-start(f16[272,128]{1,0:T(8,128)(2,1)S(1)} %convert_element_type.65), channel_id=1, source_target_pairs={{0,128},{64,192},{128,0},{192,64},{1,129},{65,193},{129,1},{193,65... | collective-permute-start | bytes 208904 | tf_op jit(solution)/shard_map/ppermute | solution.py:467
  68.5 5.9 %collective-permute-start.4 = (f16[272,128]{1,0:T(8,128)(2,1)S(1)}, f16[272,128]{1,0:T(8,128)(2,1)S(1)}, u32[]{:S(2)}, u32[]{:S(2)}) collective-permute-start(f16[272,128]{1,0:T(8,128)(2,1)S(1)} %convert_element_type.63), channel_id=1, source_target_pairs={{0,64},{64,128},{128,192},{192,0},{1,65},{65,129},{129,193},{193,1... | collective-permute-start | bytes 208904 | tf_op jit(solution)/shard_map/ppermute | solution.py:467
  115.3 12.6 %all-to-all-start.3 = ((f32[16,16,128]{2,1,0:T(8,128)}), f32[16,16,128]{2,1,0:T(8,128)S(1)}, u32[]{:S(2)}, u32[]{:S(2)}) async-start(f32[16,16,128]{2,1,0:T(8,128)} %share_sums.2), calls=%async_computation.3 | async-start | bytes 262144 | tf_op jit(solution)/shard_map/all_to_all | solution.py:520
  119.9 8.6 %collective-permute-start.7 = (bf16[16,1024]{1,0:T(8,128)(2,1)}, bf16[16,1024]{1,0:T(8,128)(2,1)S(1)}, u32[]{:S(2)}, u32[]{:S(2)}) collective-permute-start(bf16[16,1024]{1,0:T(8,128)(2,1)} %get-tuple-element.54), channel_id=1, source_target_pairs={{2,0},{4,2},{6,4},{8,6},{10,8},{12,10},{14,12},{16,14},{18,16},{20... | collective-permute-start | bytes 98312 | tf_op jit(solution)/shard_map/ppermute | solution.py:508
  128.6 11.7 %all-to-all-start.4 = ((f32[8,16,128]{2,1,0:T(8,128)}), f32[8,16,128]{2,1,0:T(8,128)S(1)}, u32[]{:S(2)}, u32[]{:S(2)}) async-start(f32[8,16,128]{2,1,0:T(8,128)} %share_sums.3), calls=%async_computation.4 | async-start | bytes 131072 | tf_op jit(solution)/shard_map/all_to_all | solution.py:527

commit v4 on v3

--- a/solution.py
+++ b/solution.py
@@ -501,7 +501,9 @@
         out_shape=[like(length, channels, dtype=BF16)] * 3
         + [like(3, 16, channels), like(16, channels, dtype=BF16), like(length, channels), like(count, length), like(count, 16, T)],
         scratch_shapes=[pltpu.VMEM((3, heads, 136, T), F32), pltpu.VMEM((3, heads, 144, T), F32), pltpu.VMEM((16, T), F32)],
-        compiler_params=params,
+        compiler_params=pltpu.CompilerParams(
+            dimension_semantics=("arbitrary",), vmem_limit_bytes=26 * MIB
+        ),
         name="block_grads",
     )(query_raw, key_raw, value_raw, halo, beta_raw.T, conv_weight, grad_out, states, *saved)
 

time: 144 us -> 140 us (0.972)
  other arithmetic: 4.87 us -> 2.93 us
  Pallas kernels: 27 us -> 25.2 us
    pallas_call x1, Pallas kernels: 7.91 us -> 6.13 us  [per_device(): pl.pallas_call(functools.partial(grads_kernel, heads), grid=(count // hea...]
where the time goes in v4:
time: 140 us; the launch traced here: 138 us
  waiting for transfers between devices  49 us (35%)
  starting transfers between devices  30.8 us (22%)
  blocking collectives  27.5 us (20%)
  Pallas kernels  25.2 us (18%)
  other arithmetic  2.93 us (2%)
    all_to_all x1, waiting for transfers between devices, per_device(): line_maps = widen(lax.all_to_all(maps.astype(LINK), 'z', 0, 0, tiled=True))  22.7 us
    all_to_all x1, blocking collectives, per_device(): lax.all_to_all(line_states.astype(LINK), 'z', 0, 0, tiled=True)  16.8 us
    all_to_all x1, blocking collectives, per_device(): sums = share(lax.all_to_all(sums, 'z', 0, 0, tiled=True), lines * planes)  10.7 us
    pallas_call x1, Pallas kernels, per_device(): pl.pallas_call(functools.partial(maps_kernel, heads), grid=(count // head...  10.6 us
    ppermute x6, waiting for transfers between devices, around(): lax.ppermute(block, axis, [(i, (i + d + 1) % size) for i in range(size)])  10.1 us
    all_to_all x1, starting transfers between devices, per_device(): line_maps = widen(lax.all_to_all(maps.astype(LINK), 'z', 0, 0, tiled=True))  9.97 us
    ppermute x6, starting transfers between devices, around(): lax.ppermute(block, axis, [(i, (i + d + 1) % size) for i in range(size)])  9.47 us
    all_to_all x1, waiting for transfers between devices, per_device(): lax.all_to_all(sums, 'z', 0, 0, tiled=True)  7.62 us
  transfers between devices with their start and end apart: 11, of which 10 were waited for; matrix products, arithmetic and copies ran while one was open for 1% of the time, Pallas kernels for 0%

profile of v4, /device:TPU:0, one launch (start us, length us, event | category | flops | bytes accessed | tf_op | source)
XLA Modules:
  0.0 137.9 jit_solution(9271063829719089796)
XLA Ops:
  0.6 1.4 %last_rows.1 = bf16[16,1024]{1,0:T(8,128)(2,1)} custom-call(bf16[128,1024]{1,0:T(8,128)(2,1)} %q_ref.5, bf16[128,1024]{1,0:T(8,128)(2,1)} %k_ref.5, bf16[128,1024]{1,0:T(8,128)(2,1)} %v_ref.5), custom_call_target="tpu_custom_call" | custom-call | tf_op jit(solution)/shard_map/last_rows/pallas_call | solution.py:417
  2.1 2.1 %collective-permute-start = (bf16[16,1024]{1,0:T(8,128)(2,1)}, bf16[16,1024]{1,0:T(8,128)(2,1)S(1)}, u32[]{:S(2)}, u32[]{:S(2)}) collective-permute-start(bf16[16,1024]{1,0:T(8,128)(2,1)} %last_rows.1), channel_id=1, source_target_pairs={{0,2},{2,4},{4,6},{6,8},{8,10},{10,12},{12,14},{14,16},{16,18},{18... | collective-permute-start | bytes 98312 | tf_op jit(solution)/shard_map/ppermute | solution.py:423
  4.1 1.9 %collective-permute-done.halo_ref = bf16[16,1024]{1,0:T(8,128)(2,1)S(1)} collective-permute-done((bf16[16,1024]{1,0:T(8,128)(2,1)}, bf16[16,1024]{1,0:T(8,128)(2,1)S(1)}, u32[]{:S(2)}, u32[]{:S(2)}) %collective-permute-start) | collective-permute-done | bytes 32800 | tf_op jit(solution)/shard_map/ppermute | solution.py:423
  6.7 10.6 %block_maps.1 = (f32[8,400,128]{2,1,0:T(8,128)}, f32[128,1024]{1,0:T(8,128)}, f32[128,1024]{1,0:T(8,128)}, f32[128,1024]{1,0:T(8,128)}, f32[128,1024]{1,0:T(8,12...) custom-call(bf16[128,1024]{1,0:T(8,128)(2,1)} %q_ref.5, ...), custom_call_target="tpu_custom_call" | custom-call | tf_op jit(solution)/shard_map/block_maps/pallas_call | solution.py:447
  17.3 2.4 %convert_element_type.57 = f16[8,400,128]{2,1,0:T(8,128)(2,1)} convert(f32[8,400,128]{2,1,0:T(8,128)} %get-tuple-element.35) | non-fusion elementwise | flops 409600 | bytes 2457600 | tf_op jit(solution)/shard_map/convert_element_type | solution.py:458
  19.7 10.0 %all-to-all-start = ((f16[8,400,128]{2,1,0:T(8,128)(2,1)}), f16[8,400,128]{2,1,0:T(8,128)(2,1)S(1)}, u32[]{:S(2)}, u32[]{:S(2)}) async-start(f16[8,400,128]{2,1,0:T(8,128)(2,1)} %convert_element_type.57), calls=%async_computation | async-start | bytes 1638400 | tf_op jit(solution)/shard_map/all_to_all | solution.py:458
  29.7 22.7 %all-to-all-done = f16[8,400,128]{2,1,0:T(8,128)(2,1)S(1)} async-done(((f16[8,400,128]{2,1,0:T(8,128)(2,1)}), f16[8,400,128]{2,1,0:T(8,128)(2,1)S(1)}, u32[]{:S(2)}, u32[]{:S(2)}) %all-to-all-start) | async-done | bytes 819232 | tf_op jit(solution)/shard_map/all_to_all | solution.py:458
  52.5 0.9 line_total.1.refs_0_
  53.4 2.8 %collective-permute-start.3 = (f16[400,128]{1,0:T(8,128)(2,1)S(1)}, f16[400,128]{1,0:T(8,128)(2,1)S(1)}, u32[]{:S(2)}, u32[]{:S(2)}) collective-permute-start(f16[400,128]{1,0:T(8,128)(2,1)S(1)} %convert_element_type.59), channel_id=1, source_target_pairs={{0,48},{16,0},{32,16},{48,32},{1,49},{17,1},{33,17},{49,33},{2,50}... | collective-permute-start | bytes 307208 | tf_op jit(solution)/shard_map/ppermute | solution.py:467
  58.8 3.7 %collective-permute-done.2 = f16[400,128]{1,0:T(8,128)(2,1)S(1)} collective-permute-done((f16[400,128]{1,0:T(8,128)(2,1)S(1)}, f16[400,128]{1,0:T(8,128)(2,1)S(1)}, u32[]{:S(2)}, u32[]{:S(2)}) %collective-permute-start.2) | collective-permute-done | bytes 102432 | tf_op jit(solution)/shard_map/ppermute | solution.py:467
  62.5 1.0 collective-permute-done.1
  63.5 1.2 plane_total.1
  64.8 3.1 %collective-permute-start.6 = (f16[272,128]{1,0:T(8,128)(2,1)S(1)}, f16[272,128]{1,0:T(8,128)(2,1)S(1)}, u32[]{:S(2)}, u32[]{:S(2)}) collective-permute-start(f16[272,128]{1,0:T(8,128)(2,1)S(1)} %convert_element_type.67), channel_id=1, source_target_pairs={{0,192},{64,0},{128,64},{192,128},{1,193},{65,1},{129,65},{193,129... | collective-permute-start | bytes 208904 | tf_op jit(solution)/shard_map/ppermute | solution.py:467
  68.5 1.2 collective-permute-start.4
  69.9 3.9 %collective-permute-done.5 = f16[272,128]{1,0:T(8,128)(2,1)S(1)} collective-permute-done((f16[272,128]{1,0:T(8,128)(2,1)S(1)}, f16[272,128]{1,0:T(8,128)(2,1)S(1)}, u32[]{:S(2)}, u32[]{:S(2)}) %collective-permute-start.5) | collective-permute-done | bytes 69664 | tf_op jit(solution)/shard_map/ppermute | solution.py:467
  74.5 3.0 %line_states.1 = f32[8,272,128]{2,1,0:T(8,128)S(1)} custom-call(s32[2]{0:T(128)S(1)} %pad_add_fusion.where_ref, f32[8,400,128]{2,1,0:T(8,128)S(1)} %convert_element_type.58.maps_ref, f32[400,128]{1,0:T(8,128)S(1)} %convert_element_type.60.refs_1_.refs_0_, f32[400,128]{1,0:T(8,128)S(1)} %convert_element_type.61.refs_2_.refs_1_, ...), custom_call_target="tpu_custom_call" | custom-call | tf_op jit(solution)/shard_map/line_states/pallas_call | solution.py:479
  77.8 16.8 %all_to_all.25 = f16[8,272,128]{2,1,0:T(8,128)(2,1)S(1)} all-to-all(f16[8,272,128]{2,1,0:T(8,128)(2,1)S(1)} %convert_element_type.69), channel_id=1, replica_groups=mesh['y'=4,'x'=4,'z'=8,'head'=2] {'z'}, dimensions={0} | all-to-all | bytes 1114112 | tf_op jit(solution)/shard_map/all_to_all | solution.py:483
  94.8 6.1 %block_grads.1 = (bf16[128,1024]{1,0:T(8,128)(2,1)}, bf16[128,1024]{1,0:T(8,128)(2,1)}, bf16[128,1024]{1,0:T(8,128)(2,1)}, f32[3,16,1024]{2,1,0:T(8,128)S(1)}, b...) custom-call(bf16[128,1024]{1,0:T(8,128)(2,1)S(1)} %copy-done, ...), custom_call_target="tpu_custom_call" | custom-call | tf_op jit(solution)/shard_map/block_grads/pallas_call | solution.py:489
  100.9 10.7 %all_to_all.26.parts_ref = f32[8,16,128]{2,1,0:T(8,128)S(1)} all-to-all(f32[8,16,128]{2,1,0:T(8,128)S(1)} %get-tuple-element.53), channel_id=1, replica_groups=mesh['y'=4,'x'=4,'z'=8,'head'=2] {'z'}, dimensions={0} | all-to-all | bytes 131072 | tf_op jit(solution)/shard_map/all_to_all | solution.py:521
  112.3 4.6 %all-to-all-start.3 = ((f32[16,16,128]{2,1,0:T(8,128)}), f32[16,16,128]{2,1,0:T(8,128)S(1)}, u32[]{:S(2)}, u32[]{:S(2)}) async-start(f32[16,16,128]{2,1,0:T(8,128)} %share_sums.2), calls=%async_computation.3 | async-start | bytes 262144 | tf_op jit(solution)/shard_map/all_to_all | solution.py:522
  116.9 1.3 collective-permute-start.7
  118.2 6.7 %all-to-all-done.3.parts_ref = f32[16,16,128]{2,1,0:T(8,128)S(1)} async-done(((f32[16,16,128]{2,1,0:T(8,128)}), f32[16,16,128]{2,1,0:T(8,128)S(1)}, u32[]{:S(2)}, u32[]{:S(2)}) %all-to-all-start.3) | async-done | bytes 131104 | tf_op jit(solution)/shard_map/all_to_all | solution.py:522
  125.6 3.4 %all-to-all-start.4 = ((f32[8,16,128]{2,1,0:T(8,128)}), f32[8,16,128]{2,1,0:T(8,128)S(1)}, u32[]{:S(2)}, u32[]{:S(2)}) async-start(f32[8,16,128]{2,1,0:T(8,128)} %share_sums.3), calls=%async_computation.4 | async-start | bytes 131072 | tf_op jit(solution)/shard_map/all_to_all | solution.py:529
  129.7 7.6 %all-to-all-done.4.parts_ref = f32[8,16,128]{2,1,0:T(8,128)S(1)} async-done(((f32[8,16,128]{2,1,0:T(8,128)}), f32[8,16,128]{2,1,0:T(8,128)S(1)}, u32[]{:S(2)}, u32[]{:S(2)}) %all-to-all-start.4) | async-done | bytes 65568 | tf_op jit(solution)/shard_map/all_to_all | solution.py:529
  (67 shorter events, 7.7 us)
Async XLA Ops:
  2.1 4.0 %collective-permute-start = (bf16[16,1024]{1,0:T(8,128)(2,1)}, bf16[16,1024]{1,0:T(8,128)(2,1)S(1)}, u32[]{:S(2)}, u32[]{:S(2)}) collective-permute-start(bf16[16,1024]{1,0:T(8,128)(2,1)} %last_rows.1), channel_id=1, source_target_pairs={{0,2},{2,4},{4,6},{6,8},{8,10},{10,12},{12,14},{14,16},{16,18},{18... | collective-permute-start | bytes 98312 | tf_op jit(solution)/shard_map/ppermute | solution.py:423
  19.7 32.6 %all-to-all-start = ((f16[8,400,128]{2,1,0:T(8,128)(2,1)}), f16[8,400,128]{2,1,0:T(8,128)(2,1)S(1)}, u32[]{:S(2)}, u32[]{:S(2)}) async-start(f16[8,400,128]{2,1,0:T(8,128)(2,1)} %convert_element_type.57), calls=%async_computation | async-start | bytes 1638400 | tf_op jit(solution)/shard_map/all_to_all | solution.py:458
  53.4 5.4 %collective-permute-start.3 = (f16[400,128]{1,0:T(8,128)(2,1)S(1)}, f16[400,128]{1,0:T(8,128)(2,1)S(1)}, u32[]{:S(2)}, u32[]{:S(2)}) collective-permute-start(f16[400,128]{1,0:T(8,128)(2,1)S(1)} %convert_element_type.59), channel_id=1, source_target_pairs={{0,48},{16,0},{32,16},{48,32},{1,49},{17,1},{33,17},{49,33},{2,50}... | collective-permute-start | bytes 307208 | tf_op jit(solution)/shard_map/ppermute | solution.py:467
  56.2 6.2 %collective-permute-start.2 = (f16[400,128]{1,0:T(8,128)(2,1)S(1)}, f16[400,128]{1,0:T(8,128)(2,1)S(1)}, u32[]{:S(2)}, u32[]{:S(2)}) collective-permute-start(f16[400,128]{1,0:T(8,128)(2,1)S(1)} %convert_element_type.59), channel_id=1, source_target_pairs={{0,32},{16,48},{32,0},{48,16},{1,33},{17,49},{33,1},{49,17},{2,34}... | collective-permute-start | bytes 307208 | tf_op jit(solution)/shard_map/ppermute | solution.py:467
  57.0 6.5 %collective-permute-start.1 = (f16[400,128]{1,0:T(8,128)(2,1)S(1)}, f16[400,128]{1,0:T(8,128)(2,1)S(1)}, u32[]{:S(2)}, u32[]{:S(2)}) collective-permute-start(f16[400,128]{1,0:T(8,128)(2,1)S(1)} %convert_element_type.59), channel_id=1, source_target_pairs={{0,16},{16,32},{32,48},{48,0},{1,17},{17,33},{33,49},{49,1},{2,18}... | collective-permute-start | bytes 307208 | tf_op jit(solution)/shard_map/ppermute | solution.py:467
  64.8 5.1 %collective-permute-start.6 = (f16[272,128]{1,0:T(8,128)(2,1)S(1)}, f16[272,128]{1,0:T(8,128)(2,1)S(1)}, u32[]{:S(2)}, u32[]{:S(2)}) collective-permute-start(f16[272,128]{1,0:T(8,128)(2,1)S(1)} %convert_element_type.67), channel_id=1, source_target_pairs={{0,192},{64,0},{128,64},{192,128},{1,193},{65,1},{129,65},{193,129... | collective-permute-start | bytes 208904 | tf_op jit(solution)/shard_map/ppermute | solution.py:467
  67.9 5.8 %collective-permute-start.5 = (f16[272,128]{1,0:T(8,128)(2,1)S(1)}, f16[272,128]{1,0:T(8,128)(2,1)S(1)}, u32[]{:S(2)}, u32[]{:S(2)}) collective-permute-start(f16[272,128]{1,0:T(8,128)(2,1)S(1)} %convert_element_type.65), channel_id=1, source_target_pairs={{0,128},{64,192},{128,0},{192,64},{1,129},{65,193},{129,1},{193,65... | collective-permute-start | bytes 208904 | tf_op jit(solution)/shard_map/ppermute | solution.py:467
  68.5 5.9 %collective-permute-start.4 = (f16[272,128]{1,0:T(8,128)(2,1)S(1)}, f16[272,128]{1,0:T(8,128)(2,1)S(1)}, u32[]{:S(2)}, u32[]{:S(2)}) collective-permute-start(f16[272,128]{1,0:T(8,128)(2,1)S(1)} %convert_element_type.63), channel_id=1, source_target_pairs={{0,64},{64,128},{128,192},{192,0},{1,65},{65,129},{129,193},{193,1... | collective-permute-start | bytes 208904 | tf_op jit(solution)/shard_map/ppermute | solution.py:467
  74.5 20.1 %copy-start.10 = (f32[128,1024]{1,0:T(8,128)S(1)}, f32[128,1024]{1,0:T(8,128)}, u32[]{:S(2)}) copy-start(f32[128,1024]{1,0:T(8,128)} %get-tuple-element.45.gf_in) | copy-start | bytes 1572868
  74.5 20.1 %copy-start.11 = (f32[128,1024]{1,0:T(8,128)S(1)}, f32[128,1024]{1,0:T(8,128)}, u32[]{:S(2)}) copy-start(f32[128,1024]{1,0:T(8,128)} %get-tuple-element.46.ld_in) | copy-start | bytes 1572868
  74.5 20.1 %copy-start.12 = (f32[8,128,128]{2,1,0:T(8,128)S(1)}, f32[8,128,128]{2,1,0:T(8,128)}, u32[]{:S(2)}) copy-start(f32[8,128,128]{2,1,0:T(8,128)} %get-tuple-element.47.w_in) | copy-start | bytes 1572868
  74.5 20.1 %copy-start.13 = (f32[8,128,128]{2,1,0:T(8,128)S(1)}, f32[8,128,128]{2,1,0:T(8,128)}, u32[]{:S(2)}) copy-start(f32[8,128,128]{2,1,0:T(8,128)} %get-tuple-element.48.u_in) | copy-start | bytes 1572868
  74.5 20.1 %copy-start.14 = (f32[8,128,128]{2,1,0:T(8,128)S(1)}, f32[8,128,128]{2,1,0:T(8,128)}, u32[]{:S(2)}) copy-start(f32[8,128,128]{2,1,0:T(8,128)} %get-tuple-element.49.pg_in) | copy-start | bytes 1572868
  74.5 20.1 %copy-start.15 = (f32[8,128,128]{2,1,0:T(8,128)S(1)}, f32[8,128,128]{2,1,0:T(8,128)}, u32[]{:S(2)}) copy-start(f32[8,128,128]{2,1,0:T(8,128)} %get-tuple-element.50.inv_in) | copy-start | bytes 1572868
  77.5 17.1 %copy-start.7 = (f32[128,1024]{1,0:T(8,128)S(1)}, f32[128,1024]{1,0:T(8,128)}, u32[]{:S(2)}) copy-start(f32[128,1024]{1,0:T(8,128)} %get-tuple-element.42.fk_in) | copy-start | bytes 1572868
  77.5 17.1 %copy-start.8 = (f32[128,1024]{1,0:T(8,128)S(1)}, f32[128,1024]{1,0:T(8,128)}, u32[]{:S(2)}) copy-start(f32[128,1024]{1,0:T(8,128)} %get-tuple-element.43.fv_in) | copy-start | bytes 1572868
  77.6 17.1 %copy-start.9 = (f32[128,1024]{1,0:T(8,128)S(1)}, f32[128,1024]{1,0:T(8,128)}, u32[]{:S(2)}) copy-start(f32[128,1024]{1,0:T(8,128)} %get-tuple-element.44.cum_in) | copy-start | bytes 1572868
  77.7 17.0 %copy-start = (bf16[128,1024]{1,0:T(8,128)(2,1)S(1)}, bf16[128,1024]{1,0:T(8,128)(2,1)}, u32[]{:S(2)}) copy-start(bf16[128,1024]{1,0:T(8,128)(2,1)} %q_ref.5) | copy-start | bytes 786436
  77.7 17.0 %copy-start.1 = (bf16[128,1024]{1,0:T(8,128)(2,1)S(1)}, bf16[128,1024]{1,0:T(8,128)(2,1)}, u32[]{:S(2)}) copy-start(bf16[128,1024]{1,0:T(8,128)(2,1)} %k_ref.5) | copy-start | bytes 786436
  77.7 17.0 %copy-start.2 = (bf16[128,1024]{1,0:T(8,128)(2,1)S(1)}, bf16[128,1024]{1,0:T(8,128)(2,1)}, u32[]{:S(2)}) copy-start(bf16[128,1024]{1,0:T(8,128)(2,1)} %v_ref.5) | copy-start | bytes 786436
  77.7 17.0 %copy-start.3 = (bf16[128,1024]{1,0:T(8,128)(2,1)S(1)}, bf16[128,1024]{1,0:T(8,128)(2,1)}, u32[]{:S(2)}) copy-start(bf16[128,1024]{1,0:T(8,128)(2,1)} %grad_ref.3) | copy-start | bytes 786436
  112.3 12.6 %all-to-all-start.3 = ((f32[16,16,128]{2,1,0:T(8,128)}), f32[16,16,128]{2,1,0:T(8,128)S(1)}, u32[]{:S(2)}, u32[]{:S(2)}) async-start(f32[16,16,128]{2,1,0:T(8,128)} %share_sums.2), calls=%async_computation.3 | async-start | bytes 262144 | tf_op jit(solution)/shard_map/all_to_all | solution.py:522
  116.9 8.6 %collective-permute-start.7 = (bf16[16,1024]{1,0:T(8,128)(2,1)S(1)}, bf16[16,1024]{1,0:T(8,128)(2,1)S(1)}, u32[]{:S(2)}, u32[]{:S(2)}) collective-permute-start(bf16[16,1024]{1,0:T(8,128)(2,1)S(1)} %get-tuple-element.54), channel_id=1, source_target_pairs={{2,0},{4,2},{6,4},{8,6},{10,8},{12,10},{14,12},{16,14},{18,16},{20... | collective-permute-start | bytes 98312 | tf_op jit(solution)/shard_map/ppermute | solution.py:510
  125.6 11.7 %all-to-all-start.4 = ((f32[8,16,128]{2,1,0:T(8,128)}), f32[8,16,128]{2,1,0:T(8,128)S(1)}, u32[]{:S(2)}, u32[]{:S(2)}) async-start(f32[8,16,128]{2,1,0:T(8,128)} %share_sums.3), calls=%async_computation.4 | async-start | bytes 131072 | tf_op jit(solution)/shard_map/all_to_all | solution.py:529
  (7 other events, 102.8 us)

commit v5 on v4

--- a/solution.py
+++ b/solution.py
@@ -114,32 +114,37 @@
     return result
 
 
+def decays_kernel(heads, gate_ref, decay_ref, cum_out, gf_out, ld_out):
+    tri = jnp.where(iota((T, T), 0) >= iota((T, T), 1), 1.0, 0.0).astype(BF16)
+    for h in range(heads):
+        lane = slice(h * T, (h + 1) * T)
+        gate = gate_ref[:, lane]
+        speed = -jnp.exp(decay_ref[:, lane])
+        log_decay = speed * (jnp.maximum(gate, 0.0) + jnp.log1p(jnp.exp(-jnp.abs(gate))))
+        ld_out[:, lane] = log_decay
+        gf_out[:, lane] = speed * sigmoid(gate)
+        both = lax.dot_general(
+            tri, jnp.concatenate(split(log_decay), axis=1), NN, preferred_element_type=F32
+        )
+        cum_out[:, lane] = both[:, :T] + both[:, T:]
+
+
 def maps_kernel(
     heads,
-    q_ref, k_ref, v_ref, halo_ref, gate_ref, beta_ref, conv_ref, decay_ref, grad_ref,
-    maps_ref, q_out, k_out, fq_out, fk_out, fv_out, cum_out, gf_out, ld_out, w_out, u_out, pg_out, inv_out,
+    q_ref, k_ref, v_ref, halo_ref, cum_ref, beta_ref, conv_ref, grad_ref,
+    maps_ref, q_out, k_out, fq_out, fk_out, fv_out, w_out, u_out, pg_out, inv_out,
     ext,
 ):
     row, col = iota((T, T), 0), iota((T, T), 1)
     strict = row > col
     lower = row >= col
     ident = jnp.where(row == col, 1.0, 0.0)
-    tri = jnp.where(lower, 1.0, 0.0).astype(BF16)
     base = pl.program_id(0) * heads
     each = range(heads)
     at = [slice(h * T, (h + 1) * T) for h in each]
     cumul, qs, ks, vs, betas = [], [], [], [], []
     for h in each:
-        gate = gate_ref[:, at[h]]
-        speed = -jnp.exp(decay_ref[:, at[h]])
-        log_decay = speed * (jnp.maximum(gate, 0.0) + jnp.log1p(jnp.exp(-jnp.abs(gate))))
-        ld_out[:, at[h]] = log_decay
-        gf_out[:, at[h]] = speed * sigmoid(gate)
-        both = lax.dot_general(
-            tri, jnp.concatenate(split(log_decay), axis=1), NN, preferred_element_type=F32
-        )
-        cumul.append(both[:, :T] + both[:, T:])
-        cum_out[:, at[h]] = cumul[h]
+        cumul.append(cum_ref[:, at[h]])
         betas.append(column(beta_ref, base + h))
         acts = []
         for j, (raw, factor) in enumerate(((q_ref, fq_out), (k_ref, fk_out), (v_ref, fv_out))):
@@ -444,16 +449,29 @@
     wide = heads * T
     tall, edge, taps, beta_spec, square = specs(heads)
     saved_specs = [tall] * 8 + [square] * 4
+    half = 4 * T
+    narrow = pl.BlockSpec((length, half), lambda h: (0, h))
+    cumul, slope, log_decay = pl.pallas_call(
+        functools.partial(decays_kernel, 4),
+        grid=(channels // half,),
+        in_specs=[narrow, pl.BlockSpec((1, half), lambda h: (0, h))],
+        out_specs=[narrow] * 3,
+        out_shape=[like(length, channels)] * 3,
+        compiler_params=params,
+        name="block_decays",
+        cost_estimate=pl.CostEstimate(flops=80_000_000, bytes_accessed=2_500_000, transcendentals=500_000),
+    )(gate_raw, decay_row)
     maps, *saved = pl.pallas_call(
         functools.partial(maps_kernel, heads),
         grid=(count // heads,),
-        in_specs=[tall, tall, tall, edge, tall, beta_spec, taps, pl.BlockSpec((1, wide), lambda h: (0, h)), tall],
-        out_specs=[pl.BlockSpec((heads, 3 * T + AUX, T), lambda h: (h, 0, 0))] + saved_specs,
-        out_shape=[like(count, 3 * T + AUX, T)] + saved_shapes,
+        in_specs=[tall, tall, tall, edge, tall, beta_spec, taps, tall],
+        out_specs=[pl.BlockSpec((heads, 3 * T + AUX, T), lambda h: (h, 0, 0))] + [tall] * 5 + [square] * 4,
+        out_shape=[like(count, 3 * T + AUX, T)] + [like(length, channels)] * 5 + [like(count, T, T)] * 4,
         scratch_shapes=[pltpu.VMEM((3, heads, 136, T), F32)],
         compiler_params=params,
         name="block_maps",
-    )(query_raw, key_raw, value_raw, halo, gate_raw, beta_raw.T, conv_weight, decay_row, grad_out)
+    )(query_raw, key_raw, value_raw, halo, cumul, beta_raw.T, conv_weight, grad_out)
+    saved = [*saved[:5], cumul, slope, log_decay, *saved[5:]]
 
     line_maps = widen(lax.all_to_all(maps.astype(LINK), "z", 0, 0, tiled=True))
     small = pltpu.CompilerParams(vmem_limit_bytes=32 * MIB)

time: 140 us -> 139 us (level)
  waiting for transfers between devices: 49 us -> 47.1 us
  Pallas kernels: 25.2 us -> 26.6 us
    pallas_call x0 -> x1, Pallas kernels: none -> 2.51 us  [per_device(): pl.pallas_call(functools.partial(decays_kernel, 4), grid=(channels // hal...]
    ppermute x1, waiting for transfers between devices: 1.89 us -> 0.01 us  [per_device(): halo = lax.ppermute(ends, SEQ, [(i, i + 1) for i in range(devices - 1)])]
  transfers between devices with their start and end apart: 11 -> 11, of which waited for: 10 -> 9; matrix products, arithmetic and copies ran while one was open for 1% -> 1% of each run, Pallas kernels for 0% -> 2%
where the time goes in v5:
time: 139 us; the launch traced here: 137 us
  waiting for transfers between devices  47.1 us (34%)
  starting transfers between devices  30.1 us (22%)
  blocking collectives  27.5 us (20%)
  Pallas kernels  26.6 us (19%)
  other arithmetic  2.93 us (2%)
    all_to_all x1, waiting for transfers between devices, per_device(): line_maps = widen(lax.all_to_all(maps.astype(LINK), 'z', 0, 0, tiled=True))  22.7 us
    all_to_all x1, blocking collectives, per_device(): lax.all_to_all(line_states.astype(LINK), 'z', 0, 0, tiled=True)  16.8 us
    all_to_all x1, blocking collectives, per_device(): sums = share(lax.all_to_all(sums, 'z', 0, 0, tiled=True), lines * planes)  10.7 us
    ppermute x6, waiting for transfers between devices, around(): lax.ppermute(block, axis, [(i, (i + d + 1) % size) for i in range(size)])  10.1 us
    pallas_call x1, Pallas kernels, per_device(): pl.pallas_call(functools.partial(maps_kernel, heads), grid=(count // head...  9.5 us
    ppermute x6, starting transfers between devices, around(): lax.ppermute(block, axis, [(i, (i + d + 1) % size) for i in range(size)])  9.47 us
    all_to_all x1, starting transfers between devices, per_device(): line_maps = widen(lax.all_to_all(maps.astype(LINK), 'z', 0, 0, tiled=True))  9.35 us
    all_to_all x1, waiting for transfers between devices, per_device(): lax.all_to_all(sums, 'z', 0, 0, tiled=True)  7.62 us
  transfers between devices with their start and end apart: 11, of which 9 were waited for; matrix products, arithmetic and copies ran while one was open for 1% of the time, Pallas kernels for 2%

profile of v5, /device:TPU:0, one launch (start us, length us, event | category | flops | bytes accessed | tf_op | source)
XLA Modules:
  0.0 136.8 jit_solution(6934160222863362065)
XLA Ops:
  0.6 1.4 %last_rows.1 = bf16[16,1024]{1,0:T(8,128)(2,1)} custom-call(bf16[128,1024]{1,0:T(8,128)(2,1)} %q_ref.5, bf16[128,1024]{1,0:T(8,128)(2,1)} %k_ref.5, bf16[128,1024]{1,0:T(8,128)(2,1)} %v_ref.5), custom_call_target="tpu_custom_call" | custom-call | tf_op jit(solution)/shard_map/last_rows/pallas_call | solution.py:422
  2.1 2.1 %collective-permute-start = (bf16[16,1024]{1,0:T(8,128)(2,1)}, bf16[16,1024]{1,0:T(8,128)(2,1)S(1)}, u32[]{:S(2)}, u32[]{:S(2)}) collective-permute-start(bf16[16,1024]{1,0:T(8,128)(2,1)} %last_rows.1), channel_id=1, source_target_pairs={{0,2},{2,4},{4,6},{6,8},{8,10},{10,12},{12,14},{14,16},{16,18},{18... | collective-permute-start | bytes 98312 | tf_op jit(solution)/shard_map/ppermute | solution.py:428
  4.1 2.5 %block_decays.1 = (f32[128,1024]{1,0:T(8,128)}, f32[128,1024]{1,0:T(8,128)}, f32[128,1024]{1,0:T(8,128)}) custom-call(f32[128,1024]{1,0:T(8,128)} %gate_ref.1, f32[1,1024]{1,0:T(1,128)} %bitcast.22), custom_call_target="tpu_custom_call" | custom-call | flops 80000000 | bytes 2500000 | tf_op jit(solution)/shard_map/block_decays/pallas_call | solution.py:454
  7.3 9.5 %block_maps.1 = (f32[8,400,128]{2,1,0:T(8,128)}, f32[128,1024]{1,0:T(8,128)}, f32[128,1024]{1,0:T(8,128)}, f32[128,1024]{1,0:T(8,128)}, f32[128,1024]{1,0:T(8,12...) custom-call(bf16[128,1024]{1,0:T(8,128)(2,1)} %q_ref.5, ...), custom_call_target="tpu_custom_call" | custom-call | tf_op jit(solution)/shard_map/block_maps/pallas_call | solution.py:464
  16.8 2.4 %convert_element_type.57 = f16[8,400,128]{2,1,0:T(8,128)(2,1)} convert(f32[8,400,128]{2,1,0:T(8,128)} %get-tuple-element.36) | non-fusion elementwise | flops 409600 | bytes 2457600 | tf_op jit(solution)/shard_map/convert_element_type | solution.py:476
  19.2 9.3 %all-to-all-start = ((f16[8,400,128]{2,1,0:T(8,128)(2,1)}), f16[8,400,128]{2,1,0:T(8,128)(2,1)S(1)}, u32[]{:S(2)}, u32[]{:S(2)}) async-start(f16[8,400,128]{2,1,0:T(8,128)(2,1)} %convert_element_type.57), calls=%async_computation | async-start | bytes 1638400 | tf_op jit(solution)/shard_map/all_to_all | solution.py:476
  28.6 22.7 %all-to-all-done = f16[8,400,128]{2,1,0:T(8,128)(2,1)S(1)} async-done(((f16[8,400,128]{2,1,0:T(8,128)(2,1)}), f16[8,400,128]{2,1,0:T(8,128)(2,1)S(1)}, u32[]{:S(2)}, u32[]{:S(2)}) %all-to-all-start) | async-done | bytes 819232 | tf_op jit(solution)/shard_map/all_to_all | solution.py:476
  51.3 0.9 line_total.1.refs_0_
  52.3 2.8 %collective-permute-start.3 = (f16[400,128]{1,0:T(8,128)(2,1)S(1)}, f16[400,128]{1,0:T(8,128)(2,1)S(1)}, u32[]{:S(2)}, u32[]{:S(2)}) collective-permute-start(f16[400,128]{1,0:T(8,128)(2,1)S(1)} %convert_element_type.59), channel_id=1, source_target_pairs={{0,48},{16,0},{32,16},{48,32},{1,49},{17,1},{33,17},{49,33},{2,50}... | collective-permute-start | bytes 307208 | tf_op jit(solution)/shard_map/ppermute | solution.py:485
  57.7 3.7 %collective-permute-done.2 = f16[400,128]{1,0:T(8,128)(2,1)S(1)} collective-permute-done((f16[400,128]{1,0:T(8,128)(2,1)S(1)}, f16[400,128]{1,0:T(8,128)(2,1)S(1)}, u32[]{:S(2)}, u32[]{:S(2)}) %collective-permute-start.2) | collective-permute-done | bytes 102432 | tf_op jit(solution)/shard_map/ppermute | solution.py:485
  61.4 1.0 collective-permute-done.1
  62.4 1.2 plane_total.1
  63.7 3.1 %collective-permute-start.6 = (f16[272,128]{1,0:T(8,128)(2,1)S(1)}, f16[272,128]{1,0:T(8,128)(2,1)S(1)}, u32[]{:S(2)}, u32[]{:S(2)}) collective-permute-start(f16[272,128]{1,0:T(8,128)(2,1)S(1)} %convert_element_type.67), channel_id=1, source_target_pairs={{0,192},{64,0},{128,64},{192,128},{1,193},{65,1},{129,65},{193,129... | collective-permute-start | bytes 208904 | tf_op jit(solution)/shard_map/ppermute | solution.py:485
  67.4 1.2 collective-permute-start.4
  68.7 3.9 %collective-permute-done.5 = f16[272,128]{1,0:T(8,128)(2,1)S(1)} collective-permute-done((f16[272,128]{1,0:T(8,128)(2,1)S(1)}, f16[272,128]{1,0:T(8,128)(2,1)S(1)}, u32[]{:S(2)}, u32[]{:S(2)}) %collective-permute-start.5) | collective-permute-done | bytes 69664 | tf_op jit(solution)/shard_map/ppermute | solution.py:485
  73.4 3.0 %line_states.1 = f32[8,272,128]{2,1,0:T(8,128)S(1)} custom-call(s32[2]{0:T(128)S(1)} %pad_add_fusion.where_ref, f32[8,400,128]{2,1,0:T(8,128)S(1)} %convert_element_type.58.maps_ref, f32[400,128]{1,0:T(8,128)S(1)} %convert_element_type.60.refs_1_.refs_0_, f32[400,128]{1,0:T(8,128)S(1)} %convert_element_type.61.refs_2_.refs_1_, ...), custom_call_target="tpu_custom_call" | custom-call | tf_op jit(solution)/shard_map/line_states/pallas_call | solution.py:497
  76.6 16.8 %all_to_all.25 = f16[8,272,128]{2,1,0:T(8,128)(2,1)S(1)} all-to-all(f16[8,272,128]{2,1,0:T(8,128)(2,1)S(1)} %convert_element_type.69), channel_id=1, replica_groups=mesh['y'=4,'x'=4,'z'=8,'head'=2] {'z'}, dimensions={0} | all-to-all | bytes 1114112 | tf_op jit(solution)/shard_map/all_to_all | solution.py:501
  93.7 6.1 %block_grads.1 = (bf16[128,1024]{1,0:T(8,128)(2,1)}, bf16[128,1024]{1,0:T(8,128)(2,1)}, bf16[128,1024]{1,0:T(8,128)(2,1)}, f32[3,16,1024]{2,1,0:T(8,128)S(1)}, b...) custom-call(bf16[128,1024]{1,0:T(8,128)(2,1)S(1)} %copy-done, ...), custom_call_target="tpu_custom_call" | custom-call | tf_op jit(solution)/shard_map/block_grads/pallas_call | solution.py:507
  99.8 10.7 %all_to_all.26.parts_ref = f32[8,16,128]{2,1,0:T(8,128)S(1)} all-to-all(f32[8,16,128]{2,1,0:T(8,128)S(1)} %get-tuple-element.53), channel_id=1, replica_groups=mesh['y'=4,'x'=4,'z'=8,'head'=2] {'z'}, dimensions={0} | all-to-all | bytes 131072 | tf_op jit(solution)/shard_map/all_to_all | solution.py:539
  111.2 4.6 %all-to-all-start.3 = ((f32[16,16,128]{2,1,0:T(8,128)}), f32[16,16,128]{2,1,0:T(8,128)S(1)}, u32[]{:S(2)}, u32[]{:S(2)}) async-start(f32[16,16,128]{2,1,0:T(8,128)} %share_sums.2), calls=%async_computation.3 | async-start | bytes 262144 | tf_op jit(solution)/shard_map/all_to_all | solution.py:540
  115.8 1.3 collective-permute-start.7
  117.1 6.7 %all-to-all-done.3.parts_ref = f32[16,16,128]{2,1,0:T(8,128)S(1)} async-done(((f32[16,16,128]{2,1,0:T(8,128)}), f32[16,16,128]{2,1,0:T(8,128)S(1)}, u32[]{:S(2)}, u32[]{:S(2)}) %all-to-all-start.3) | async-done | bytes 131104 | tf_op jit(solution)/shard_map/all_to_all | solution.py:540
  124.5 3.4 %all-to-all-start.4 = ((f32[8,16,128]{2,1,0:T(8,128)}), f32[8,16,128]{2,1,0:T(8,128)S(1)}, u32[]{:S(2)}, u32[]{:S(2)}) async-start(f32[8,16,128]{2,1,0:T(8,128)} %share_sums.3), calls=%async_computation.4 | async-start | bytes 131072 | tf_op jit(solution)/shard_map/all_to_all | solution.py:547
  128.5 7.6 %all-to-all-done.4.parts_ref = f32[8,16,128]{2,1,0:T(8,128)S(1)} async-done(((f32[8,16,128]{2,1,0:T(8,128)}), f32[8,16,128]{2,1,0:T(8,128)S(1)}, u32[]{:S(2)}, u32[]{:S(2)}) %all-to-all-start.4) | async-done | bytes 65568 | tf_op jit(solution)/shard_map/all_to_all | solution.py:547
  (68 shorter events, 7.7 us)
Async XLA Ops:
  2.1 4.6 %collective-permute-start = (bf16[16,1024]{1,0:T(8,128)(2,1)}, bf16[16,1024]{1,0:T(8,128)(2,1)S(1)}, u32[]{:S(2)}, u32[]{:S(2)}) collective-permute-start(bf16[16,1024]{1,0:T(8,128)(2,1)} %last_rows.1), channel_id=1, source_target_pairs={{0,2},{2,4},{4,6},{6,8},{8,10},{10,12},{12,14},{14,16},{16,18},{18... | collective-permute-start | bytes 98312 | tf_op jit(solution)/shard_map/ppermute | solution.py:428
  19.2 32.0 %all-to-all-start = ((f16[8,400,128]{2,1,0:T(8,128)(2,1)}), f16[8,400,128]{2,1,0:T(8,128)(2,1)S(1)}, u32[]{:S(2)}, u32[]{:S(2)}) async-start(f16[8,400,128]{2,1,0:T(8,128)(2,1)} %convert_element_type.57), calls=%async_computation | async-start | bytes 1638400 | tf_op jit(solution)/shard_map/all_to_all | solution.py:476
  52.3 5.4 %collective-permute-start.3 = (f16[400,128]{1,0:T(8,128)(2,1)S(1)}, f16[400,128]{1,0:T(8,128)(2,1)S(1)}, u32[]{:S(2)}, u32[]{:S(2)}) collective-permute-start(f16[400,128]{1,0:T(8,128)(2,1)S(1)} %convert_element_type.59), channel_id=1, source_target_pairs={{0,48},{16,0},{32,16},{48,32},{1,49},{17,1},{33,17},{49,33},{2,50}... | collective-permute-start | bytes 307208 | tf_op jit(solution)/shard_map/ppermute | solution.py:485
  55.1 6.2 %collective-permute-start.2 = (f16[400,128]{1,0:T(8,128)(2,1)S(1)}, f16[400,128]{1,0:T(8,128)(2,1)S(1)}, u32[]{:S(2)}, u32[]{:S(2)}) collective-permute-start(f16[400,128]{1,0:T(8,128)(2,1)S(1)} %convert_element_type.59), channel_id=1, source_target_pairs={{0,32},{16,48},{32,0},{48,16},{1,33},{17,49},{33,1},{49,17},{2,34}... | collective-permute-start | bytes 307208 | tf_op jit(solution)/shard_map/ppermute | solution.py:485
  55.9 6.5 %collective-permute-start.1 = (f16[400,128]{1,0:T(8,128)(2,1)S(1)}, f16[400,128]{1,0:T(8,128)(2,1)S(1)}, u32[]{:S(2)}, u32[]{:S(2)}) collective-permute-start(f16[400,128]{1,0:T(8,128)(2,1)S(1)} %convert_element_type.59), channel_id=1, source_target_pairs={{0,16},{16,32},{32,48},{48,0},{1,17},{17,33},{33,49},{49,1},{2,18}... | collective-permute-start | bytes 307208 | tf_op jit(solution)/shard_map/ppermute | solution.py:485
  63.7 5.1 %collective-permute-start.6 = (f16[272,128]{1,0:T(8,128)(2,1)S(1)}, f16[272,128]{1,0:T(8,128)(2,1)S(1)}, u32[]{:S(2)}, u32[]{:S(2)}) collective-permute-start(f16[272,128]{1,0:T(8,128)(2,1)S(1)} %convert_element_type.67), channel_id=1, source_target_pairs={{0,192},{64,0},{128,64},{192,128},{1,193},{65,1},{129,65},{193,129... | collective-permute-start | bytes 208904 | tf_op jit(solution)/shard_map/ppermute | solution.py:485
  66.8 5.8 %collective-permute-start.5 = (f16[272,128]{1,0:T(8,128)(2,1)S(1)}, f16[272,128]{1,0:T(8,128)(2,1)S(1)}, u32[]{:S(2)}, u32[]{:S(2)}) collective-permute-start(f16[272,128]{1,0:T(8,128)(2,1)S(1)} %convert_element_type.65), channel_id=1, source_target_pairs={{0,128},{64,192},{128,0},{192,64},{1,129},{65,193},{129,1},{193,65... | collective-permute-start | bytes 208904 | tf_op jit(solution)/shard_map/ppermute | solution.py:485
  67.4 5.9 %collective-permute-start.4 = (f16[272,128]{1,0:T(8,128)(2,1)S(1)}, f16[272,128]{1,0:T(8,128)(2,1)S(1)}, u32[]{:S(2)}, u32[]{:S(2)}) collective-permute-start(f16[272,128]{1,0:T(8,128)(2,1)S(1)} %convert_element_type.63), channel_id=1, source_target_pairs={{0,64},{64,128},{128,192},{192,0},{1,65},{65,129},{129,193},{193,1... | collective-permute-start | bytes 208904 | tf_op jit(solution)/shard_map/ppermute | solution.py:485
  73.3 20.1 %copy-start.10 = (f32[128,1024]{1,0:T(8,128)S(1)}, f32[128,1024]{1,0:T(8,128)}, u32[]{:S(2)}) copy-start(f32[128,1024]{1,0:T(8,128)} %get-tuple-element.43.fk_in) | copy-start | bytes 1572868
  73.4 20.1 %copy-start.11 = (f32[128,1024]{1,0:T(8,128)S(1)}, f32[128,1024]{1,0:T(8,128)}, u32[]{:S(2)}) copy-start(f32[128,1024]{1,0:T(8,128)} %get-tuple-element.44.fv_in) | copy-start | bytes 1572868
  73.4 20.1 %copy-start.12 = (f32[8,128,128]{2,1,0:T(8,128)S(1)}, f32[8,128,128]{2,1,0:T(8,128)}, u32[]{:S(2)}) copy-start(f32[8,128,128]{2,1,0:T(8,128)} %get-tuple-element.47.w_in) | copy-start | bytes 1572868
  73.4 20.1 %copy-start.13 = (f32[8,128,128]{2,1,0:T(8,128)S(1)}, f32[8,128,128]{2,1,0:T(8,128)}, u32[]{:S(2)}) copy-start(f32[8,128,128]{2,1,0:T(8,128)} %get-tuple-element.48.u_in) | copy-start | bytes 1572868
  73.4 20.1 %copy-start.14 = (f32[8,128,128]{2,1,0:T(8,128)S(1)}, f32[8,128,128]{2,1,0:T(8,128)}, u32[]{:S(2)}) copy-start(f32[8,128,128]{2,1,0:T(8,128)} %get-tuple-element.49.pg_in) | copy-start | bytes 1572868
  73.4 20.1 %copy-start.15 = (f32[8,128,128]{2,1,0:T(8,128)S(1)}, f32[8,128,128]{2,1,0:T(8,128)}, u32[]{:S(2)}) copy-start(f32[8,128,128]{2,1,0:T(8,128)} %get-tuple-element.50.inv_in) | copy-start | bytes 1572868
  76.4 17.1 %copy-start.7 = (f32[128,1024]{1,0:T(8,128)S(1)}, f32[128,1024]{1,0:T(8,128)}, u32[]{:S(2)}) copy-start(f32[128,1024]{1,0:T(8,128)} %get-tuple-element.40.q_in) | copy-start | bytes 1572868
  76.4 17.1 %copy-start.8 = (f32[128,1024]{1,0:T(8,128)S(1)}, f32[128,1024]{1,0:T(8,128)}, u32[]{:S(2)}) copy-start(f32[128,1024]{1,0:T(8,128)} %get-tuple-element.41.k_in) | copy-start | bytes 1572868
  76.4 17.1 %copy-start.9 = (f32[128,1024]{1,0:T(8,128)S(1)}, f32[128,1024]{1,0:T(8,128)}, u32[]{:S(2)}) copy-start(f32[128,1024]{1,0:T(8,128)} %get-tuple-element.42.fq_in) | copy-start | bytes 1572868
  76.5 17.1 %copy-start = (bf16[128,1024]{1,0:T(8,128)(2,1)S(1)}, bf16[128,1024]{1,0:T(8,128)(2,1)}, u32[]{:S(2)}) copy-start(bf16[128,1024]{1,0:T(8,128)(2,1)} %q_ref.5) | copy-start | bytes 786436
  76.5 17.1 %copy-start.1 = (bf16[128,1024]{1,0:T(8,128)(2,1)S(1)}, bf16[128,1024]{1,0:T(8,128)(2,1)}, u32[]{:S(2)}) copy-start(bf16[128,1024]{1,0:T(8,128)(2,1)} %k_ref.5) | copy-start | bytes 786436
  76.5 17.1 %copy-start.2 = (bf16[128,1024]{1,0:T(8,128)(2,1)S(1)}, bf16[128,1024]{1,0:T(8,128)(2,1)}, u32[]{:S(2)}) copy-start(bf16[128,1024]{1,0:T(8,128)(2,1)} %v_ref.5) | copy-start | bytes 786436
  76.6 17.0 %copy-start.3 = (f32[128,1024]{1,0:T(8,128)S(1)}, f32[128,1024]{1,0:T(8,128)}, u32[]{:S(2)}) copy-start(f32[128,1024]{1,0:T(8,128)} %get-tuple-element.35.cum_ref.cum_in) | copy-start | bytes 1572868
  111.2 12.6 %all-to-all-start.3 = ((f32[16,16,128]{2,1,0:T(8,128)}), f32[16,16,128]{2,1,0:T(8,128)S(1)}, u32[]{:S(2)}, u32[]{:S(2)}) async-start(f32[16,16,128]{2,1,0:T(8,128)} %share_sums.2), calls=%async_computation.3 | async-start | bytes 262144 | tf_op jit(solution)/shard_map/all_to_all | solution.py:540
  115.8 8.6 %collective-permute-start.7 = (bf16[16,1024]{1,0:T(8,128)(2,1)S(1)}, bf16[16,1024]{1,0:T(8,128)(2,1)S(1)}, u32[]{:S(2)}, u32[]{:S(2)}) collective-permute-start(bf16[16,1024]{1,0:T(8,128)(2,1)S(1)} %get-tuple-element.54), channel_id=1, source_target_pairs={{2,0},{4,2},{6,4},{8,6},{10,8},{12,10},{14,12},{16,14},{18,16},{20... | collective-permute-start | bytes 98312 | tf_op jit(solution)/shard_map/ppermute | solution.py:528
  124.5 11.7 %all-to-all-start.4 = ((f32[8,16,128]{2,1,0:T(8,128)}), f32[8,16,128]{2,1,0:T(8,128)S(1)}, u32[]{:S(2)}, u32[]{:S(2)}) async-start(f32[8,16,128]{2,1,0:T(8,128)} %share_sums.3), calls=%async_computation.4 | async-start | bytes 131072 | tf_op jit(solution)/shard_map/all_to_all | solution.py:547
  (7 other events, 102.9 us)
